TPU v7x, 128 devices: a whole 4x4x4 slice. The times are simulated.
128 devices in a mesh: grp: 4 (over x), mem: 32 (over z, y, core).
Axes of the slice: x: 4, y: 4, z: 4, core: 2. Of those that a mesh axis runs over, the one named last changes fastest.
Arguments:
- embeddings: float32 [32768, 768], P(('grp', 'mem')), may hold values from -6 to 6
- cluster_ids: int32 [32768, 1], P(('grp', 'mem')), may hold values from 0 to 3; in each aligned block of 256 rows (0 to 255, 256 to 511, ...) at most 128 rows name the same one
Outputs:
- nearest: float32 [32768], P(('grp', 'mem'))
Inputs may be any that keep to these rules, and one draw needn't show every extreme that they name: `cluster_ids`: among the rows of one device no cluster id appears more than 128 times, and some cluster reaches 128 on some device.
All inputs are finite; a program needn't handle non-finite values.
Results may differ from a plain program's by a relative error of at most 0.0011.
Values may be sent and summed in bfloat16 or wider, within the bound.
A program may use at most 64 MiB of HBM per device.

v0:
```python
import jax
import jax.numpy as jnp
from jax import lax
from jax.sharding import PartitionSpec as P

CL_GRP = 1


FILL = -4.0


def masked_scores(mine, mine_valid, piece, piece_valid, mine_index, piece_index):
    sims = jnp.einsum("csd,ctd->cst", mine, piece, preferred_element_type=jnp.float32)
    differ = (mine_index[:, None] != piece_index[None, :])[None, :, :]
    keep = (mine_valid[:, :, None] > 0) & (piece_valid[:, None, :] > 0) & differ
    return jnp.where(keep, sims, FILL)


def body(embeddings, cluster_ids):
    local_rows = embeddings.shape[0]
    width = embeddings.shape[1]
    squares = jnp.sum(embeddings * embeddings, axis=1, keepdims=True)
    unit = (embeddings * lax.rsqrt(squares + 1e-06)).astype(jnp.bfloat16)
    labels = cluster_ids[:, 0]
    groups = lax.axis_size("grp")
    owned = CL_GRP
    clusters = owned * groups
    capacity = local_rows // 2
    onehot = (labels[:, None] == jnp.arange(clusters, dtype=jnp.int32)[None, :]).astype(jnp.int32)
    ranks = jnp.sum(onehot * (jnp.cumsum(onehot, axis=0) - 1), axis=1)
    owner = labels // owned
    within = labels % owned
    outgoing = (
        jnp.zeros((owned, groups, capacity, width), jnp.bfloat16).at[within, owner, ranks].set(unit)
    )
    flags = jnp.zeros((owned, groups, capacity), jnp.bfloat16).at[within, owner, ranks].set(1.0)
    arrived, arrived_flags = (
        lax.all_to_all(outgoing, "grp", split_axis=1, concat_axis=1, tiled=True),
        lax.all_to_all(flags, "grp", split_axis=1, concat_axis=1, tiled=True),
    )
    slots = groups * capacity
    mine = arrived.reshape(owned, slots, width)
    mine_valid = arrived_flags.reshape(owned, slots)
    local_index = jnp.arange(slots, dtype=jnp.int32)
    own_index = lax.axis_index("mem") * slots + local_index
    start_best = jnp.full((owned, slots), FILL, jnp.float32)
    piece = lax.all_gather(mine, "mem", axis=1, tiled=True)
    piece_valid = lax.all_gather(mine_valid, "mem", axis=1, tiled=True)
    span = 4 * slots
    turns = piece.shape[1] // span

    def one_span(turn, acc):
        offset = turn * span
        part = lax.dynamic_slice_in_dim(piece, offset, span, 1)
        part_valid = lax.dynamic_slice_in_dim(piece_valid, offset, span, 1)
        part_index = offset + jnp.arange(span, dtype=jnp.int32)
        scores = masked_scores(mine, mine_valid, part, part_valid, own_index, part_index)
        return jnp.maximum(acc, jnp.max(scores, axis=2))

    best = lax.fori_loop(0, turns, one_span, start_best)
    results = lax.all_to_all(
        best.reshape(owned, groups, capacity), "grp", split_axis=1, concat_axis=1, tiled=True
    )
    return results[within, owner, ranks]


def solution(mesh):
    return jax.shard_map(
        body,
        mesh=mesh,
        in_specs=(P(("grp", "mem"), None), P(("grp", "mem"), None)),
        out_specs=P(("grp", "mem")),
        check_vma=False,
    )
```

profile of v0, /device:TPU:1, one launch (start us, length us, event | category | flops | bytes accessed | tf_op | source)
XLA Modules:
  0.0 189.1 jit_solution(10520630682669411987)
XLA Ops:
  6.5 0.0 all-gather.2.cloned.1.call-start
  6.5 0.7 compare_convert_fusion
  7.2 1.2 reduce-window.6
  8.4 0.1 slice.21
  8.5 0.1 copy.13
  8.6 0.1 copy.14
  8.7 0.1 add_bitcast_fusion
  8.8 0.7 fusion.9
  9.5 0.7 or_select_fusion
  10.2 1.3 multiply_reduce_fusion
  11.5 1.2 multiply_convert_fusion
  12.7 0.1 broadcast.191
  12.8 15.3 %scatter_fusion.1 = bf16[4,128,768]{2,1,0:T(8,128)(2,1)S(1)} fusion(bf16[4,128,768]{2,1,0:T(8,128)(2,1)S(1)} %broadcast.191, s32[256]{0:T(256)S(1)} %bitcast.51, bf16[256,768]{1,0:T(8,128)(2,1)S(1)} %multiply_convert_fusion), kind=kCustom, calls=%fused_computation.2 | custom fusion | bytes 1181696 | tf_op jit(solution)/shard_map/scatter | solution.py:34
  28.1 16.1 %all_to_all.15 = bf16[1,4,128,768]{3,2,0,1:T(8,128)(2,1)} all-to-all(bf16[1,4,128,768]{3,2,0,1:T(8,128)(2,1)S(1)} %bitcast.53), channel_id=1, replica_groups=mesh['grp'=4,'mem'=32] {'grp'}, dimensions={1} | all-to-all | bytes 1572864 | tf_op jit(solution)/shard_map/all_to_all | solution.py:38
  44.2 0.0 all-gather.2.cloned.1.call-update
  44.3 11.8 %scatter_fusion = bf16[4,128]{1,0:T(4,128)(2,1)S(1)} fusion(bf16[4,128]{1,0:T(4,128)(2,1)S(1)} %broadcast.185, s32[256]{0:T(256)S(1)} %bitcast.52, bf16[256]{0:T(256)(128)(2,1)S(1)} %broadcast.190), kind=kCustom, calls=%fused_computation.1 | custom fusion | bytes 3584 | tf_op jit(solution)/shard_map/scatter | solution.py:36
  56.0 0.5 copy.15
  56.6 3.2 %all-to-all-start = ((bf16[1,4,128]{2,0,1:T(2,128)(2,1)}), bf16[1,4,128]{2,0,1:T(2,128)(2,1)S(1)}, u32[]{:S(2)}, u32[]{:S(2)}) async-start(bf16[1,4,128]{2,0,1:T(2,128)(2,1)} %copy.15), calls=%async_computation | async-start | bytes 4096 | tf_op jit(solution)/shard_map/all_to_all | solution.py:39
  59.8 4.2 %all-to-all-done = bf16[1,4,128]{2,0,1:T(2,128)(2,1)S(1)} async-done(((bf16[1,4,128]{2,0,1:T(2,128)(2,1)}), bf16[1,4,128]{2,0,1:T(2,128)(2,1)S(1)}, u32[]{:S(2)}, u32[]{:S(2)}) %all-to-all-start) | async-done | bytes 1056 | tf_op jit(solution)/shard_map/all_to_all | solution.py:39
  64.0 28.4 %all_gather.6 = bf16[1,16384]{1,0:T(2,128)(2,1)S(1)} all-gather(bf16[1,512]{1,0:T(2,128)(2,1)S(1)} %bitcast.59), channel_id=1, replica_groups=mesh['grp'=4,'mem'=32] {'mem'}, dimensions={1}, use_global_device_ids=true | all-gather | bytes 33792 | tf_op jit(solution)/shard_map/all_gather | solution.py:48
  92.4 46.5 %all-gather.2.cloned.1.call-done = bf16[1,16384,768]{2,1,0:T(8,128)(2,1)} async-done(((bf16[1,512,768]{2,1,0:T(8,128)(2,1)}), bf16[1,16384,768]{2,1,0:T(8,128)(2,1)}) %all-gather.2.cloned.1.call-update) | async-done | bytes 25165840 | tf_op jit(solution)/shard_map/all_gather | solution.py:47
  138.9 32.8 %while.14 = (s32[]{:T(128)}, f32[1,512]{1,0:T(1,128)S(1)}, bf16[1,4,128]{2,1,0:T(4,128)(2,1)S(1)}, bf16[1,16384]{1,0:T(2,128)(2,1)S(1)}, bf16[1,16384,768]{2,1,0...) while((s32[]{:T(128)}, f32[1,512]{1,0:T(1,128)S(1)}, ...), condition=%wide.region_8.9_spmd.clone, body=%wide.region_6.8_spmd.clone.sunk | while | flops 1615865344 | bytes 3971253 | solution.py:60
  138.9 4.0 %fusion.18 = f32[512]{0:T(512)S(1)} fusion(bf16[1,16384,768]{2,1,0:T(8,128)(2,1)} %get-tuple-element.256, s32[]{:T(128)S(6)} %select_n.63, s32[512]{0:T(512)S(1)} %iota_add_fusion.4, s32[2048]{0:T(1024)S(1)} %iota_add_fusion.5, pred[512]{0:T(512)(128)(4,1)S(1)} %compare_bitcast_fusion.2, pred[2048]{0:T(1024)(128)(4,1)S(1)} %compare_reduce_fusion.2, ...), kind=kOutput, calls=%fused_computation.5.clone.1 | convolution fusion | flops 1615855104 | bytes 3947012 | tf_op jit(solution)/shard_map/while/body/eval_jaxpr/csd,ctd->cst/dot_general | solution.py:13
  143.1 4.0 %fusion.18 = f32[512]{0:T(512)S(1)} fusion(bf16[1,16384,768]{2,1,0:T(8,128)(2,1)} %get-tuple-element.256, s32[]{:T(128)S(6)} %select_n.63, s32[512]{0:T(512)S(1)} %iota_add_fusion.4, s32[2048]{0:T(1024)S(1)} %iota_add_fusion.5, pred[512]{0:T(512)(128)(4,1)S(1)} %compare_bitcast_fusion.2, pred[2048]{0:T(1024)(128)(4,1)S(1)} %compare_reduce_fusion.2, ...), kind=kOutput, calls=%fused_computation.5.clone.1 | convolution fusion | flops 1615855104 | bytes 3947012 | tf_op jit(solution)/shard_map/while/body/eval_jaxpr/csd,ctd->cst/dot_general | solution.py:13
  147.2 4.0 %fusion.18 = f32[512]{0:T(512)S(1)} fusion(bf16[1,16384,768]{2,1,0:T(8,128)(2,1)} %get-tuple-element.256, s32[]{:T(128)S(6)} %select_n.63, s32[512]{0:T(512)S(1)} %iota_add_fusion.4, s32[2048]{0:T(1024)S(1)} %iota_add_fusion.5, pred[512]{0:T(512)(128)(4,1)S(1)} %compare_bitcast_fusion.2, pred[2048]{0:T(1024)(128)(4,1)S(1)} %compare_reduce_fusion.2, ...), kind=kOutput, calls=%fused_computation.5.clone.1 | convolution fusion | flops 1615855104 | bytes 3947012 | tf_op jit(solution)/shard_map/while/body/eval_jaxpr/csd,ctd->cst/dot_general | solution.py:13
  151.3 4.0 %fusion.18 = f32[512]{0:T(512)S(1)} fusion(bf16[1,16384,768]{2,1,0:T(8,128)(2,1)} %get-tuple-element.256, s32[]{:T(128)S(6)} %select_n.63, s32[512]{0:T(512)S(1)} %iota_add_fusion.4, s32[2048]{0:T(1024)S(1)} %iota_add_fusion.5, pred[512]{0:T(512)(128)(4,1)S(1)} %compare_bitcast_fusion.2, pred[2048]{0:T(1024)(128)(4,1)S(1)} %compare_reduce_fusion.2, ...), kind=kOutput, calls=%fused_computation.5.clone.1 | convolution fusion | flops 1615855104 | bytes 3947012 | tf_op jit(solution)/shard_map/while/body/eval_jaxpr/csd,ctd->cst/dot_general | solution.py:13
  155.4 4.0 %fusion.18 = f32[512]{0:T(512)S(1)} fusion(bf16[1,16384,768]{2,1,0:T(8,128)(2,1)} %get-tuple-element.256, s32[]{:T(128)S(6)} %select_n.63, s32[512]{0:T(512)S(1)} %iota_add_fusion.4, s32[2048]{0:T(1024)S(1)} %iota_add_fusion.5, pred[512]{0:T(512)(128)(4,1)S(1)} %compare_bitcast_fusion.2, pred[2048]{0:T(1024)(128)(4,1)S(1)} %compare_reduce_fusion.2, ...), kind=kOutput, calls=%fused_computation.5.clone.1 | convolution fusion | flops 1615855104 | bytes 3947012 | tf_op jit(solution)/shard_map/while/body/eval_jaxpr/csd,ctd->cst/dot_general | solution.py:13
  159.5 4.0 %fusion.18 = f32[512]{0:T(512)S(1)} fusion(bf16[1,16384,768]{2,1,0:T(8,128)(2,1)} %get-tuple-element.256, s32[]{:T(128)S(6)} %select_n.63, s32[512]{0:T(512)S(1)} %iota_add_fusion.4, s32[2048]{0:T(1024)S(1)} %iota_add_fusion.5, pred[512]{0:T(512)(128)(4,1)S(1)} %compare_bitcast_fusion.2, pred[2048]{0:T(1024)(128)(4,1)S(1)} %compare_reduce_fusion.2, ...), kind=kOutput, calls=%fused_computation.5.clone.1 | convolution fusion | flops 1615855104 | bytes 3947012 | tf_op jit(solution)/shard_map/while/body/eval_jaxpr/csd,ctd->cst/dot_general | solution.py:13
  163.6 4.0 %fusion.18 = f32[512]{0:T(512)S(1)} fusion(bf16[1,16384,768]{2,1,0:T(8,128)(2,1)} %get-tuple-element.256, s32[]{:T(128)S(6)} %select_n.63, s32[512]{0:T(512)S(1)} %iota_add_fusion.4, s32[2048]{0:T(1024)S(1)} %iota_add_fusion.5, pred[512]{0:T(512)(128)(4,1)S(1)} %compare_bitcast_fusion.2, pred[2048]{0:T(1024)(128)(4,1)S(1)} %compare_reduce_fusion.2, ...), kind=kOutput, calls=%fused_computation.5.clone.1 | convolution fusion | flops 1615855104 | bytes 3947012 | tf_op jit(solution)/shard_map/while/body/eval_jaxpr/csd,ctd->cst/dot_general | solution.py:13
  167.7 4.0 %fusion.18 = f32[512]{0:T(512)S(1)} fusion(bf16[1,16384,768]{2,1,0:T(8,128)(2,1)} %get-tuple-element.256, s32[]{:T(128)S(6)} %select_n.63, s32[512]{0:T(512)S(1)} %iota_add_fusion.4, s32[2048]{0:T(1024)S(1)} %iota_add_fusion.5, pred[512]{0:T(512)(128)(4,1)S(1)} %compare_bitcast_fusion.2, pred[2048]{0:T(1024)(128)(4,1)S(1)} %compare_reduce_fusion.2, ...), kind=kOutput, calls=%fused_computation.5.clone.1 | convolution fusion | flops 1615855104 | bytes 3947012 | tf_op jit(solution)/shard_map/while/body/eval_jaxpr/csd,ctd->cst/dot_general | solution.py:13
  171.7 7.9 %all_to_all.16 = f32[1,4,128]{2,0,1:T(1,128)S(1)} all-to-all(f32[1,4,128]{2,0,1:T(1,128)S(1)} %bitcast.57), channel_id=1, replica_groups=mesh['grp'=4,'mem'=32] {'grp'}, dimensions={1} | all-to-all | bytes 4096 | tf_op jit(solution)/shard_map/all_to_all | solution.py:61
  179.5 2.7 %gather_fusion = f32[256]{0:T(256)} fusion(f32[1,4,128]{2,0,1:T(1,128)S(1)} %all_to_all.16, s32[256]{0:T(256)S(1)} %bitcast.54), kind=kCustom, calls=%fused_computation | custom fusion | bytes 5120 | tf_op jit(solution)/shard_map/gather | solution.py:64
  (47 shorter events, 0.7 us)
Async XLA Ops:
  6.5 132.3 %all-gather.2.cloned.1.call-start = ((), (), s32[]{:S(2)}) async-start(), calls=%async_computation.3 | async-start | bytes 25952256 | tf_op jit(solution)/shard_map/all_gather | solution.py:47
  56.6 7.4 %all-to-all-start = ((bf16[1,4,128]{2,0,1:T(2,128)(2,1)}), bf16[1,4,128]{2,0,1:T(2,128)(2,1)S(1)}, u32[]{:S(2)}, u32[]{:S(2)}) async-start(bf16[1,4,128]{2,0,1:T(2,128)(2,1)} %copy.15), calls=%async_computation | async-start | bytes 4096 | tf_op jit(solution)/shard_map/all_to_all | solution.py:39
Sparse Core Ops, SparseCore 0:
  44.4 94.4 all-gather.1
where the time goes:
time: 190 us; the launch traced here: 189 us
  blocking collectives  52.4 us (28%)
  waiting for transfers between devices  50.7 us (27%)
  matrix products  31.8 us (17%)
  local copies, waits for them, and re-layouts  30.6 us (16%)
  between operations  13.5 us (7%)
  other arithmetic  6.5 us (3%)
  starting transfers between devices  3.2 us (2%)
    all_gather x1, waiting for transfers between devices, body(): piece = lax.all_gather(mine, 'mem', axis=1, tiled=True)  46.5 us
    dot_general x8, matrix products, masked_scores(): jnp.einsum('csd,ctd->cst', mine, piece, preferred_element_type=jnp.float32)  31.8 us
    all_gather x1, blocking collectives, body(): piece_valid = lax.all_gather(mine_valid, 'mem', axis=1, tiled=True)  28.4 us
    all_to_all x1, blocking collectives, body(): lax.all_to_all(outgoing, 'grp', split_axis=1, concat_axis=1, tiled=True)  16.1 us
    scatter x1, local copies, waits for them, and re-layouts, body(): jnp.zeros((owned, groups, capacity, width), jnp.bfloat16)  15.3 us
    scatter x2, local copies, waits for them, and re-layouts, body(): jnp.zeros((owned, groups, capacity), jnp.bfloat16).at[within, owner, ranks]  12.3 us
    all_to_all x1, blocking collectives, body(): lax.all_to_all(best.reshape(owned, groups, capacity), 'grp', split_axis=1...  7.87 us
    all_to_all x1, waiting for transfers between devices, body(): lax.all_to_all(flags, 'grp', split_axis=1, concat_axis=1, tiled=True)  4.16 us
  transfers between devices with their start and end apart: 2, of which 2 were waited for; matrix products, arithmetic and copies ran while one was open for 7% of the time, Pallas kernels for 0%

commit v1 on v0

v1 whole, which is shorter than its diff:
```python
import functools

import jax
import jax.numpy as jnp
from jax import lax
from jax.experimental import pallas as pl
from jax.experimental.pallas import tpu as pltpu
from jax.sharding import PartitionSpec as P

FILL = -4.0
MESH = pl.DeviceIdType.MESH
SIDE = 4
DIRS = ((1, 0, 0), (3, 0, 0), (0, 1, 0), (0, 3, 0), (0, 0, 1), (0, 0, 3))

OFFSETS = (
    (0, 0, 0),
    (0, 0, 2),
    (2, 0, 2),
    (0, 0, 3),
    (3, 0, 0),
    (0, 1, 0),
    (1, 1, 0),
    (0, 2, 0),
    (1, 2, 0),
    (0, 3, 0),
    (2, 0, 1),
    (3, 0, 1),
)

FIRST_SENDS = (
    ((0, 3, 5), (0, 4, 1), (0, 9, 3), (1, 3, 5), (1, 4, 1), (1, 5, 2), (0, 5, 2), (1, 9, 3)),
    ((1, 5, 2), (0, 3, 5), (0, 4, 1), (0, 5, 2), (0, 9, 3), (1, 3, 5), (1, 4, 1), (1, 9, 3)),
)

STEPS = (
    (((('o', 0),), (('o', 0),)), ((0, 0), (0, 0))),
    (((('a', 3, 0, ((1, 5),)), ('a', 4, 0, ((11, 4),)), ('a', 9, 0, ((7, 3),)), ('a', 11, 0, ((10, 1),)), ('a', 3, 1, ((1, 5),)), ('a', 4, 1, ((11, 4),)), ('a', 5, 1, ((6, 0),)), ('a', 7, 0, ((8, 0),))), (('a', 5, 1, ((6, 0), (7, 2))), ('a', 3, 0, ((1, 5),)), ('a', 4, 0, ((11, 4),)), ('a', 5, 0, ((6, 0),)), ('a', 9, 0, ((7, 3),)))), ((0, 3), (0, 5))),
    (((), (('a', 6, 1, ()), ('a', 6, 0, ((8, 2),)), ('a', 11, 0, ((10, 1),)))), ((0, 4), (0, 6))),
    (((('a', 5, 0, ((6, 0),)), ('a', 9, 1, ((7, 3),))), (('a', 3, 1, ((1, 5),)), ('a', 4, 1, ((11, 4),)))), ((0, 5), (0, 3))),
    (((('o', 5),), ()), ((5, 3), (0, 4))),
    (((('a', 6, 1, ((8, 2),)), ('a', 11, 1, ((10, 1),))), (('o', 3),)), ((5, 9), (3, 6))),
    (((('o', 3),), (('o', 4),)), ((3, 9), (4, 3))),
    (((('o', 4),), ()), ((4, 3), (4, 6))),
    (((('a', 1, 0, ()), ('a', 10, 0, ((2, 4),))), (('a', 7, 0, ()), ('a', 7, 1, ((8, 0),)), ('o', 5))), ((4, 5), (5, 3))),
    (((), ()), ((3, 11), (0, 7))),
    (((('a', 6, 0, ()),), (('a', 11, 1, ((10, 1),)),)), ((5, 11), (3, 7))),
    (((), ()), ((3, 6), (4, 7))),
    (((), ()), ((4, 6), (3, 11))),
    (((('a', 7, 1, ()), ('o', 11)), (('a', 1, 0, ()), ('a', 8, 0, ()), ('a', 10, 0, ((2, 4),)))), ((11, 6), (5, 11))),
    (((), (('o', 11),)), ((11, 9), (11, 6))),
    (((('a', 2, 0, ()), ('a', 8, 0, ())), ()), ((3, 7), (11, 7))),
    (((), (('o', 6),)), ((4, 7), (6, 7))),
    (((('o', 6),), (('a', 9, 1, ()),)), ((6, 7), (3, 9))),
    (((('a', 1, 1, ()), ('a', 8, 1, ()), ('a', 10, 1, ((2, 4),))), ()), ((11, 7), (11, 9))),
    (((), (('a', 2, 0, ()), ('a', 8, 1, ()))), ((0, 1), (3, 8))),
    (((), ()), ((0, 10), (4, 8))),
    (((('f', 0),), (('f', 4),)), ((3, 8), (11, 8))),
    (((), (('a', 1, 1, ()), ('a', 10, 1, ((2, 4),)))), ((3, 10), (0, 1))),
    (((('f', 3),), ()), ((4, 8), (0, 10))),
    (((('f', 4), ('a', 2, 1, ())), (('f', 0),)), ((5, 1), (3, 10))),
    (((), (('f', 3),)), ((6, 1), (5, 1))),
    (((), ()), ((6, 10), (6, 1))),
    (((('o', 7),), ()), ((7, 1), (6, 10))),
    (((), (('a', 2, 1, ()), ('o', 7))), ((11, 1), (7, 1))),
    (((), (('o', 8),)), ((11, 8), (8, 1))),
    (((('f', 11), ('o', 9)), (('f', 8), ('o', 9))), ((9, 10), (9, 10))),
    (((('f', 9), ('f', 10), ('o', 8)), (('f', 9), ('f', 10))), ((8, 1), (11, 1))),
    (((('f', 8), ('o', 1)), (('f', 11), ('o', 1))), ((1, 2), (1, 2))),
    (((('f', 1),), (('f', 1),)), ((5, 2), (5, 2))),
    (((('f', 5),), (('f', 5),)), ((6, 2), (6, 2))),
    (((('f', 6),), (('f', 6),)), ((7, 2), (7, 2))),
    (((('f', 2), ('f', 7)), (('f', 2), ('f', 7))), None),
)


SLOTS = len(OFFSETS)


def greeted():
    both = set()
    for x, y, z in OFFSETS:
        both.add((x, y, z))
        both.add(((-x) % SIDE, (-y) % SIDE, (-z) % SIDE))
    near = [(d, 0) for d in DIRS if d not in both]
    far = [(d, k) for d in sorted(both) for k in (0, 1) if any(d) or k]
    return near + far


def kernel(chunks, emb_ref, lab_ref, out_ref, emb, buf, labels, label_rows, row_best, column_best, outgoing,
           incoming, load_sem, send_sem, recv_sem, give_sem, take_sem, label_send, label_recv, result_send,
           result_recv):
    rows, width = emb.shape
    part = rows // chunks
    gx = lax.axis_index("grp")
    mem = lax.axis_index("mem")
    core = lax.rem(mem, 2)
    other = 1 - core
    gy = lax.rem(mem // 2, SIDE)
    gz = mem // (2 * SIDE)
    xs = [lax.rem(gx + k, SIDE) for k in range(SIDE)]
    ys = [lax.rem(gy + k, SIDE) for k in range(SIDE)]
    zs = [lax.rem(gz + k, SIDE) for k in range(SIDE)]

    def at(offset, on):
        x, y, z = (k % SIDE for k in offset)
        return (xs[x], (zs[z] * SIDE + ys[y]) * 2 + on)

    load = pltpu.make_async_copy(emb_ref, emb, load_sem)
    load.start()
    barrier = pltpu.get_barrier_semaphore()
    friends = greeted()
    for offset, flip in friends:
        pl.semaphore_signal(barrier, inc=1, device_id=at(offset, other if flip else core), device_id_type=MESH)

    def chunk_of(slot, h, on):
        return buf.at[slot, on, pl.ds(h * part, part)]

    def relay(source, target, h, direction):
        return pltpu.make_async_remote_copy(
            src_ref=chunk_of(source, h, core), dst_ref=chunk_of(target, h, core),
            send_sem=send_sem.at[target, h], recv_sem=recv_sem.at[target, h],
            device_id=at(DIRS[direction], core), device_id_type=MESH)

    def share(slot, h, on):
        return pltpu.make_async_remote_copy(
            src_ref=chunk_of(slot, h, on), dst_ref=chunk_of(slot, h, on),
            send_sem=give_sem.at[slot, h], recv_sem=take_sem.at[slot, h],
            device_id=at((0, 0, 0), other), device_id_type=MESH)

    labels[0, core] = lab_ref[...].astype(jnp.float32)
    load.wait()

    def normalise(h):
        e = emb[pl.ds(h * part, part)]
        squares = jnp.sum(e * e, axis=1, keepdims=True)
        buf[0, core, pl.ds(h * part, part)] = (e * lax.rsqrt(squares + 1e-06)).astype(jnp.bfloat16)

    for h in range(chunks):
        normalise(h)
    pl.semaphore_wait(barrier, len(friends))

    for which in (0, 1):
        @pl.when(core == which)
        def _(which=which):
            for h, target, direction in FIRST_SENDS[which]:
                relay(0, target, h, direction).start()

    for h in range(chunks):
        share(0, h, core).start()

    def tell(slot, on, flip):
        return pltpu.make_async_remote_copy(
            src_ref=labels.at[0, core], dst_ref=labels.at[slot, core],
            send_sem=label_send.at[slot, flip], recv_sem=label_recv.at[1 if slot else 0],
            device_id=at(OFFSETS[slot], on), device_id_type=MESH)

    tell(0, other, 1).start()
    for slot in range(1, SLOTS):
        tell(slot, core, 0).start()
        tell(slot, other, 1).start()

    def clear(slot, carry):
        row_best[slot] = jnp.full(row_best.shape[1:], FILL, jnp.float32)
        column_best[slot] = jnp.full(column_best.shape[1:], FILL, jnp.float32)
        return carry

    lax.fori_loop(0, SLOTS, clear, 0)

    pltpu.make_async_copy(labels.at[0, other], labels.at[0, other], label_recv.at[0]).wait()
    rest = labels.at[pl.ds(1, SLOTS - 1)]
    pltpu.make_async_copy(rest, rest, label_recv.at[1]).wait()

    def spread(slot, carry):
        for unit in (0, 1):
            line = jnp.broadcast_to(labels[slot, unit], (128, rows))
            label_rows[slot, pl.ds(unit * rows, rows)] = line.T
        return carry

    lax.fori_loop(0, SLOTS, spread, 0)

    def tile(i, j, own=False):
        sims = lax.dot_general(buf[i].reshape(2 * rows, width), buf[j, core], (((1,), (1,)), ((), ())),
                               preferred_element_type=jnp.float32)
        names = label_rows[i]
        best = row_best[i]
        if own:
            row_at = lax.broadcasted_iota(jnp.int32, (2 * rows, 128), 0) - core * rows
            column_at = lax.broadcasted_iota(jnp.int32, (2 * rows, 128), 1)
        for k in range(rows // 128):
            lanes = slice(k * 128, (k + 1) * 128)
            keep = names == labels[j, core, :, lanes]
            if own:
                keep = keep & (row_at != column_at + k * 128)
            scores = jnp.where(keep, sims[:, lanes], FILL)
            best = jnp.maximum(best, scores)
            column_best[j, :, lanes] = jnp.maximum(
                column_best[j, :, lanes], jnp.max(scores.reshape(2 * rows // 8, 8, 128), axis=0))
        row_best[i] = best

    def answer(slot, unit):
        back = tuple(-k for k in OFFSETS[slot])
        return pltpu.make_async_remote_copy(
            src_ref=outgoing.at[slot, unit], dst_ref=incoming.at[slot, core],
            send_sem=result_send.at[slot, unit], recv_sem=result_recv.at[1 if slot else 0],
            device_id=at(back, unit), device_id_type=MESH)

    def finish(slot):
        by_row = jnp.max(row_best[slot].T, axis=0, keepdims=True)
        by_column = jnp.max(column_best[slot], axis=0, keepdims=True)
        for unit in (0, 1):
            mine = by_row[:, unit * rows:(unit + 1) * rows]
            outgoing[slot, unit] = jnp.where(core == unit, jnp.maximum(mine, by_column), mine)
        if slot:
            answer(slot, 0).start()
            answer(slot, 1).start()
        else:
            incoming[0, core] = outgoing[0, core]
            answer(0, other).start()

    for before, pair in STEPS:
        for which in (0, 1):
            if not before[which]:
                continue

            @pl.when(core == which)
            def _(todo=before[which]):
                for op in todo:
                    if op[0] == "a":
                        slot, h = op[1], op[2]
                        pltpu.make_async_copy(
                            chunk_of(slot, h, core), chunk_of(slot, h, core), recv_sem.at[slot, h]).wait()
                        for target, direction in op[3]:
                            relay(slot, target, h, direction).start()
                        share(slot, h, core).start()
                    elif op[0] == "o":
                        for h in range(chunks):
                            pltpu.make_async_copy(
                                chunk_of(op[1], h, other), chunk_of(op[1], h, other), take_sem.at[op[1], h]).wait()
                    else:
                        finish(op[1])
        if pair is not None:
            (i, j), (p, q) = pair
            tile(i + core * (p - i), j + core * (q - j), own=(i == j))

    pltpu.make_async_copy(incoming.at[0, other], incoming.at[0, other], result_recv.at[0]).wait()
    rest = incoming.at[pl.ds(1, SLOTS - 1)]
    pltpu.make_async_copy(rest, rest, result_recv.at[1]).wait()
    out_ref[...] = jnp.max(incoming[...].reshape(2 * SLOTS, 1, rows), axis=0)

    shared = {w: {op[1] for before, _ in STEPS for op in before[w] if op[0] == "o"} for w in (0, 1)}
    for which in (0, 1):
        @pl.when(core == which)
        def _(which=which):
            for slot in range(SLOTS):
                if slot not in shared[which]:
                    for h in range(chunks):
                        pltpu.make_async_copy(
                            chunk_of(slot, h, other), chunk_of(slot, h, other), take_sem.at[slot, h]).wait()
    for slot in range(SLOTS):
        for h in range(chunks):
            share(slot, h, core).wait_send()
            if slot:
                relay(0, slot, h, 0).wait_send()
        if slot:
            tell(slot, core, 0).wait_send()
            answer(slot, 0).wait_send()
            answer(slot, 1).wait_send()
        else:
            answer(0, other).wait_send()
        tell(slot, other, 1).wait_send()


def body(embeddings, cluster_ids):
    rows, width = embeddings.shape
    chunks = 1 + max(h for h, _, _ in FIRST_SENDS[0])
    copies = pltpu.SemaphoreType.DMA((SLOTS, chunks))
    pairs = pltpu.SemaphoreType.DMA((SLOTS, 2))
    best = pl.pallas_call(
        functools.partial(kernel, chunks),
        out_shape=jax.ShapeDtypeStruct((1, rows), jnp.float32),
        in_specs=[pl.BlockSpec(memory_space=pl.ANY), pl.BlockSpec(memory_space=pltpu.VMEM)],
        out_specs=pl.BlockSpec(memory_space=pltpu.VMEM),
        scratch_shapes=[
            pltpu.VMEM((rows, width), jnp.float32),
            pltpu.VMEM((SLOTS, 2, rows, width), jnp.bfloat16),
            pltpu.VMEM((SLOTS, 2, 1, rows), jnp.float32),
            pltpu.VMEM((SLOTS, 2 * rows, 128), jnp.float32),
            pltpu.VMEM((SLOTS, 2 * rows, 128), jnp.float32),
            pltpu.VMEM((SLOTS, 8, rows), jnp.float32),
            pltpu.VMEM((SLOTS, 2, 1, rows), jnp.float32),
            pltpu.VMEM((SLOTS, 2, 1, rows), jnp.float32),
            pltpu.SemaphoreType.DMA,
            copies, copies, copies, copies,
            pairs, pltpu.SemaphoreType.DMA((2,)),
            pairs, pltpu.SemaphoreType.DMA((2,)),
        ],
        compiler_params=pltpu.CompilerParams(
            collective_id=0, has_side_effects=True, vmem_limit_bytes=48 * 1024 * 1024),
    )(embeddings, cluster_ids.reshape(1, rows))
    return best.reshape(rows)


def solution(mesh):
    return jax.shard_map(
        body,
        mesh=mesh,
        in_specs=(P(("grp", "mem"), None), P(("grp", "mem"), None)),
        out_specs=P(("grp", "mem")),
        check_vma=False,
    )
```

time: 190 us -> 68.3 us (0.36)
  Pallas kernels: 0 us -> 65.8 us
  blocking collectives: 52.4 us -> 0 us
  waiting for transfers between devices: 50.7 us -> 0 us
  matrix products: 31.8 us -> 0 us
  local copies, waits for them, and re-layouts: 30.6 us -> 2.38 us
  between operations: 13.5 us -> 0.01 us
  other arithmetic: 6.5 us -> 0 us
  starting transfers between devices: 3.2 us -> 0 us
    pallas_call x0 -> x1, Pallas kernels: none -> 65.8 us  [body(): pl.pallas_call(functools.partial(kernel, chunks), out_shape=jax.ShapeDtyp...]
    all_gather x1 -> x0, waiting for transfers between devices: 46.5 us -> none  [body(): piece = lax.all_gather(mine, 'mem', axis=1, tiled=True)]
    dot_general x8 -> x0, matrix products: 31.8 us -> none  [masked_scores(): jnp.einsum('csd,ctd->cst', mine, piece, preferred_element_type=jnp.float32)]
    all_gather x1 -> x0, blocking collectives: 28.4 us -> none  [body(): piece_valid = lax.all_gather(mine_valid, 'mem', axis=1, tiled=True)]
    scatter x3 -> x0, local copies, waits for them, and re-layouts: 27.6 us -> none  [the longest x1 15.3 us: body(): jnp.zeros((owned, groups, capacity, width), jnp.bfloat16)]
    all_to_all x2 -> x0, blocking collectives: 24 us -> none  [the longest x1 16.1 us: body(): lax.all_to_all(outgoing, 'grp', split_axis=1, concat_axis=1, tiled=True)]
    all_to_all x1 -> x0, waiting for transfers between devices: 4.16 us -> none  [body(): lax.all_to_all(flags, 'grp', split_axis=1, concat_axis=1, tiled=True)]
    all_to_all x1 -> x0, starting transfers between devices: 3.2 us -> none  [body(): lax.all_to_all(flags, 'grp', split_axis=1, concat_axis=1, tiled=True)]
  transfers between devices with their start and end apart: 2 -> 0, of which waited for: 2 -> 0; matrix products, arithmetic and copies ran while one was open for 7% -> 0% of each run, Pallas kernels for 0% -> 0%
where the time goes in v1:
time: 68.3 us; the launch traced here: 68.2 us
  Pallas kernels  65.8 us (96%)
  local copies, waits for them, and re-layouts  2.38 us (3%)
    pallas_call x1, Pallas kernels, body(): pl.pallas_call(functools.partial(kernel, chunks), out_shape=jax.ShapeDtyp...  65.8 us
    unnamed x5, local copies, waits for them, and re-layouts  2.38 us

profile of v1, /device:TPU:1, one launch (start us, length us, event | category | flops | bytes accessed | tf_op | source)
XLA Modules:
  0.0 68.2 jit_solution(12308012516923954900)
XLA Ops:
  0.0 0.0 copy-start.1
  0.0 0.7 copy-done.1
  0.7 0.0 copy-start
  0.7 1.1 %copy-done = f32[256,768]{1,0:T(8,128)S(1)} copy-done((f32[256,768]{1,0:T(8,128)S(1)}, f32[256,768]{1,0:T(8,128)}, u32[]{:S(2)}) %copy-start) | copy-done | bytes 786456
  1.8 65.8 %shard_map.28 = f32[1,256]{1,0:T(1,128)S(1)} custom-call(f32[256,768]{1,0:T(8,128)S(1)} %copy-done, s32[1,256]{1,0:T(1,128)S(1)} %bitcast.3), custom_call_target="tpu_custom_call" | custom-call | tf_op jit(solution)/shard_map/pallas_call | solution.py:278
  67.6 0.6 copy.4
Async XLA Ops:
  0.0 0.7 copy-start.1
  0.7 1.1 %copy-start = (f32[256,768]{1,0:T(8,128)S(1)}, f32[256,768]{1,0:T(8,128)}, u32[]{:S(2)}) copy-start(f32[256,768]{1,0:T(8,128)} %emb_ref.1) | copy-start | bytes 2359300

commit v2 on v1

--- a/solution.py
+++ b/solution.py
@@ -10,6 +10,7 @@
 FILL = -4.0
 MESH = pl.DeviceIdType.MESH
 SIDE = 4
+VMEM_BYTES = 64 * 1024 * 1024 - 512 * 1024
 DIRS = ((1, 0, 0), (3, 0, 0), (0, 1, 0), (0, 3, 0), (0, 0, 1), (0, 0, 3))
 
 OFFSETS = (
@@ -86,11 +87,43 @@
     return near + far
 
 
-def kernel(chunks, emb_ref, lab_ref, out_ref, emb, buf, labels, label_rows, row_best, column_best, outgoing,
-           incoming, load_sem, send_sem, recv_sem, give_sem, take_sem, label_send, label_recv, result_send,
-           result_recv):
+def packed(values, bits):
+    return sum(v << (bits * n) for n, v in enumerate(values))
+
+
+def digit(word, n, bits):
+    return lax.rem(lax.shift_right_logical(word, bits * n), 1 << bits)
+
+
+def lookup(values, n):
+    words = [packed(values[k:k + 7], 4) for k in range(0, len(values), 7)]
+    word = jnp.int32(words[0])
+    for k, w in enumerate(words[1:], 1):
+        word = jnp.where(n >= 7 * k, jnp.int32(w), word)
+    return digit(word, lax.rem(n, 7), 4)
+
+
+NONE = 15
+
+
+def finishing(which):
+    waiting, at_step = [], []
+    for before, pair in STEPS:
+        waiting += [op[1] for op in before[which] if op[0] == "f"]
+        if pair is not None:
+            at_step.append(waiting.pop(0) if waiting else NONE)
+    return at_step, waiting
+
+
+def kernel(chunks, emb_ref, lab_ref, out_ref, emb, ids, buf, labels, label_rows, row_best, column_best, outgoing,
+           incoming, load_sem, send_sem, recv_sem, give_sem, take_sem, label_send,
+           label_recv, result_send, result_recv):
     rows, width = emb.shape
     part = rows // chunks
+    load = pltpu.make_async_copy(emb_ref, emb, load_sem.at[0])
+    load.start()
+    load_ids = pltpu.make_async_copy(lab_ref, ids, load_sem.at[1])
+    load_ids.start()
     gx = lax.axis_index("grp")
     mem = lax.axis_index("mem")
     core = lax.rem(mem, 2)
@@ -105,8 +138,6 @@
         x, y, z = (k % SIDE for k in offset)
         return (xs[x], (zs[z] * SIDE + ys[y]) * 2 + on)
 
-    load = pltpu.make_async_copy(emb_ref, emb, load_sem)
-    load.start()
     barrier = pltpu.get_barrier_semaphore()
     friends = greeted()
     for offset, flip in friends:
@@ -127,16 +158,13 @@
             send_sem=give_sem.at[slot, h], recv_sem=take_sem.at[slot, h],
             device_id=at((0, 0, 0), other), device_id_type=MESH)
 
-    labels[0, core] = lab_ref[...].astype(jnp.float32)
+    load_ids.wait()
+    labels[0, core] = ids[...].astype(jnp.float32)
     load.wait()
-
-    def normalise(h):
+    for h in range(chunks):
         e = emb[pl.ds(h * part, part)]
         squares = jnp.sum(e * e, axis=1, keepdims=True)
         buf[0, core, pl.ds(h * part, part)] = (e * lax.rsqrt(squares + 1e-06)).astype(jnp.bfloat16)
-
-    for h in range(chunks):
-        normalise(h)
     pl.semaphore_wait(barrier, len(friends))
 
     for which in (0, 1):
@@ -198,11 +226,29 @@
         row_best[i] = best
 
     def answer(slot, unit):
-        back = tuple(-k for k in OFFSETS[slot])
+        x, y, z = (SIDE - digit(jnp.int32(packed([o[k] for o in OFFSETS], 2)), slot, 2) for k in range(3))
+        x, y, z = lax.rem(gx + x, SIDE), lax.rem(gy + y, SIDE), lax.rem(gz + z, SIDE)
         return pltpu.make_async_remote_copy(
             src_ref=outgoing.at[slot, unit], dst_ref=incoming.at[slot, core],
-            send_sem=result_send.at[slot, unit], recv_sem=result_recv.at[1 if slot else 0],
-            device_id=at(back, unit), device_id_type=MESH)
+            send_sem=result_send.at[slot, unit], recv_sem=result_recv.at[1],
+            device_id=(x, (z * SIDE + y) * 2 + unit), device_id_type=MESH)
+
+    def answer_chip():
+        return pltpu.make_async_remote_copy(
+            src_ref=outgoing.at[0, other], dst_ref=incoming.at[0, core],
+            send_sem=result_send.at[0, 0], recv_sem=result_recv.at[0],
+            device_id=at((0, 0, 0), other), device_id_type=MESH)
+
+    def arrived(slot, h, onward):
+        pltpu.make_async_copy(chunk_of(slot, h, core), chunk_of(slot, h, core), recv_sem.at[slot, h]).wait()
+        for target, direction in onward:
+            relay(slot, target, h, direction).start()
+        share(slot, h, core).start()
+
+    def taken(slot):
+        for h in range(chunks):
+            pltpu.make_async_copy(
+                chunk_of(slot, h, other), chunk_of(slot, h, other), take_sem.at[slot, h]).wait()
 
     def finish(slot):
         by_row = jnp.max(row_best[slot].T, axis=0, keepdims=True)
@@ -210,52 +256,81 @@
         for unit in (0, 1):
             mine = by_row[:, unit * rows:(unit + 1) * rows]
             outgoing[slot, unit] = jnp.where(core == unit, jnp.maximum(mine, by_column), mine)
-        if slot:
+
+        @pl.when(slot > 0)
+        def _():
             answer(slot, 0).start()
             answer(slot, 1).start()
-        else:
+
+        @pl.when(slot == 0)
+        def _():
             incoming[0, core] = outgoing[0, core]
-            answer(0, other).start()
-
-    for before, pair in STEPS:
+            answer_chip().start()
+
+    def handle(before):
         for which in (0, 1):
-            if not before[which]:
-                continue
-
-            @pl.when(core == which)
-            def _(todo=before[which]):
-                for op in todo:
-                    if op[0] == "a":
-                        slot, h = op[1], op[2]
-                        pltpu.make_async_copy(
-                            chunk_of(slot, h, core), chunk_of(slot, h, core), recv_sem.at[slot, h]).wait()
-                        for target, direction in op[3]:
-                            relay(slot, target, h, direction).start()
-                        share(slot, h, core).start()
-                    elif op[0] == "o":
-                        for h in range(chunks):
-                            pltpu.make_async_copy(
-                                chunk_of(op[1], h, other), chunk_of(op[1], h, other), take_sem.at[op[1], h]).wait()
-                    else:
-                        finish(op[1])
-        if pair is not None:
-            (i, j), (p, q) = pair
-            tile(i + core * (p - i), j + core * (q - j), own=(i == j))
+            todo = [op for op in before[which] if op[0] != "f"]
+            if todo:
+                @pl.when(core == which)
+                def _(todo=todo):
+                    for op in todo:
+                        if op[0] == "a":
+                            arrived(*op[1:])
+                        else:
+                            taken(op[1])
+
+    ends = [finishing(0), finishing(1)]
+    pairs = [pair for _, pair in STEPS if pair is not None]
+
+    def chosen(values, n):
+        return jnp.where(core == 0, lookup(values[0], n), lookup(values[1], n))
+
+    taken(0)
+    tile(0, 0, own=True)
+
+    def step(n, carry):
+        for g in range(0, len(pairs), 6):
+            @pl.when(lax.div(n, 6) == g // 6)
+            def _(g=g):
+                for k in range(max(g, 1), min(g + 6, len(pairs))):
+                    @pl.when(n == k)
+                    def _(k=k):
+                        handle(STEPS[k][0])
+        ended = chosen([e[0] for e in ends], n)
+
+        @pl.when(ended != NONE)
+        def _():
+            finish(ended)
+        tile(chosen([[p[w][0] for p in pairs] for w in (0, 1)], n),
+             chosen([[p[w][1] for p in pairs] for w in (0, 1)], n))
+        return carry
+
+    lax.fori_loop(1, len(pairs), step, 0)
+    handle(STEPS[-1][0])
+    left = max(len(e[1]) for e in ends)
+
+    def last(n, carry):
+        ended = chosen([(e[1] + [NONE] * left)[:left] for e in ends], n)
+
+        @pl.when(ended != NONE)
+        def _():
+            finish(ended)
+        return carry
+
+    lax.fori_loop(0, left, last, 0)
 
     pltpu.make_async_copy(incoming.at[0, other], incoming.at[0, other], result_recv.at[0]).wait()
     rest = incoming.at[pl.ds(1, SLOTS - 1)]
     pltpu.make_async_copy(rest, rest, result_recv.at[1]).wait()
     out_ref[...] = jnp.max(incoming[...].reshape(2 * SLOTS, 1, rows), axis=0)
 
-    shared = {w: {op[1] for before, _ in STEPS for op in before[w] if op[0] == "o"} for w in (0, 1)}
+    shared = [{op[1] for before, _ in STEPS for op in before[w] if op[0] == "o"} for w in (0, 1)]
     for which in (0, 1):
         @pl.when(core == which)
         def _(which=which):
             for slot in range(SLOTS):
                 if slot not in shared[which]:
-                    for h in range(chunks):
-                        pltpu.make_async_copy(
-                            chunk_of(slot, h, other), chunk_of(slot, h, other), take_sem.at[slot, h]).wait()
+                    taken(slot)
     for slot in range(SLOTS):
         for h in range(chunks):
             share(slot, h, core).wait_send()
@@ -266,7 +341,7 @@
             answer(slot, 0).wait_send()
             answer(slot, 1).wait_send()
         else:
-            answer(0, other).wait_send()
+            answer_chip().wait_send()
         tell(slot, other, 1).wait_send()
 
 
@@ -278,10 +353,11 @@
     best = pl.pallas_call(
         functools.partial(kernel, chunks),
         out_shape=jax.ShapeDtypeStruct((1, rows), jnp.float32),
-        in_specs=[pl.BlockSpec(memory_space=pl.ANY), pl.BlockSpec(memory_space=pltpu.VMEM)],
+        in_specs=[pl.BlockSpec(memory_space=pl.ANY), pl.BlockSpec(memory_space=pl.ANY)],
         out_specs=pl.BlockSpec(memory_space=pltpu.VMEM),
         scratch_shapes=[
             pltpu.VMEM((rows, width), jnp.float32),
+            pltpu.VMEM((1, rows), jnp.int32),
             pltpu.VMEM((SLOTS, 2, rows, width), jnp.bfloat16),
             pltpu.VMEM((SLOTS, 2, 1, rows), jnp.float32),
             pltpu.VMEM((SLOTS, 2 * rows, 128), jnp.float32),
@@ -289,13 +365,13 @@
             pltpu.VMEM((SLOTS, 8, rows), jnp.float32),
             pltpu.VMEM((SLOTS, 2, 1, rows), jnp.float32),
             pltpu.VMEM((SLOTS, 2, 1, rows), jnp.float32),
-            pltpu.SemaphoreType.DMA,
+            pltpu.SemaphoreType.DMA((2,)),
             copies, copies, copies, copies,
             pairs, pltpu.SemaphoreType.DMA((2,)),
             pairs, pltpu.SemaphoreType.DMA((2,)),
         ],
         compiler_params=pltpu.CompilerParams(
-            collective_id=0, has_side_effects=True, vmem_limit_bytes=48 * 1024 * 1024),
+            collective_id=0, has_side_effects=True, vmem_limit_bytes=VMEM_BYTES),
     )(embeddings, cluster_ids.reshape(1, rows))
     return best.reshape(rows)
 

time: 68.3 us -> 67.6 us (0.990)
  local copies, waits for them, and re-layouts: 2.38 us -> 1.22 us
    unnamed x5 -> x3, local copies, waits for them, and re-layouts: 2.38 us -> 1.22 us
where the time goes in v2:
time: 67.6 us; the launch traced here: 67.5 us
  Pallas kernels  66.2 us (98%)
  local copies, waits for them, and re-layouts  1.22 us (2%)
    pallas_call x1, Pallas kernels, body(): pl.pallas_call(functools.partial(kernel, chunks), out_shape=jax.ShapeDtyp...  66.2 us

profile of v2, /device:TPU:1, one launch (start us, length us, event | category | flops | bytes accessed | tf_op | source)
XLA Modules:
  0.0 67.5 jit_solution(13635004189190793370)
XLA Ops:
  0.0 66.2 %shard_map.28 = f32[1,256]{1,0:T(1,128)} custom-call(f32[256,768]{1,0:T(8,128)} %emb_ref.1, s32[1,256]{1,0:T(1,128)} %bitcast.3), custom_call_target="tpu_custom_call" | custom-call | tf_op jit(solution)/shard_map/pallas_call | solution.py:353
  66.2 0.0 copy-start
  66.3 0.7 copy-done
  66.9 0.6 copy.4
Async XLA Ops:
  66.2 0.7 copy-start

commit v3 on v2

--- a/solution.py
+++ b/solution.py
@@ -29,48 +29,93 @@
 )
 
 FIRST_SENDS = (
-    ((0, 3, 5), (0, 4, 1), (0, 9, 3), (1, 3, 5), (1, 4, 1), (1, 5, 2), (0, 5, 2), (1, 9, 3)),
-    ((1, 5, 2), (0, 3, 5), (0, 4, 1), (0, 5, 2), (0, 9, 3), (1, 3, 5), (1, 4, 1), (1, 9, 3)),
+    ((0, 4, 0, 1), (0, 9, 0, 3), (0, 3, 0, 5)),
+    ((0, 5, 1, 2),),
 )
 
+LAST_SENDS = (
+    ((1, 1), (2, 1), (7, 1), (8, 0), (8, 1), (10, 1)),
+    ((1, 1), (2, 1), (8, 0), (8, 1), (9, 1), (10, 1)),
+)
+
 STEPS = (
-    (((('o', 0),), (('o', 0),)), ((0, 0), (0, 0))),
-    (((('a', 3, 0, ((1, 5),)), ('a', 4, 0, ((11, 4),)), ('a', 9, 0, ((7, 3),)), ('a', 11, 0, ((10, 1),)), ('a', 3, 1, ((1, 5),)), ('a', 4, 1, ((11, 4),)), ('a', 5, 1, ((6, 0),)), ('a', 7, 0, ((8, 0),))), (('a', 5, 1, ((6, 0), (7, 2))), ('a', 3, 0, ((1, 5),)), ('a', 4, 0, ((11, 4),)), ('a', 5, 0, ((6, 0),)), ('a', 9, 0, ((7, 3),)))), ((0, 3), (0, 5))),
-    (((), (('a', 6, 1, ()), ('a', 6, 0, ((8, 2),)), ('a', 11, 0, ((10, 1),)))), ((0, 4), (0, 6))),
-    (((('a', 5, 0, ((6, 0),)), ('a', 9, 1, ((7, 3),))), (('a', 3, 1, ((1, 5),)), ('a', 4, 1, ((11, 4),)))), ((0, 5), (0, 3))),
-    (((('o', 5),), ()), ((5, 3), (0, 4))),
-    (((('a', 6, 1, ((8, 2),)), ('a', 11, 1, ((10, 1),))), (('o', 3),)), ((5, 9), (3, 6))),
-    (((('o', 3),), (('o', 4),)), ((3, 9), (4, 3))),
-    (((('o', 4),), ()), ((4, 3), (4, 6))),
-    (((('a', 1, 0, ()), ('a', 10, 0, ((2, 4),))), (('a', 7, 0, ()), ('a', 7, 1, ((8, 0),)), ('o', 5))), ((4, 5), (5, 3))),
-    (((), ()), ((3, 11), (0, 7))),
-    (((('a', 6, 0, ()),), (('a', 11, 1, ((10, 1),)),)), ((5, 11), (3, 7))),
-    (((), ()), ((3, 6), (4, 7))),
-    (((), ()), ((4, 6), (3, 11))),
-    (((('a', 7, 1, ()), ('o', 11)), (('a', 1, 0, ()), ('a', 8, 0, ()), ('a', 10, 0, ((2, 4),)))), ((11, 6), (5, 11))),
-    (((), (('o', 11),)), ((11, 9), (11, 6))),
-    (((('a', 2, 0, ()), ('a', 8, 0, ())), ()), ((3, 7), (11, 7))),
-    (((), (('o', 6),)), ((4, 7), (6, 7))),
-    (((('o', 6),), (('a', 9, 1, ()),)), ((6, 7), (3, 9))),
-    (((('a', 1, 1, ()), ('a', 8, 1, ()), ('a', 10, 1, ((2, 4),))), ()), ((11, 7), (11, 9))),
-    (((), (('a', 2, 0, ()), ('a', 8, 1, ()))), ((0, 1), (3, 8))),
-    (((), ()), ((0, 10), (4, 8))),
-    (((('f', 0),), (('f', 4),)), ((3, 8), (11, 8))),
-    (((), (('a', 1, 1, ()), ('a', 10, 1, ((2, 4),)))), ((3, 10), (0, 1))),
-    (((('f', 3),), ()), ((4, 8), (0, 10))),
-    (((('f', 4), ('a', 2, 1, ())), (('f', 0),)), ((5, 1), (3, 10))),
-    (((), (('f', 3),)), ((6, 1), (5, 1))),
-    (((), ()), ((6, 10), (6, 1))),
-    (((('o', 7),), ()), ((7, 1), (6, 10))),
-    (((), (('a', 2, 1, ()), ('o', 7))), ((11, 1), (7, 1))),
-    (((), (('o', 8),)), ((11, 8), (8, 1))),
-    (((('f', 11), ('o', 9)), (('f', 8), ('o', 9))), ((9, 10), (9, 10))),
-    (((('f', 9), ('f', 10), ('o', 8)), (('f', 9), ('f', 10))), ((8, 1), (11, 1))),
-    (((('f', 8), ('o', 1)), (('f', 11), ('o', 1))), ((1, 2), (1, 2))),
-    (((('f', 1),), (('f', 1),)), ((5, 2), (5, 2))),
-    (((('f', 5),), (('f', 5),)), ((6, 2), (6, 2))),
-    (((('f', 6),), (('f', 6),)), ((7, 2), (7, 2))),
-    (((('f', 2), ('f', 7)), (('f', 2), ('f', 7))), None),
+    (((), 0, None, 0, 0),
+     ((), 0, None, 0, 0)),
+    (((('a', 3, 0), ('a', 4, 0), ('a', 9, 0), ('s', 4, 11, 0, 4), ('s', 0, 4, 1, 1, 4, 0), ('s', 0, 5, 1, 2), ('s', 9, 7, 0, 3, 9, 0), ('s', 0, 3, 1, 5, 3, 0), ('a', 11, 0), ('s', 0, 5, 0, 2, 5, 1), ('s', 0, 9, 1, 3, 7, 0), ('a', 3, 1), ('a', 4, 1), ('a', 5, 1), ('a', 7, 0)), None, None, 0, 3),
+     ((('s', 0, 4, 0, 1), ('s', 0, 5, 0, 2, 5, 1), ('s', 0, 9, 0, 3), ('s', 0, 3, 0, 5), ('a', 5, 1), ('s', 5, 6, 1, 0), ('a', 3, 0), ('a', 4, 0), ('a', 5, 0), ('a', 9, 0)), None, None, 0, 5)),
+    (((('s', 5, 6, 1, 0), ('s', 4, 11, 1, 4, 11, 0)), None, None, 0, 4),
+     ((('s', 5, 6, 0, 0, 6, 1), ('s', 4, 11, 0, 4), ('a', 6, 1), ('s', 0, 4, 1, 1, 4, 0), ('s', 0, 3, 1, 5, 3, 0), ('a', 6, 0), ('a', 11, 0)), None, None, 0, 6)),
+    (((('s', 11, 10, 0, 1, 4, 1), ('s', 3, 1, 0, 5, 3, 1), ('a', 5, 0), ('a', 9, 1)), None, None, 0, 5),
+     ((('s', 5, 7, 1, 2, 5, 0), ('s', 9, 7, 0, 3, 9, 0), ('a', 3, 1), ('a', 4, 1)), None, None, 0, 3)),
+    (((('s', 5, 6, 0, 0, 6, 1),), 5, None, 5, 3),
+     ((('s', 4, 11, 1, 4, 11, 0),), None, None, 0, 4)),
+    (((('a', 6, 1), ('a', 11, 1)), None, None, 5, 9),
+     ((), 3, None, 3, 6)),
+    (((('s', 9, 7, 1, 3, 9, 1),), 3, None, 3, 9),
+     ((('s', 11, 10, 0, 1, 4, 1), ('s', 6, 8, 0, 2, 7, 1), ('s', 3, 1, 0, 5, 3, 1)), 4, None, 4, 3)),
+    (((('a', 1, 0), ('a', 10, 0), ('s', 7, 8, 0, 0, 6, 0), ('s', 10, 2, 0, 4, 11, 1)), 4, None, 4, 3),
+     ((('a', 7, 0), ('a', 7, 1)), None, None, 4, 6)),
+    (((), None, None, 4, 5),
+     ((), 5, None, 5, 3)),
+    (((('a', 6, 0),), None, None, 3, 11),
+     ((('a', 11, 1),), None, None, 0, 7)),
+    (((('s', 11, 10, 1, 1, 10, 0), ('s', 6, 8, 1, 2, 5, 0), ('s', 3, 1, 1, 5, 1, 0)), None, None, 5, 11),
+     ((('s', 0, 9, 1, 3, 7, 0),), None, None, 3, 7)),
+    (((), None, None, 3, 6),
+     ((), None, None, 4, 7)),
+    (((('a', 7, 1),), None, None, 4, 6),
+     ((('a', 1, 0), ('a', 8, 0), ('a', 10, 0), ('s', 7, 8, 1, 0, 6, 0), ('s', 10, 2, 0, 4, 11, 1)), None, None, 3, 11)),
+    (((('a', 2, 0), ('a', 8, 0)), 11, None, 11, 6),
+     ((), None, None, 5, 11)),
+    (((), None, None, 11, 9),
+     ((('s', 11, 10, 1, 1, 10, 0), ('s', 3, 1, 1, 5, 1, 0)), 11, None, 11, 6)),
+    (((), None, None, 3, 7),
+     ((), None, None, 11, 7)),
+    (((('a', 1, 1), ('a', 8, 1), ('a', 10, 1), ('s', 10, 2, 1, 4, 2, 0)), None, None, 4, 7),
+     ((('a', 9, 1),), 6, None, 6, 7)),
+    (((), 6, None, 6, 7),
+     ((('a', 2, 0), ('a', 8, 1)), None, None, 3, 9)),
+    (((), None, None, 11, 7),
+     ((), None, None, 11, 9)),
+    (((), None, None, 0, 1),
+     ((), None, None, 3, 8)),
+    (((), None, None, 0, 10),
+     ((('a', 1, 1), ('a', 10, 1), ('s', 10, 2, 1, 4, 2, 0)), None, None, 4, 8)),
+    (((('a', 2, 1),), None, 0, 3, 8),
+     ((), None, 4, 11, 8)),
+    (((), None, None, 3, 10),
+     ((), None, None, 0, 1)),
+    (((), None, 3, 4, 8),
+     ((), None, None, 0, 10)),
+    (((), None, 4, 5, 1),
+     ((), None, 0, 3, 10)),
+    (((), None, None, 6, 1),
+     ((('a', 2, 1),), None, 3, 5, 1)),
+    (((), None, None, 6, 10),
+     ((), None, None, 6, 1)),
+    (((), 7, None, 7, 1),
+     ((), None, None, 6, 10)),
+    (((), None, None, 11, 1),
+     ((), 7, None, 7, 1)),
+    (((), None, None, 11, 8),
+     ((), 8, None, 8, 1)),
+    (((), 9, 11, 9, 10),
+     ((), 9, 8, 9, 10)),
+    (((), 8, 9, 8, 1),
+     ((), None, 9, 11, 1)),
+    (((), 1, 10, 1, 2),
+     ((), 1, 10, 1, 2)),
+    (((), None, 8, 5, 2),
+     ((), None, 11, 5, 2)),
+    (((), None, 1, 6, 2),
+     ((), None, 1, 6, 2)),
+    (((), None, 5, 7, 2),
+     ((), None, 5, 7, 2)),
+)
+
+TAIL = (
+    ((), (6, 7, 2)),
+    ((), (6, 7, 2)),
 )
 
 
@@ -106,13 +151,8 @@
 NONE = 15
 
 
-def finishing(which):
-    waiting, at_step = [], []
-    for before, pair in STEPS:
-        waiting += [op[1] for op in before[which] if op[0] == "f"]
-        if pair is not None:
-            at_step.append(waiting.pop(0) if waiting else NONE)
-    return at_step, waiting
+def column(which, place):
+    return [NONE if pair[which][place] is None else pair[which][place] for pair in STEPS]
 
 
 def kernel(chunks, emb_ref, lab_ref, out_ref, emb, ids, buf, labels, label_rows, row_best, column_best, outgoing,
@@ -165,13 +205,20 @@
         e = emb[pl.ds(h * part, part)]
         squares = jnp.sum(e * e, axis=1, keepdims=True)
         buf[0, core, pl.ds(h * part, part)] = (e * lax.rsqrt(squares + 1e-06)).astype(jnp.bfloat16)
+
+    def clear(slot, carry):
+        row_best[slot] = jnp.full(row_best.shape[1:], FILL, jnp.float32)
+        column_best[slot] = jnp.full(column_best.shape[1:], FILL, jnp.float32)
+        return carry
+
+    lax.fori_loop(0, SLOTS, clear, 0)
     pl.semaphore_wait(barrier, len(friends))
 
     for which in (0, 1):
         @pl.when(core == which)
         def _(which=which):
-            for h, target, direction in FIRST_SENDS[which]:
-                relay(0, target, h, direction).start()
+            for move in FIRST_SENDS[which]:
+                relay(*move).start()
 
     for h in range(chunks):
         share(0, h, core).start()
@@ -187,24 +234,14 @@
         tell(slot, core, 0).start()
         tell(slot, other, 1).start()
 
-    def clear(slot, carry):
-        row_best[slot] = jnp.full(row_best.shape[1:], FILL, jnp.float32)
-        column_best[slot] = jnp.full(column_best.shape[1:], FILL, jnp.float32)
-        return carry
-
-    lax.fori_loop(0, SLOTS, clear, 0)
-
     pltpu.make_async_copy(labels.at[0, other], labels.at[0, other], label_recv.at[0]).wait()
     rest = labels.at[pl.ds(1, SLOTS - 1)]
     pltpu.make_async_copy(rest, rest, label_recv.at[1]).wait()
 
-    def spread(slot, carry):
+    def spread(slot):
         for unit in (0, 1):
             line = jnp.broadcast_to(labels[slot, unit], (128, rows))
             label_rows[slot, pl.ds(unit * rows, rows)] = line.T
-        return carry
-
-    lax.fori_loop(0, SLOTS, spread, 0)
 
     def tile(i, j, own=False):
         sims = lax.dot_general(buf[i].reshape(2 * rows, width), buf[j, core], (((1,), (1,)), ((), ())),
@@ -239,11 +276,12 @@
             send_sem=result_send.at[0, 0], recv_sem=result_recv.at[0],
             device_id=at((0, 0, 0), other), device_id_type=MESH)
 
-    def arrived(slot, h, onward):
+    def arrived(slot, h):
         pltpu.make_async_copy(chunk_of(slot, h, core), chunk_of(slot, h, core), recv_sem.at[slot, h]).wait()
-        for target, direction in onward:
-            relay(slot, target, h, direction).start()
         share(slot, h, core).start()
+
+    def sent(slot, h):
+        relay(0, slot, h, 0).wait_send()
 
     def taken(slot):
         for h in range(chunks):
@@ -267,9 +305,9 @@
             incoming[0, core] = outgoing[0, core]
             answer_chip().start()
 
-    def handle(before):
+    def moves(n):
         for which in (0, 1):
-            todo = [op for op in before[which] if op[0] != "f"]
+            todo = STEPS[n][which][0]
             if todo:
                 @pl.when(core == which)
                 def _(todo=todo):
@@ -277,40 +315,45 @@
                         if op[0] == "a":
                             arrived(*op[1:])
                         else:
-                            taken(op[1])
-
-    ends = [finishing(0), finishing(1)]
-    pairs = [pair for _, pair in STEPS if pair is not None]
-
-    def chosen(values, n):
-        return jnp.where(core == 0, lookup(values[0], n), lookup(values[1], n))
+                            if len(op) > 5:
+                                sent(*op[5:])
+                            relay(*op[1:5]).start()
+
+    def chosen(place, n):
+        return jnp.where(core == 0, lookup(column(0, place), n), lookup(column(1, place), n))
 
     taken(0)
+    spread(0)
     tile(0, 0, own=True)
 
     def step(n, carry):
-        for g in range(0, len(pairs), 6):
+        for g in range(0, len(STEPS), 6):
             @pl.when(lax.div(n, 6) == g // 6)
             def _(g=g):
-                for k in range(max(g, 1), min(g + 6, len(pairs))):
+                for k in range(max(g, 1), min(g + 6, len(STEPS))):
                     @pl.when(n == k)
                     def _(k=k):
-                        handle(STEPS[k][0])
-        ended = chosen([e[0] for e in ends], n)
+                        moves(k)
+        opened, ended = chosen(1, n), chosen(2, n)
+
+        @pl.when(opened != NONE)
+        def _():
+            spread(opened)
+            taken(opened)
 
         @pl.when(ended != NONE)
         def _():
             finish(ended)
-        tile(chosen([[p[w][0] for p in pairs] for w in (0, 1)], n),
-             chosen([[p[w][1] for p in pairs] for w in (0, 1)], n))
+
+        tile(chosen(3, n), chosen(4, n))
         return carry
 
-    lax.fori_loop(1, len(pairs), step, 0)
-    handle(STEPS[-1][0])
-    left = max(len(e[1]) for e in ends)
+    lax.fori_loop(1, len(STEPS), step, 0)
+    left = max(len(t[1]) for t in TAIL)
 
     def last(n, carry):
-        ended = chosen([(e[1] + [NONE] * left)[:left] for e in ends], n)
+        ends = [(list(t[1]) + [NONE] * left)[:left] for t in TAIL]
+        ended = jnp.where(core == 0, lookup(ends[0], n), lookup(ends[1], n))
 
         @pl.when(ended != NONE)
         def _():
@@ -324,18 +367,17 @@
     pltpu.make_async_copy(rest, rest, result_recv.at[1]).wait()
     out_ref[...] = jnp.max(incoming[...].reshape(2 * SLOTS, 1, rows), axis=0)
 
-    shared = [{op[1] for before, _ in STEPS for op in before[w] if op[0] == "o"} for w in (0, 1)]
     for which in (0, 1):
         @pl.when(core == which)
         def _(which=which):
             for slot in range(SLOTS):
-                if slot not in shared[which]:
+                if slot not in column(which, 1):
                     taken(slot)
+            for move in LAST_SENDS[which]:
+                sent(*move)
     for slot in range(SLOTS):
         for h in range(chunks):
             share(slot, h, core).wait_send()
-            if slot:
-                relay(0, slot, h, 0).wait_send()
         if slot:
             tell(slot, core, 0).wait_send()
             answer(slot, 0).wait_send()
@@ -347,7 +389,7 @@
 
 def body(embeddings, cluster_ids):
     rows, width = embeddings.shape
-    chunks = 1 + max(h for h, _, _ in FIRST_SENDS[0])
+    chunks = 1 + max(h for sends in LAST_SENDS for _, h in sends)
     copies = pltpu.SemaphoreType.DMA((SLOTS, chunks))
     pairs = pltpu.SemaphoreType.DMA((SLOTS, 2))
     best = pl.pallas_call(

time: 67.6 us -> 61.5 us (0.910)
  Pallas kernels: 66.2 us -> 60.1 us
    pallas_call x1, Pallas kernels: 66.2 us -> 60.1 us  [body(): pl.pallas_call(functools.partial(kernel, chunks), out_shape=jax.ShapeDtyp...]
where the time goes in v3:
time: 61.5 us; the launch traced here: 61.3 us
  Pallas kernels  60.1 us (98%)
  local copies, waits for them, and re-layouts  1.22 us (2%)
    pallas_call x1, Pallas kernels, body(): pl.pallas_call(functools.partial(kernel, chunks), out_shape=jax.ShapeDtyp...  60.1 us

profile of v3, /device:TPU:1, one launch (start us, length us, event | category | flops | bytes accessed | tf_op | source)
XLA Modules:
  0.0 61.3 jit_solution(5713579465712239164)
XLA Ops:
  0.0 60.1 %shard_map.28 = f32[1,256]{1,0:T(1,128)} custom-call(f32[256,768]{1,0:T(8,128)} %emb_ref.1, s32[1,256]{1,0:T(1,128)} %bitcast.3), custom_call_target="tpu_custom_call" | custom-call | tf_op jit(solution)/shard_map/pallas_call | solution.py:395
  60.1 0.0 copy-start
  60.1 0.7 %copy-done = f32[1,256]{1,0:T(1,128)S(1)} copy-done((f32[1,256]{1,0:T(1,128)S(1)}, f32[1,256]{1,0:T(1,128)}, u32[]{:S(2)}) %copy-start) | copy-done | bytes 1048
  60.8 0.6 copy.4
Async XLA Ops:
  60.1 0.7 %copy-start = (f32[1,256]{1,0:T(1,128)S(1)}, f32[1,256]{1,0:T(1,128)}, u32[]{:S(2)}) copy-start(f32[1,256]{1,0:T(1,128)} %shard_map.28) | copy-start | bytes 3076

commit v4 on v3

--- a/solution.py
+++ b/solution.py
@@ -155,15 +155,7 @@
     return [NONE if pair[which][place] is None else pair[which][place] for pair in STEPS]
 
 
-def kernel(chunks, emb_ref, lab_ref, out_ref, emb, ids, buf, labels, label_rows, row_best, column_best, outgoing,
-           incoming, load_sem, send_sem, recv_sem, give_sem, take_sem, label_send,
-           label_recv, result_send, result_recv):
-    rows, width = emb.shape
-    part = rows // chunks
-    load = pltpu.make_async_copy(emb_ref, emb, load_sem.at[0])
-    load.start()
-    load_ids = pltpu.make_async_copy(lab_ref, ids, load_sem.at[1])
-    load_ids.start()
+def place():
     gx = lax.axis_index("grp")
     mem = lax.axis_index("mem")
     core = lax.rem(mem, 2)
@@ -178,6 +170,18 @@
         x, y, z = (k % SIDE for k in offset)
         return (xs[x], (zs[z] * SIDE + ys[y]) * 2 + on)
 
+    return core, other, gx, gy, gz, at
+
+
+def gather(chunks, emb_ref, lab_ref, rows_ref, names_ref, emb, ids, buf, labels, load_sem, send_sem, recv_sem,
+           give_sem, take_sem, label_send, label_recv, own_out, other_out):
+    rows, width = emb.shape
+    part = rows // chunks
+    load = pltpu.make_async_copy(emb_ref, emb, load_sem.at[0])
+    load.start()
+    load_ids = pltpu.make_async_copy(lab_ref, ids, load_sem.at[1])
+    load_ids.start()
+    core, other, gx, gy, gz, at = place()
     barrier = pltpu.get_barrier_semaphore()
     friends = greeted()
     for offset, flip in friends:
@@ -206,12 +210,6 @@
         squares = jnp.sum(e * e, axis=1, keepdims=True)
         buf[0, core, pl.ds(h * part, part)] = (e * lax.rsqrt(squares + 1e-06)).astype(jnp.bfloat16)
 
-    def clear(slot, carry):
-        row_best[slot] = jnp.full(row_best.shape[1:], FILL, jnp.float32)
-        column_best[slot] = jnp.full(column_best.shape[1:], FILL, jnp.float32)
-        return carry
-
-    lax.fori_loop(0, SLOTS, clear, 0)
     pl.semaphore_wait(barrier, len(friends))
 
     for which in (0, 1):
@@ -234,14 +232,101 @@
         tell(slot, core, 0).start()
         tell(slot, other, 1).start()
 
+    def write_out(slot, h, on, sem):
+        return pltpu.make_async_copy(
+            chunk_of(slot, h, on), rows_ref.at[slot, on, pl.ds(h * part, part)], sem.at[slot, h])
+
+    for h in range(chunks):
+        write_out(0, h, core, own_out).start()
+
     pltpu.make_async_copy(labels.at[0, other], labels.at[0, other], label_recv.at[0]).wait()
     rest = labels.at[pl.ds(1, SLOTS - 1)]
     pltpu.make_async_copy(rest, rest, label_recv.at[1]).wait()
 
-    def spread(slot):
+    def arrived(slot, h):
+        pltpu.make_async_copy(chunk_of(slot, h, core), chunk_of(slot, h, core), recv_sem.at[slot, h]).wait()
+        share(slot, h, core).start()
+        write_out(slot, h, core, own_out).start()
+
+    def sent(slot, h):
+        relay(0, slot, h, 0).wait_send()
+
+    def taken(slot):
+        for h in range(chunks):
+            pltpu.make_async_copy(
+                chunk_of(slot, h, other), chunk_of(slot, h, other), take_sem.at[slot, h]).wait()
+            write_out(slot, h, other, other_out).start()
+
+    labels_out = pltpu.make_async_copy(labels, names_ref, load_sem.at[0])
+    labels_out.start()
+    for n in range(len(STEPS)):
+        for which in (0, 1):
+            todo = STEPS[n][which][0]
+            first = [STEPS[n][which][1]] if STEPS[n][which][1] is not None else []
+            if todo or first:
+                @pl.when(core == which)
+                def _(todo=todo, first=first):
+                    for op in todo:
+                        if op[0] == "a":
+                            arrived(*op[1:])
+                        else:
+                            if len(op) > 5:
+                                sent(*op[5:])
+                            relay(*op[1:5]).start()
+                    for slot in first:
+                        taken(slot)
+
+    for which in (0, 1):
+        @pl.when(core == which)
+        def _(which=which):
+            for slot in range(SLOTS):
+                if slot not in column(which, 1):
+                    taken(slot)
+            for move in LAST_SENDS[which]:
+                sent(*move)
+    for slot in range(SLOTS):
+        for h in range(chunks):
+            share(slot, h, core).wait_send()
+            write_out(slot, h, core, own_out).wait()
+            write_out(slot, h, other, other_out).wait()
+        if slot:
+            tell(slot, core, 0).wait_send()
+        tell(slot, other, 1).wait_send()
+    labels_out.wait()
+
+
+def compare(rows_ref, names_ref, out_ref, buf, labels, label_rows, row_best, column_best, load_sem, names_sem):
+    rows, width = buf.shape[2:]
+    core = lax.rem(lax.axis_index("mem"), 2)
+    names_in = pltpu.make_async_copy(names_ref, labels, names_sem)
+    names_in.start()
+
+    def bring(slot):
+        return pltpu.make_async_copy(rows_ref.at[slot], buf.at[slot], load_sem.at[slot])
+
+    order = []
+    for pair in STEPS:
+        for slot in pair[0][3:]:
+            if slot not in order:
+                order.append(slot)
+    for slot in order:
+        bring(slot).start()
+
+    def clear(slot, carry):
+        row_best[slot] = jnp.full(row_best.shape[1:], FILL, jnp.float32)
+        column_best[slot] = jnp.full(column_best.shape[1:], FILL, jnp.float32)
+        return carry
+
+    lax.fori_loop(0, SLOTS, clear, 0)
+    names_in.wait()
+
+    def spread(slot, carry):
         for unit in (0, 1):
             line = jnp.broadcast_to(labels[slot, unit], (128, rows))
             label_rows[slot, pl.ds(unit * rows, rows)] = line.T
+        return carry
+
+    lax.fori_loop(0, SLOTS, spread, 0)
 
     def tile(i, j, own=False):
         sims = lax.dot_general(buf[i].reshape(2 * rows, width), buf[j, core], (((1,), (1,)), ((), ())),
@@ -262,129 +347,66 @@
                 column_best[j, :, lanes], jnp.max(scores.reshape(2 * rows // 8, 8, 128), axis=0))
         row_best[i] = best
 
-    def answer(slot, unit):
-        x, y, z = (SIDE - digit(jnp.int32(packed([o[k] for o in OFFSETS], 2)), slot, 2) for k in range(3))
-        x, y, z = lax.rem(gx + x, SIDE), lax.rem(gy + y, SIDE), lax.rem(gz + z, SIDE)
-        return pltpu.make_async_remote_copy(
-            src_ref=outgoing.at[slot, unit], dst_ref=incoming.at[slot, core],
-            send_sem=result_send.at[slot, unit], recv_sem=result_recv.at[1],
-            device_id=(x, (z * SIDE + y) * 2 + unit), device_id_type=MESH)
-
-    def answer_chip():
-        return pltpu.make_async_remote_copy(
-            src_ref=outgoing.at[0, other], dst_ref=incoming.at[0, core],
-            send_sem=result_send.at[0, 0], recv_sem=result_recv.at[0],
-            device_id=at((0, 0, 0), other), device_id_type=MESH)
-
-    def arrived(slot, h):
-        pltpu.make_async_copy(chunk_of(slot, h, core), chunk_of(slot, h, core), recv_sem.at[slot, h]).wait()
-        share(slot, h, core).start()
-
-    def sent(slot, h):
-        relay(0, slot, h, 0).wait_send()
-
-    def taken(slot):
-        for h in range(chunks):
-            pltpu.make_async_copy(
-                chunk_of(slot, h, other), chunk_of(slot, h, other), take_sem.at[slot, h]).wait()
-
-    def finish(slot):
+    seen, fresh = [0], [[NONE], [NONE]]
+    for pair in STEPS[1:]:
+        for k in (0, 1):
+            slot = pair[0][3 + k]
+            fresh[k].append(NONE if slot in seen else slot)
+            seen.append(slot)
+    bring(0).wait()
+    tile(0, 0, own=True)
+
+    def step(n, carry):
+        for k in (0, 1):
+            slot = lookup(fresh[k], n)
+
+            @pl.when(slot != NONE)
+            def _(slot=slot):
+                bring(slot).wait()
+        tile(lookup(column(0, 3), n), lookup(column(0, 4), n))
+        return carry
+
+    lax.fori_loop(1, len(STEPS), step, 0)
+
+    def finish(slot, carry):
         by_row = jnp.max(row_best[slot].T, axis=0, keepdims=True)
         by_column = jnp.max(column_best[slot], axis=0, keepdims=True)
         for unit in (0, 1):
             mine = by_row[:, unit * rows:(unit + 1) * rows]
-            outgoing[slot, unit] = jnp.where(core == unit, jnp.maximum(mine, by_column), mine)
-
-        @pl.when(slot > 0)
-        def _():
-            answer(slot, 0).start()
-            answer(slot, 1).start()
-
-        @pl.when(slot == 0)
-        def _():
-            incoming[0, core] = outgoing[0, core]
-            answer_chip().start()
-
-    def moves(n):
-        for which in (0, 1):
-            todo = STEPS[n][which][0]
-            if todo:
-                @pl.when(core == which)
-                def _(todo=todo):
-                    for op in todo:
-                        if op[0] == "a":
-                            arrived(*op[1:])
-                        else:
-                            if len(op) > 5:
-                                sent(*op[5:])
-                            relay(*op[1:5]).start()
-
-    def chosen(place, n):
-        return jnp.where(core == 0, lookup(column(0, place), n), lookup(column(1, place), n))
-
-    taken(0)
-    spread(0)
-    tile(0, 0, own=True)
-
-    def step(n, carry):
-        for g in range(0, len(STEPS), 6):
-            @pl.when(lax.div(n, 6) == g // 6)
-            def _(g=g):
-                for k in range(max(g, 1), min(g + 6, len(STEPS))):
-                    @pl.when(n == k)
-                    def _(k=k):
-                        moves(k)
-        opened, ended = chosen(1, n), chosen(2, n)
-
-        @pl.when(opened != NONE)
-        def _():
-            spread(opened)
-            taken(opened)
-
-        @pl.when(ended != NONE)
-        def _():
-            finish(ended)
-
-        tile(chosen(3, n), chosen(4, n))
+            out_ref[slot, unit] = jnp.where(core == unit, jnp.maximum(mine, by_column), mine)
         return carry
 
-    lax.fori_loop(1, len(STEPS), step, 0)
-    left = max(len(t[1]) for t in TAIL)
-
-    def last(n, carry):
-        ends = [(list(t[1]) + [NONE] * left)[:left] for t in TAIL]
-        ended = jnp.where(core == 0, lookup(ends[0], n), lookup(ends[1], n))
-
-        @pl.when(ended != NONE)
-        def _():
-            finish(ended)
-        return carry
-
-    lax.fori_loop(0, left, last, 0)
-
+    lax.fori_loop(0, SLOTS, finish, 0)
+
+
+def reply(found_ref, out_ref, incoming, result_send, result_recv):
+    rows = out_ref.shape[1]
+    core, other, gx, gy, gz, at = place()
+    barrier = pltpu.get_barrier_semaphore()
+    friends = greeted()
+    for offset, flip in friends:
+        pl.semaphore_signal(barrier, inc=1, device_id=at(offset, other if flip else core), device_id_type=MESH)
+    incoming[0, core] = found_ref[0, core]
+    pl.semaphore_wait(barrier, len(friends))
+
+    def answer(slot, unit):
+        return pltpu.make_async_remote_copy(
+            src_ref=found_ref.at[slot, unit], dst_ref=incoming.at[slot, core],
+            send_sem=result_send.at[slot, unit], recv_sem=result_recv.at[1 if slot else 0],
+            device_id=at([-k for k in OFFSETS[slot]], unit), device_id_type=MESH)
+
+    for slot in range(1, SLOTS):
+        answer(slot, 0).start()
+        answer(slot, 1).start()
+    answer(0, other).start()
     pltpu.make_async_copy(incoming.at[0, other], incoming.at[0, other], result_recv.at[0]).wait()
     rest = incoming.at[pl.ds(1, SLOTS - 1)]
     pltpu.make_async_copy(rest, rest, result_recv.at[1]).wait()
     out_ref[...] = jnp.max(incoming[...].reshape(2 * SLOTS, 1, rows), axis=0)
-
-    for which in (0, 1):
-        @pl.when(core == which)
-        def _(which=which):
-            for slot in range(SLOTS):
-                if slot not in column(which, 1):
-                    taken(slot)
-            for move in LAST_SENDS[which]:
-                sent(*move)
-    for slot in range(SLOTS):
-        for h in range(chunks):
-            share(slot, h, core).wait_send()
-        if slot:
-            tell(slot, core, 0).wait_send()
-            answer(slot, 0).wait_send()
-            answer(slot, 1).wait_send()
-        else:
-            answer_chip().wait_send()
-        tell(slot, other, 1).wait_send()
+    for slot in range(1, SLOTS):
+        answer(slot, 0).wait_send()
+        answer(slot, 1).wait_send()
+    answer(0, other).wait_send()
 
 
 def body(embeddings, cluster_ids):
@@ -392,29 +414,56 @@
     chunks = 1 + max(h for sends in LAST_SENDS for _, h in sends)
     copies = pltpu.SemaphoreType.DMA((SLOTS, chunks))
     pairs = pltpu.SemaphoreType.DMA((SLOTS, 2))
-    best = pl.pallas_call(
-        functools.partial(kernel, chunks),
-        out_shape=jax.ShapeDtypeStruct((1, rows), jnp.float32),
-        in_specs=[pl.BlockSpec(memory_space=pl.ANY), pl.BlockSpec(memory_space=pl.ANY)],
-        out_specs=pl.BlockSpec(memory_space=pltpu.VMEM),
+    anywhere = pl.BlockSpec(memory_space=pl.ANY)
+    near = pl.BlockSpec(memory_space=pltpu.VMEM)
+    units = jax.ShapeDtypeStruct((SLOTS, 2, rows, width), jnp.bfloat16)
+    lines = jax.ShapeDtypeStruct((SLOTS, 2, 1, rows), jnp.float32)
+    held, names = pl.pallas_call(
+        functools.partial(gather, chunks),
+        out_shape=(units, lines),
+        in_specs=[anywhere, anywhere],
+        out_specs=(anywhere, anywhere),
         scratch_shapes=[
             pltpu.VMEM((rows, width), jnp.float32),
             pltpu.VMEM((1, rows), jnp.int32),
-            pltpu.VMEM((SLOTS, 2, rows, width), jnp.bfloat16),
-            pltpu.VMEM((SLOTS, 2, 1, rows), jnp.float32),
-            pltpu.VMEM((SLOTS, 2 * rows, 128), jnp.float32),
-            pltpu.VMEM((SLOTS, 2 * rows, 128), jnp.float32),
-            pltpu.VMEM((SLOTS, 8, rows), jnp.float32),
-            pltpu.VMEM((SLOTS, 2, 1, rows), jnp.float32),
-            pltpu.VMEM((SLOTS, 2, 1, rows), jnp.float32),
+            pltpu.VMEM(units.shape, units.dtype),
+            pltpu.VMEM(lines.shape, lines.dtype),
             pltpu.SemaphoreType.DMA((2,)),
             copies, copies, copies, copies,
             pairs, pltpu.SemaphoreType.DMA((2,)),
-            pairs, pltpu.SemaphoreType.DMA((2,)),
+            copies, copies,
         ],
         compiler_params=pltpu.CompilerParams(
             collective_id=0, has_side_effects=True, vmem_limit_bytes=VMEM_BYTES),
     )(embeddings, cluster_ids.reshape(1, rows))
+    found = pl.pallas_call(
+        compare,
+        out_shape=lines,
+        in_specs=[anywhere, anywhere],
+        out_specs=near,
+        scratch_shapes=[
+            pltpu.VMEM(units.shape, units.dtype),
+            pltpu.VMEM(lines.shape, lines.dtype),
+            pltpu.VMEM((SLOTS, 2 * rows, 128), jnp.float32),
+            pltpu.VMEM((SLOTS, 2 * rows, 128), jnp.float32),
+            pltpu.VMEM((SLOTS, 8, rows), jnp.float32),
+            pltpu.SemaphoreType.DMA((SLOTS,)),
+            pltpu.SemaphoreType.DMA,
+        ],
+        compiler_params=pltpu.CompilerParams(vmem_limit_bytes=VMEM_BYTES),
+    )(held, names)
+    best = pl.pallas_call(
+        reply,
+        out_shape=jax.ShapeDtypeStruct((1, rows), jnp.float32),
+        in_specs=[near],
+        out_specs=near,
+        scratch_shapes=[
+            pltpu.VMEM(lines.shape, lines.dtype),
+            pairs, pltpu.SemaphoreType.DMA((2,)),
+        ],
+        compiler_params=pltpu.CompilerParams(
+            collective_id=1, has_side_effects=True, vmem_limit_bytes=VMEM_BYTES),
+    )(found)
     return best.reshape(rows)
 
 

time: 61.5 us -> 82.4 us (1.34)
  Pallas kernels: 60.1 us -> 80.9 us
    pallas_call x1 -> x3, Pallas kernels: 60.1 us -> 80.9 us  [the longest x1 48.3 us: body(): pl.pallas_call(functools.partial(gather, chunks), out_shape=(units, lines...]
where the time goes in v4:
time: 82.4 us; the launch traced here: 82.2 us
  Pallas kernels  80.9 us (98%)
  local copies, waits for them, and re-layouts  1.22 us (1%)
    pallas_call x1, Pallas kernels, body(): pl.pallas_call(functools.partial(gather, chunks), out_shape=(units, lines...  48.3 us
    pallas_call x1, Pallas kernels, body(): pl.pallas_call(compare, out_shape=lines, in_specs=[anywhere, anywhere], o...  23 us
    pallas_call x1, Pallas kernels, body(): pl.pallas_call(reply, out_shape=jax.ShapeDtypeStruct((1, rows), jnp.float...  9.63 us

profile of v4, /device:TPU:1, one launch (start us, length us, event | category | flops | bytes accessed | tf_op | source)
XLA Modules:
  0.0 82.2 jit_solution(2111045314253136660)
XLA Ops:
  0.0 48.3 %shard_map.28 = (bf16[12,2,256,768]{3,2,1,0:T(8,128)(2,1)}, f32[12,2,1,256]{3,2,1,0:T(1,128)}) custom-call(f32[256,768]{1,0:T(8,128)} %emb_ref.1, s32[1,256]{1,0:T(1,128)} %bitcast.3), custom_call_target="tpu_custom_call" | custom-call | tf_op jit(solution)/shard_map/pallas_call | solution.py:421
  48.3 23.0 %shard_map.29.found_ref = f32[12,2,1,256]{3,2,1,0:T(1,128)} custom-call(bf16[12,2,256,768]{3,2,1,0:T(8,128)(2,1)} %get-tuple-element.7.rows_ref, f32[12,2,1,256]{3,2,1,0:T(1,128)} %get-tuple-element.8.names_ref), custom_call_target="tpu_custom_call" | custom-call | tf_op jit(solution)/shard_map/pallas_call | solution.py:439
  71.3 9.6 %shard_map.30 = f32[1,256]{1,0:T(1,128)} custom-call(f32[12,2,1,256]{3,2,1,0:T(1,128)} %shard_map.29.found_ref), custom_call_target="tpu_custom_call" | custom-call | tf_op jit(solution)/shard_map/pallas_call | solution.py:455
  80.9 1.2 %copy.4 = f32[256]{0:T(256)} copy(f32[256]{0:T(256)} %bitcast.2) | data formatting | bytes 2048

commit v5 on v0

v5 whole, which is shorter than its diff:
```python
import functools

import jax
import jax.numpy as jnp
from jax import lax
from jax.experimental import pallas as pl
from jax.experimental.pallas import tpu as pltpu
from jax.sharding import PartitionSpec as P

FILL = -4.0
MESH = pl.DeviceIdType.MESH
SIDE = 4
VMEM_BYTES = 64 * 1024 * 1024 - 512 * 1024
DIRS = ((1, 0, 0), (3, 0, 0), (0, 1, 0), (0, 3, 0), (0, 0, 1), (0, 0, 3))

OFFSETS = (
    (0, 0, 0),
    (0, 3, 0),
    (0, 1, 0),
    (1, 1, 0),
    (0, 0, 1),
    (0, 1, 1),
    (0, 2, 1),
    (3, 3, 3),
    (0, 0, 3),
    (2, 0, 3),
    (3, 0, 3),
    (1, 1, 3),
)

SHARED = ((1, 7, 8, 9, 11), (1, 7, 8, 9, 11))

FIRST_SENDS = (
    ((0, 1, 0, 3), (0, 4, 0, 4), (0, 8, 0, 5)),
    ((0, 2, 0, 2),),
)

LAST_SENDS = (
    ((3, 0), (4, 1), (6, 1), (7, 1), (9, 1), (11, 0)),
    ((3, 1), (4, 1), (6, 1), (7, 1), (9, 1), (11, 1)),
)

STEPS = (
    (((('s', 0, 2, 1, 2), ('a', 1, 0), ('a', 4, 0), ('a', 8, 0), ('s', 8, 10, 0, 1), ('s', 0, 1, 1, 3, 1, 0), ('s', 0, 8, 1, 5, 8, 0), ('a', 2, 1), ('s', 2, 3, 1, 0), ('a', 10, 0), ('s', 0, 2, 0, 2, 2, 1), ('s', 10, 7, 0, 3, 1, 1), ('s', 2, 5, 1, 4, 4, 0), ('a', 1, 1), ('a', 8, 1)), 1, 8, None, 1, 8, 0),
     ((('s', 0, 1, 0, 3), ('s', 0, 4, 0, 4), ('s', 0, 8, 0, 5), ('a', 2, 0), ('s', 2, 3, 0, 0), ('s', 0, 2, 1, 2, 2, 0), ('s', 2, 5, 0, 4, 4, 0), ('a', 1, 0), ('a', 4, 0), ('a', 8, 0), ('s', 8, 10, 0, 1), ('a', 3, 0), ('s', 0, 8, 1, 5, 8, 0), ('a', 2, 1), ('a', 5, 0), ('s', 2, 3, 1, 0, 3, 0), ('a', 10, 0), ('t', 0)), 2, None, None, 0, 2, 12)),
    (((('s', 8, 10, 1, 1, 10, 0), ('a', 3, 1), ('s', 4, 5, 0, 2, 2, 0), ('a', 2, 0), ('a', 5, 1), ('a', 7, 0)), 2, None, None, 8, 2, 1),
     ((('s', 10, 7, 0, 3, 1, 0), ('s', 2, 5, 1, 4, 5, 0), ('s', 3, 11, 0, 5, 8, 1), ('t', 2)), None, None, None, 0, 2, 14)),
    (((('s', 2, 3, 0, 0, 3, 1), ('t', 2)), None, None, None, 0, 2, 14),
     ((('a', 8, 1),), 8, None, None, 2, 8, 0)),
    (((('a', 10, 1), ('s', 10, 7, 1, 3, 7, 0), ('s', 0, 4, 1, 4, 5, 1), ('s', 3, 11, 1, 5, 8, 1)), None, None, None, 0, 1, 10),
     ((('s', 8, 10, 1, 1, 10, 0), ('a', 3, 1)), None, None, None, 0, 8, 3)),
    (((), 10, None, None, 8, 10, 2),
     ((('s', 5, 6, 0, 2, 2, 1),), 3, None, None, 8, 3, 2)),
    (((('a', 5, 0), ('s', 10, 9, 0, 1, 10, 1)), None, None, None, 1, 10, 5),
     ((), None, None, None, 8, 3, 12)),
    (((), 5, None, None, 10, 5, 8),
     ((('a', 5, 1), ('a', 7, 0), ('a', 11, 0)), None, None, None, 8, 3, 14)),
    (((('a', 3, 0), ('s', 5, 6, 0, 2, 5, 0), ('s', 3, 11, 0, 5, 11, 1)), None, None, None, 10, 5, 14),
     ((), None, None, None, 3, 8, 5)),
    (((), None, None, None, 0, 1, 3),
     ((('a', 10, 1),), None, None, None, 0, 3, 10)),
    (((('a', 4, 1), ('a', 7, 1), ('a', 11, 1)), None, None, None, 5, 10, 3),
     ((('s', 0, 1, 1, 3, 7, 0), ('s', 0, 4, 1, 4, 5, 1)), 5, 10, None, 5, 10, 12)),
    (((), None, None, None, 2, 5, 7),
     ((('a', 6, 0), ('s', 10, 9, 0, 1, 10, 1)), None, None, None, 5, 10, 14)),
    (((('a', 9, 0),), 3, 4, None, 3, 4, 14),
     ((('t', 1),), None, None, None, 2, 3, 13)),
    (((('s', 5, 6, 1, 2, 6, 0),), 7, None, None, 4, 7, 3),
     ((('s', 10, 7, 1, 3, 1, 1), ('s', 3, 11, 1, 5, 11, 0), ('a', 1, 1), ('a', 4, 1)), 1, None, None, 1, 0, 14)),
    (((('a', 6, 0), ('a', 11, 0), ('s', 10, 9, 1, 1, 9, 0)), None, None, None, 8, 10, 4),
     ((), None, None, 14, 2, 3, 1)),
    (((), None, None, None, 1, 7, 11),
     ((('a', 9, 0),), None, None, None, 2, 3, 4)),
    (((), 11, None, None, 7, 11, 14),
     ((('s', 5, 6, 1, 2, 6, 0),), None, None, None, 5, 1, 13)),
    (((), None, None, None, 10, 0, 11),
     ((('a', 7, 1), ('a', 11, 1), ('s', 10, 9, 1, 1, 9, 0)), None, None, None, 8, 10, 4)),
    (((('a', 6, 1), ('t', 0)), None, None, None, 0, 3, 12),
     ((), None, None, None, 10, 1, 5)),
    (((), None, None, None, 0, 3, 12),
     ((('t', 4),), None, None, None, 0, 2, 16)),
    (((('a', 9, 1),), None, None, None, 5, 10, 12),
     ((), 4, None, None, 4, 5, 16)),
    (((), None, None, None, 3, 7, 6),
     ((('a', 6, 1),), None, None, None, 10, 0, 16)),
    (((), None, None, None, 0, 1, 9),
     ((), None, None, 16, 2, 3, 7)),
    (((('t', 4),), None, None, None, 0, 2, 16),
     ((('a', 9, 1),), 11, None, None, 4, 11, 13)),
    (((('t', 1),), None, None, None, 1, 2, 13),
     ((), None, None, 13, 5, 11, 7)),
    (((), None, None, 1, 3, 5, 13),
     ((), None, None, None, 10, 0, 11)),
    (((), None, None, None, 4, 5, 9),
     ((), None, None, None, 10, 11, 1)),
    (((), 6, None, 4, 5, 6, 16),
     ((('t', 3),), None, None, 10, 0, 2, 15)),
    (((), 9, None, None, 6, 9, 13),
     ((), None, None, 2, 3, 4, 15)),
    (((), None, None, 13, 6, 9, 14),
     ((), 7, None, None, 3, 7, 6)),
    (((), None, None, 14, 7, 8, 9),
     ((), 6, None, 3, 5, 6, 15)),
    (((), None, None, 7, 8, 9, 6),
     ((), None, None, 15, 0, 1, 9)),
    (((), None, None, 8, 9, 10, 16),
     ((), None, None, 0, 4, 5, 9)),
    (((), None, None, 6, 11, 9, 12),
     ((), None, None, 1, 7, 8, 9)),
    (((('t', 3),), None, None, 10, 0, 2, 15),
     ((), 9, None, 4, 8, 9, 6)),
    (((), None, None, 16, 3, 5, 15),
     ((), None, None, 5, 11, 9, 12)),
)

TAIL = (
    (11, 9, 12, 0, 2, 3, 5, 15),
    (7, 8, 6, 11, 9, 12),
)


SLOTS = len(OFFSETS)
EXTRA = len(SHARED[0])
HELD = SLOTS + EXTRA
NONE = 31


def lookup(values, n, bits=5):
    each = 30 // bits
    words = [sum(v << (bits * k) for k, v in enumerate(values[s:s + each])) for s in range(0, len(values), each)]
    word = jnp.int32(words[0])
    for k, w in enumerate(words[1:], 1):
        word = jnp.where(n >= each * k, jnp.int32(w), word)
    return lax.rem(lax.shift_right_logical(word, bits * lax.rem(n, each)), 1 << bits)


def column(which, place):
    return [NONE if pair[which][place] is None else pair[which][place] for pair in STEPS]


def kernel(chunks, emb_ref, lab_ref, out_ref, emb, ids, buf, labels, label_rows, row_best, column_best, outgoing,
           incoming, load_sem, send_sem, recv_sem, give_sem, take_sem, label_send, label_recv, label_give,
           label_take, result_send, result_recv):
    rows, width = emb.shape
    part = rows // chunks
    load = pltpu.make_async_copy(emb_ref, emb, load_sem.at[0])
    load.start()
    load_ids = pltpu.make_async_copy(lab_ref, ids, load_sem.at[1])
    load_ids.start()
    gx = lax.axis_index("grp")
    mem = lax.axis_index("mem")
    core = lax.rem(mem, 2)
    other = 1 - core
    gy = lax.rem(mem // 2, SIDE)
    gz = mem // (2 * SIDE)

    def at(offset, on):
        x, y, z = (lax.rem(g + k, SIDE) for g, k in zip((gx, gy, gz), offset))
        return (x, (z * SIDE + y) * 2 + on)

    barrier = pltpu.get_barrier_semaphore()
    for direction in DIRS:
        pl.semaphore_signal(barrier, inc=1, device_id=at(direction, core), device_id_type=MESH)
    pl.semaphore_signal(barrier, inc=1, device_id=at((0, 0, 0), other), device_id_type=MESH)

    def chunk_of(slot, h):
        return buf.at[slot, pl.ds(h * part, part)]

    def relay(source, target, h, direction):
        return pltpu.make_async_remote_copy(
            src_ref=chunk_of(source, h), dst_ref=chunk_of(target, h),
            send_sem=send_sem.at[target, h], recv_sem=recv_sem.at[target, h],
            device_id=at(DIRS[direction], core), device_id_type=MESH)

    def relay_label(source, target, direction):
        return pltpu.make_async_remote_copy(
            src_ref=labels.at[source], dst_ref=labels.at[target],
            send_sem=label_send.at[target], recv_sem=label_recv.at[target],
            device_id=at(DIRS[direction], core), device_id_type=MESH)

    def send(source, target, h, direction):
        if h == 0:
            relay_label(source, target, direction).start()
        relay(source, target, h, direction).start()

    def share(slot, k, h):
        return pltpu.make_async_remote_copy(
            src_ref=chunk_of(slot, h), dst_ref=chunk_of(SLOTS + k, h),
            send_sem=give_sem.at[k, h], recv_sem=take_sem.at[k, h],
            device_id=at((0, 0, 0), other), device_id_type=MESH)

    def share_label(slot, k):
        return pltpu.make_async_remote_copy(
            src_ref=labels.at[slot], dst_ref=labels.at[SLOTS + k],
            send_sem=label_give.at[k], recv_sem=label_take.at[k],
            device_id=at((0, 0, 0), other), device_id_type=MESH)

    def give(which, slot, h):
        if slot in SHARED[1 - which]:
            k = SHARED[1 - which].index(slot)
            if h == 0:
                share_label(slot, k).start()
            share(slot, k, h).start()

    load_ids.wait()
    labels[0] = ids[...].astype(jnp.float32)
    load.wait()
    for h in range(chunks):
        e = emb[pl.ds(h * part, part)]
        squares = jnp.sum(e * e, axis=1, keepdims=True)
        buf[0, pl.ds(h * part, part)] = (e * lax.rsqrt(squares + 1e-06)).astype(jnp.bfloat16)
    pl.semaphore_wait(barrier, len(DIRS) + 1)

    for which in (0, 1):
        @pl.when(core == which)
        def _(which=which):
            for move in FIRST_SENDS[which]:
                send(*move)
            for h in range(chunks):
                give(which, 0, h)

    def clear(slot, carry):
        column_best[slot] = jnp.full(column_best.shape[1:], FILL, jnp.float32)

        @pl.when(slot < SLOTS)
        def _():
            row_best[slot] = jnp.full(row_best.shape[1:], FILL, jnp.float32)
        return carry

    lax.fori_loop(0, HELD, clear, 0)

    def spread(slot):
        label_rows[slot] = jnp.broadcast_to(labels[slot], (128, rows)).T

    def tile(left, right, own=False):
        sims = lax.dot_general(jnp.concatenate([buf[a] for a in left], axis=0), buf[right], (((1,), (1,)), ((), ())),
                               preferred_element_type=jnp.float32)
        names = labels[right]
        tops = [row_best[a] for a in left]
        for k in range(rows // 128):
            lanes = slice(k * 128, (k + 1) * 128)
            high = column_best[right, :, lanes]
            for n, a in enumerate(left):
                keep = label_rows[a] == names[:, lanes]
                if own:
                    keep = keep & (lax.broadcasted_iota(jnp.int32, (rows, 128), 0)
                                   != lax.broadcasted_iota(jnp.int32, (rows, 128), 1) + k * 128)
                scores = jnp.where(keep, sims[n * rows:(n + 1) * rows, lanes], FILL)
                tops[n] = jnp.maximum(tops[n], scores)
                high = jnp.maximum(high, jnp.max(scores.reshape(rows // 8, 8, 128), axis=0))
            column_best[right, :, lanes] = high
        for n, a in enumerate(left):
            row_best[a] = tops[n]

    def answer(slot):
        offsets = [[OFFSETS[s] for s in tuple(range(SLOTS)) + SHARED[w]] for w in (0, 1)]
        back = [SIDE - jnp.where(core == 0, *(lookup([o[k] for o in offsets[w]], slot, 2) for w in (0, 1)))
                for k in range(3)]
        return pltpu.make_async_remote_copy(
            src_ref=outgoing.at[slot], dst_ref=incoming.at[slot],
            send_sem=result_send.at[slot], recv_sem=result_recv,
            device_id=at(back, jnp.where(slot < SLOTS, core, other)), device_id_type=MESH)

    def finish(slot):
        by_column = jnp.max(column_best[slot], axis=0, keepdims=True)

        @pl.when(slot < SLOTS)
        def _():
            outgoing[slot] = jnp.maximum(by_column, jnp.max(row_best[slot].T, axis=0, keepdims=True))

        @pl.when(slot >= SLOTS)
        def _():
            outgoing[slot] = by_column

        @pl.when(slot > 0)
        def _():
            answer(slot).start()

        @pl.when(slot == 0)
        def _():
            incoming[0] = outgoing[0]

    def arrived(which, slot, h):
        pltpu.make_async_copy(chunk_of(slot, h), chunk_of(slot, h), recv_sem.at[slot, h]).wait()
        if h == 0:
            pltpu.make_async_copy(labels.at[slot], labels.at[slot], label_recv.at[slot]).wait()
        give(which, slot, h)

    def taken(k):
        for h in range(chunks):
            pltpu.make_async_copy(chunk_of(SLOTS + k, h), chunk_of(SLOTS + k, h), take_sem.at[k, h]).wait()
        pltpu.make_async_copy(labels.at[SLOTS + k], labels.at[SLOTS + k], label_take.at[k]).wait()

    def sent(slot, h):
        relay(0, slot, h, 0).wait_send()

    def moves(n):
        for which in (0, 1):
            todo = STEPS[n][which][0]
            if todo:
                @pl.when(core == which)
                def _(which=which, todo=todo):
                    for op in todo:
                        if op[0] == "a":
                            arrived(which, *op[1:])
                        elif op[0] == "t":
                            taken(op[1])
                        else:
                            if len(op) > 5:
                                sent(*op[5:])
                            send(*op[1:5])

    def chosen(place, n):
        return jnp.where(core == 0, lookup(column(0, place), n), lookup(column(1, place), n))

    spread(0)
    tile((0,), 0, own=True)

    def step(n, carry):
        for g in range(0, len(STEPS), 6):
            @pl.when(lax.div(n, 6) == g // 6)
            def _(g=g):
                for k in range(g, min(g + 6, len(STEPS))):
                    @pl.when(n == k)
                    def _(k=k):
                        moves(k)
        for place in (1, 2):
            opened = chosen(place, n)

            @pl.when(opened != NONE)
            def _(opened=opened):
                spread(opened)
        ended = chosen(3, n)

        @pl.when(ended != NONE)
        def _():
            finish(ended)

        tile((chosen(4, n), chosen(5, n)), chosen(6, n))
        return carry

    lax.fori_loop(0, len(STEPS), step, 0)
    left = max(len(t) for t in TAIL)

    def last(n, carry):
        ends = [(list(t) + [NONE] * left)[:left] for t in TAIL]
        ended = jnp.where(core == 0, lookup(ends[0], n), lookup(ends[1], n))

        @pl.when(ended != NONE)
        def _():
            finish(ended)
        return carry

    lax.fori_loop(0, left, last, 0)

    rest = incoming.at[pl.ds(1, HELD - 1)]
    pltpu.make_async_copy(rest, rest, result_recv).wait()
    out_ref[...] = jnp.max(incoming[...], axis=0)

    for which in (0, 1):
        @pl.when(core == which)
        def _(which=which):
            for move in LAST_SENDS[which]:
                sent(*move)
    for k in range(EXTRA):
        for h in range(chunks):
            share(0, k, h).wait_send()
        share_label(0, k).wait_send()
    for slot in range(1, SLOTS):
        relay_label(0, slot, 0).wait_send()
    for slot in range(1, HELD):
        answer(slot).wait_send()


def body(embeddings, cluster_ids):
    rows, width = embeddings.shape
    chunks = 1 + max(h for sends in LAST_SENDS for _, h in sends)
    dma = pltpu.SemaphoreType.DMA
    best = pl.pallas_call(
        functools.partial(kernel, chunks),
        out_shape=jax.ShapeDtypeStruct((1, rows), jnp.float32),
        in_specs=[pl.BlockSpec(memory_space=pl.ANY), pl.BlockSpec(memory_space=pl.ANY)],
        out_specs=pl.BlockSpec(memory_space=pltpu.VMEM),
        scratch_shapes=[
            pltpu.VMEM((rows, width), jnp.float32),
            pltpu.VMEM((1, rows), jnp.int32),
            pltpu.VMEM((HELD, rows, width), jnp.bfloat16),
            pltpu.VMEM((HELD, 1, rows), jnp.float32),
            pltpu.VMEM((SLOTS, rows, 128), jnp.float32),
            pltpu.VMEM((SLOTS, rows, 128), jnp.float32),
            pltpu.VMEM((HELD, 8, rows), jnp.float32),
            pltpu.VMEM((HELD, 1, rows), jnp.float32),
            pltpu.VMEM((HELD, 1, rows), jnp.float32),
            dma((2,)), dma((SLOTS, chunks)), dma((SLOTS, chunks)), dma((EXTRA, chunks)), dma((EXTRA, chunks)),
            dma((SLOTS,)), dma((SLOTS,)), dma((EXTRA,)), dma((EXTRA,)), dma((HELD,)), dma,
        ],
        compiler_params=pltpu.CompilerParams(
            collective_id=0, has_side_effects=True, vmem_limit_bytes=VMEM_BYTES),
    )(embeddings, cluster_ids.reshape(1, rows))
    return best.reshape(rows)


def solution(mesh):
    return jax.shard_map(
        body,
        mesh=mesh,
        in_specs=(P(("grp", "mem"), None), P(("grp", "mem"), None)),
        out_specs=P(("grp", "mem")),
        check_vma=False,
    )
```

time: 190 us -> 63.5 us (0.33)
  Pallas kernels: 0 us -> 62.1 us
  blocking collectives: 52.4 us -> 0 us
  waiting for transfers between devices: 50.7 us -> 0 us
  matrix products: 31.8 us -> 0 us
  local copies, waits for them, and re-layouts: 30.6 us -> 1.22 us
  between operations: 13.5 us -> 0.02 us
  other arithmetic: 6.5 us -> 0 us
  starting transfers between devices: 3.2 us -> 0 us
    pallas_call x0 -> x1, Pallas kernels: none -> 62.1 us  [body(): pl.pallas_call(functools.partial(kernel, chunks), out_shape=jax.ShapeDtyp...]
    all_gather x1 -> x0, waiting for transfers between devices: 46.5 us -> none  [body(): piece = lax.all_gather(mine, 'mem', axis=1, tiled=True)]
    dot_general x8 -> x0, matrix products: 31.8 us -> none  [masked_scores(): jnp.einsum('csd,ctd->cst', mine, piece, preferred_element_type=jnp.float32)]
    all_gather x1 -> x0, blocking collectives: 28.4 us -> none  [body(): piece_valid = lax.all_gather(mine_valid, 'mem', axis=1, tiled=True)]
    scatter x3 -> x0, local copies, waits for them, and re-layouts: 27.6 us -> none  [the longest x1 15.3 us: body(): jnp.zeros((owned, groups, capacity, width), jnp.bfloat16)]
    all_to_all x2 -> x0, blocking collectives: 24 us -> none  [the longest x1 16.1 us: body(): lax.all_to_all(outgoing, 'grp', split_axis=1, concat_axis=1, tiled=True)]
    all_to_all x1 -> x0, waiting for transfers between devices: 4.16 us -> none  [body(): lax.all_to_all(flags, 'grp', split_axis=1, concat_axis=1, tiled=True)]
    all_to_all x1 -> x0, starting transfers between devices: 3.2 us -> none  [body(): lax.all_to_all(flags, 'grp', split_axis=1, concat_axis=1, tiled=True)]
  transfers between devices with their start and end apart: 2 -> 0, of which waited for: 2 -> 0; matrix products, arithmetic and copies ran while one was open for 7% -> 0% of each run, Pallas kernels for 0% -> 0%
where the time goes in v5:
time: 63.5 us; the launch traced here: 63.3 us
  Pallas kernels  62.1 us (98%)
  local copies, waits for them, and re-layouts  1.22 us (2%)
    pallas_call x1, Pallas kernels, body(): pl.pallas_call(functools.partial(kernel, chunks), out_shape=jax.ShapeDtyp...  62.1 us

profile of v5, /device:TPU:1, one launch (start us, length us, event | category | flops | bytes accessed | tf_op | source)
XLA Modules:
  0.0 63.3 jit_solution(16939651336623844280)
XLA Ops:
  0.0 62.1 %shard_map.28 = f32[1,256]{1,0:T(1,128)} custom-call(f32[256,768]{1,0:T(8,128)} %emb_ref.1, s32[1,256]{1,0:T(1,128)} %bitcast.3), custom_call_target="tpu_custom_call" | custom-call | tf_op jit(solution)/shard_map/pallas_call | solution.py:379
  62.1 0.0 copy-start
  62.1 0.7 %copy-done = f32[1,256]{1,0:T(1,128)S(1)} copy-done((f32[1,256]{1,0:T(1,128)S(1)}, f32[1,256]{1,0:T(1,128)}, u32[]{:S(2)}) %copy-start) | copy-done | bytes 1048
  62.8 0.6 copy.4
Async XLA Ops:
  62.1 0.7 %copy-start = (f32[1,256]{1,0:T(1,128)S(1)}, f32[1,256]{1,0:T(1,128)}, u32[]{:S(2)}) copy-start(f32[1,256]{1,0:T(1,128)} %shard_map.28) | copy-start | bytes 3076

commit v6 on v5

--- a/solution.py
+++ b/solution.py
@@ -14,112 +14,106 @@
 DIRS = ((1, 0, 0), (3, 0, 0), (0, 1, 0), (0, 3, 0), (0, 0, 1), (0, 0, 3))
 
 OFFSETS = (
-    (0, 0, 0),
-    (0, 3, 0),
-    (0, 1, 0),
-    (1, 1, 0),
-    (0, 0, 1),
-    (0, 1, 1),
-    (0, 2, 1),
-    (3, 3, 3),
-    (0, 0, 3),
-    (2, 0, 3),
-    (3, 0, 3),
-    (1, 1, 3),
+    ((0, 0, 0), (1, 0, 0), (2, 0, 0), (0, 1, 0), (0, 2, 0), (0, 3, 0),
+     (3, 0, 1), (0, 0, 1), (2, 0, 2), (3, 0, 2), (0, 1, 3), (0, 2, 3)),
+    ((0, 0, 0), (1, 0, 3), (2, 0, 3), (0, 0, 3), (0, 1, 3), (0, 2, 3),
+     (0, 3, 3), (3, 0, 0), (2, 0, 1), (3, 0, 1), (0, 1, 2), (0, 2, 2)),
 )
 
-SHARED = ((1, 7, 8, 9, 11), (1, 7, 8, 9, 11))
+SHARED = ((0, 1, 6, 7, 10, 11), (1, 2, 4, 5, 6, 10))
 
 FIRST_SENDS = (
-    ((0, 1, 0, 3), (0, 4, 0, 4), (0, 8, 0, 5)),
-    ((0, 2, 0, 2),),
+    ((0, 1, 0, 0), (0, 3, 0, 2), (0, 5, 1, 3), (0, 7, 0, 4)),
+    ((0, 7, 0, 1), (0, 3, 0, 5)),
 )
 
 LAST_SENDS = (
-    ((3, 0), (4, 1), (6, 1), (7, 1), (9, 1), (11, 0)),
-    ((3, 1), (4, 1), (6, 1), (7, 1), (9, 1), (11, 1)),
+    ((2, 1), (4, 0), (4, 1), (8, 1), (9, 1), (11, 1)),
+    ((2, 1), (5, 1), (8, 1), (9, 1), (10, 1), (11, 1)),
 )
 
 STEPS = (
-    (((('s', 0, 2, 1, 2), ('a', 1, 0), ('a', 4, 0), ('a', 8, 0), ('s', 8, 10, 0, 1), ('s', 0, 1, 1, 3, 1, 0), ('s', 0, 8, 1, 5, 8, 0), ('a', 2, 1), ('s', 2, 3, 1, 0), ('a', 10, 0), ('s', 0, 2, 0, 2, 2, 1), ('s', 10, 7, 0, 3, 1, 1), ('s', 2, 5, 1, 4, 4, 0), ('a', 1, 1), ('a', 8, 1)), 1, 8, None, 1, 8, 0),
-     ((('s', 0, 1, 0, 3), ('s', 0, 4, 0, 4), ('s', 0, 8, 0, 5), ('a', 2, 0), ('s', 2, 3, 0, 0), ('s', 0, 2, 1, 2, 2, 0), ('s', 2, 5, 0, 4, 4, 0), ('a', 1, 0), ('a', 4, 0), ('a', 8, 0), ('s', 8, 10, 0, 1), ('a', 3, 0), ('s', 0, 8, 1, 5, 8, 0), ('a', 2, 1), ('a', 5, 0), ('s', 2, 3, 1, 0, 3, 0), ('a', 10, 0), ('t', 0)), 2, None, None, 0, 2, 12)),
-    (((('s', 8, 10, 1, 1, 10, 0), ('a', 3, 1), ('s', 4, 5, 0, 2, 2, 0), ('a', 2, 0), ('a', 5, 1), ('a', 7, 0)), 2, None, None, 8, 2, 1),
-     ((('s', 10, 7, 0, 3, 1, 0), ('s', 2, 5, 1, 4, 5, 0), ('s', 3, 11, 0, 5, 8, 1), ('t', 2)), None, None, None, 0, 2, 14)),
-    (((('s', 2, 3, 0, 0, 3, 1), ('t', 2)), None, None, None, 0, 2, 14),
-     ((('a', 8, 1),), 8, None, None, 2, 8, 0)),
-    (((('a', 10, 1), ('s', 10, 7, 1, 3, 7, 0), ('s', 0, 4, 1, 4, 5, 1), ('s', 3, 11, 1, 5, 8, 1)), None, None, None, 0, 1, 10),
-     ((('s', 8, 10, 1, 1, 10, 0), ('a', 3, 1)), None, None, None, 0, 8, 3)),
-    (((), 10, None, None, 8, 10, 2),
-     ((('s', 5, 6, 0, 2, 2, 1),), 3, None, None, 8, 3, 2)),
-    (((('a', 5, 0), ('s', 10, 9, 0, 1, 10, 1)), None, None, None, 1, 10, 5),
-     ((), None, None, None, 8, 3, 12)),
-    (((), 5, None, None, 10, 5, 8),
-     ((('a', 5, 1), ('a', 7, 0), ('a', 11, 0)), None, None, None, 8, 3, 14)),
-    (((('a', 3, 0), ('s', 5, 6, 0, 2, 5, 0), ('s', 3, 11, 0, 5, 11, 1)), None, None, None, 10, 5, 14),
-     ((), None, None, None, 3, 8, 5)),
-    (((), None, None, None, 0, 1, 3),
-     ((('a', 10, 1),), None, None, None, 0, 3, 10)),
-    (((('a', 4, 1), ('a', 7, 1), ('a', 11, 1)), None, None, None, 5, 10, 3),
-     ((('s', 0, 1, 1, 3, 7, 0), ('s', 0, 4, 1, 4, 5, 1)), 5, 10, None, 5, 10, 12)),
-    (((), None, None, None, 2, 5, 7),
-     ((('a', 6, 0), ('s', 10, 9, 0, 1, 10, 1)), None, None, None, 5, 10, 14)),
-    (((('a', 9, 0),), 3, 4, None, 3, 4, 14),
-     ((('t', 1),), None, None, None, 2, 3, 13)),
-    (((('s', 5, 6, 1, 2, 6, 0),), 7, None, None, 4, 7, 3),
-     ((('s', 10, 7, 1, 3, 1, 1), ('s', 3, 11, 1, 5, 11, 0), ('a', 1, 1), ('a', 4, 1)), 1, None, None, 1, 0, 14)),
-    (((('a', 6, 0), ('a', 11, 0), ('s', 10, 9, 1, 1, 9, 0)), None, None, None, 8, 10, 4),
-     ((), None, None, 14, 2, 3, 1)),
-    (((), None, None, None, 1, 7, 11),
-     ((('a', 9, 0),), None, None, None, 2, 3, 4)),
-    (((), 11, None, None, 7, 11, 14),
-     ((('s', 5, 6, 1, 2, 6, 0),), None, None, None, 5, 1, 13)),
-    (((), None, None, None, 10, 0, 11),
-     ((('a', 7, 1), ('a', 11, 1), ('s', 10, 9, 1, 1, 9, 0)), None, None, None, 8, 10, 4)),
-    (((('a', 6, 1), ('t', 0)), None, None, None, 0, 3, 12),
-     ((), None, None, None, 10, 1, 5)),
-    (((), None, None, None, 0, 3, 12),
-     ((('t', 4),), None, None, None, 0, 2, 16)),
-    (((('a', 9, 1),), None, None, None, 5, 10, 12),
-     ((), 4, None, None, 4, 5, 16)),
-    (((), None, None, None, 3, 7, 6),
-     ((('a', 6, 1),), None, None, None, 10, 0, 16)),
-    (((), None, None, None, 0, 1, 9),
-     ((), None, None, 16, 2, 3, 7)),
-    (((('t', 4),), None, None, None, 0, 2, 16),
-     ((('a', 9, 1),), 11, None, None, 4, 11, 13)),
-    (((('t', 1),), None, None, None, 1, 2, 13),
-     ((), None, None, 13, 5, 11, 7)),
-    (((), None, None, 1, 3, 5, 13),
-     ((), None, None, None, 10, 0, 11)),
-    (((), None, None, None, 4, 5, 9),
-     ((), None, None, None, 10, 11, 1)),
-    (((), 6, None, 4, 5, 6, 16),
-     ((('t', 3),), None, None, 10, 0, 2, 15)),
-    (((), 9, None, None, 6, 9, 13),
-     ((), None, None, 2, 3, 4, 15)),
-    (((), None, None, 13, 6, 9, 14),
-     ((), 7, None, None, 3, 7, 6)),
-    (((), None, None, 14, 7, 8, 9),
-     ((), 6, None, 3, 5, 6, 15)),
-    (((), None, None, 7, 8, 9, 6),
-     ((), None, None, 15, 0, 1, 9)),
-    (((), None, None, 8, 9, 10, 16),
-     ((), None, None, 0, 4, 5, 9)),
-    (((), None, None, 6, 11, 9, 12),
-     ((), None, None, 1, 7, 8, 9)),
-    (((('t', 3),), None, None, 10, 0, 2, 15),
-     ((), 9, None, 4, 8, 9, 6)),
-    (((), None, None, 16, 3, 5, 15),
-     ((), None, None, 5, 11, 9, 12)),
+    (((('s', 0, 1, 1, 0, 1, 0), ('s', 0, 3, 1, 2, 3, 0), ('s', 0, 5, 0, 3, 5, 1), ('s', 0, 7, 1, 4, 7, 0), ('a', 1, 0), ('a', 3, 0), ('a', 5, 1), ('a', 7, 0), ('s', 7, 6, 0, 1), ('s', 3, 10, 0, 5), ('a', 1, 1), ('a', 3, 1), ('a', 5, 0), ('a', 7, 1)), 1, None, None, None, 0, 1, 7),
+     ((('s', 0, 7, 1, 1, 7, 0), ('s', 0, 3, 1, 5, 3, 0), ('a', 3, 0), ('a', 7, 0), ('s', 3, 1, 0, 0), ('s', 3, 4, 0, 2), ('s', 3, 6, 0, 3), ('s', 7, 9, 0, 4), ('a', 3, 1), ('a', 7, 1)), 3, 7, None, None, 3, 7, 0)),
+    (((('t', 0),), None, None, None, None, 0, 1, 12),
+     ((('s', 3, 1, 1, 0, 1, 0), ('s', 3, 4, 1, 2, 4, 0), ('s', 7, 9, 1, 4, 9, 0), ('a', 1, 0), ('a', 4, 0), ('a', 6, 0), ('a', 9, 0), ('s', 9, 8, 0, 1, 7, 1), ('s', 3, 6, 1, 3, 6, 0), ('s', 4, 10, 0, 5, 3, 1), ('a', 1, 1), ('a', 4, 1), ('a', 9, 1)), 1, None, None, None, 0, 1, 4)),
+    (((), 3, None, None, None, 1, 3, 0),
+     ((), None, None, None, None, 1, 3, 9)),
+    (((), 5, None, None, None, 3, 5, 1),
+     ((), 4, None, None, None, 1, 4, 7)),
+    (((), None, None, None, None, 3, 5, 12),
+     ((('t', 3),), None, None, None, None, 3, 1, 15)),
+    (((('s', 7, 6, 1, 1, 6, 0), ('s', 5, 4, 1, 3, 5, 0), ('s', 3, 10, 1, 5, 10, 0)), 7, None, None, None, 5, 7, 3),
+     ((('t', 0),), 9, None, None, None, 4, 9, 12)),
+    (((('t', 3),), None, None, None, None, 1, 3, 15),
+     ((('s', 1, 2, 0, 0, 1, 1), ('s', 9, 8, 1, 1, 8, 0), ('s', 6, 5, 0, 3, 6, 1), ('s', 4, 10, 1, 5, 10, 0)), None, None, None, None, 4, 9, 15)),
+    (((('a', 6, 0), ('a', 10, 0)), None, None, None, None, 5, 7, 15),
+     ((), None, None, None, None, 7, 4, 3)),
+    (((('s', 1, 2, 0, 0, 1, 1), ('s', 3, 4, 0, 2, 3, 1), ('s', 6, 9, 0, 4, 7, 1), ('a', 4, 1), ('a', 6, 1), ('a', 10, 1)), None, None, None, None, 1, 3, 6),
+     ((('a', 6, 1), ('a', 8, 0), ('a', 10, 0), ('s', 10, 11, 0, 2, 4, 1), ('t', 4)), None, None, None, None, 3, 4, 16)),
+    (((), None, None, None, None, 1, 5, 10),
+     ((), None, None, None, None, 0, 1, 6)),
+    (((), 6, None, None, None, 6, 7, 10),
+     ((), None, None, None, None, 7, 9, 6)),
+    (((), None, None, None, None, 7, 6, 5),
+     ((), 6, None, None, None, 9, 6, 4)),
+    (((), None, None, None, None, 7, 6, 12),
+     ((('t', 5),), None, None, None, None, 9, 6, 17)),
+    (((('s', 6, 9, 1, 4, 9, 0),), 10, None, None, None, 10, 0, 12),
+     ((('s', 6, 5, 1, 3, 5, 0), ('t', 2)), None, None, None, None, 4, 9, 14)),
+    (((('t', 1),), None, None, 12, None, 3, 6, 13),
+     ((('a', 2, 0), ('a', 5, 0), ('a', 8, 1), ('a', 10, 1)), None, None, None, None, 0, 1, 10)),
+    (((('a', 2, 0), ('a', 4, 0), ('a', 9, 0)), None, None, None, None, 1, 6, 4),
+     ((('s', 10, 11, 1, 2, 11, 0),), 10, None, None, None, 4, 10, 8)),
+    (((), 4, None, None, None, 10, 4, 13),
+     ((('a', 11, 0),), 8, None, None, None, 6, 8, 12)),
+    (((), None, None, None, None, 10, 4, 15),
+     ((), None, None, None, None, 6, 9, 10)),
+    (((('s', 1, 2, 1, 0, 2, 0), ('s', 9, 8, 0, 1, 6, 1), ('s', 4, 11, 0, 5, 10, 1), ('a', 9, 1)), None, None, None, None, 0, 1, 9),
+     ((), None, None, None, None, 6, 10, 16)),
+    (((), None, None, None, None, 4, 5, 9),
+     ((('s', 1, 2, 1, 0, 2, 0),), None, None, 6, None, 8, 0, 14)),
+    (((('t', 2),), 9, None, 5, None, 7, 9, 14),
+     ((), None, None, 14, None, 8, 10, 15)),
+    (((('t', 4),), None, None, None, None, 0, 7, 16),
+     ((('a', 5, 1),), None, None, 15, None, 1, 7, 5)),
+    (((('s', 9, 8, 1, 1, 8, 0), ('s', 4, 11, 1, 5, 11, 0), ('a', 2, 1), ('a', 8, 0), ('a', 11, 0)), None, None, None, None, 0, 3, 2),
+     ((), None, None, None, None, 8, 9, 5)),
+    (((), None, None, None, None, 4, 6, 2),
+     ((('a', 11, 1),), 5, None, 9, None, 10, 5, 12)),
+    (((), 2, None, 6, None, 9, 2, 10),
+     ((('t', 1),), None, None, None, None, 3, 4, 13)),
+    (((), None, None, None, None, 9, 2, 15),
+     ((), None, None, None, None, 5, 8, 13)),
+    (((), None, None, 15, None, 9, 2, 16),
+     ((), None, None, None, None, 0, 1, 11)),
+    (((('t', 5),), None, None, None, None, 7, 9, 17),
+     ((('a', 2, 1),), 11, None, 1, None, 5, 11, 16)),
+    (((('a', 8, 1), ('a', 11, 1)), None, None, 9, None, 1, 2, 11),
+     ((), None, None, None, None, 11, 0, 12)),
+    (((), None, None, 1, None, 2, 3, 8),
+     ((), None, None, 12, None, 11, 0, 13)),
+    (((), 8, None, 3, None, 2, 8, 14),
+     ((), 2, None, 13, None, 2, 0, 16)),
+    (((), None, None, 2, 14, 4, 10, 8),
+     ((), None, None, 16, None, 3, 4, 2)),
+    (((), None, None, 4, 10, 7, 0, 11),
+     ((), None, None, 3, 4, 5, 7, 2)),
+    (((), None, None, 7, 11, 8, 0, 13),
+     ((), None, None, 5, 7, 8, 2, 17)),
+    (((), None, None, 13, None, 8, 0, 16),
+     ((), None, None, 17, None, 10, 0, 2)),
+    (((), None, None, 16, None, 8, 0, 17),
+     ((), None, None, 10, 0, 11, 2, 8)),
 )
 
 TAIL = (
-    (11, 9, 12, 0, 2, 3, 5, 15),
-    (7, 8, 6, 11, 9, 12),
+    (8, 0, 17),
+    (11, 2, 8),
 )
 
 
-SLOTS = len(OFFSETS)
+SLOTS = len(OFFSETS[0])
 EXTRA = len(SHARED[0])
 HELD = SLOTS + EXTRA
 NONE = 31
@@ -209,13 +203,18 @@
         e = emb[pl.ds(h * part, part)]
         squares = jnp.sum(e * e, axis=1, keepdims=True)
         buf[0, pl.ds(h * part, part)] = (e * lax.rsqrt(squares + 1e-06)).astype(jnp.bfloat16)
-    pl.semaphore_wait(barrier, len(DIRS) + 1)
+        if h == 0:
+            pl.semaphore_wait(barrier, len(DIRS) + 1)
+        for which in (0, 1):
+            @pl.when(core == which)
+            def _(which=which, h=h):
+                for move in FIRST_SENDS[which]:
+                    if move[2] == h:
+                        send(*move)
 
     for which in (0, 1):
         @pl.when(core == which)
         def _(which=which):
-            for move in FIRST_SENDS[which]:
-                send(*move)
             for h in range(chunks):
                 give(which, 0, h)
 
@@ -253,7 +252,7 @@
             row_best[a] = tops[n]
 
     def answer(slot):
-        offsets = [[OFFSETS[s] for s in tuple(range(SLOTS)) + SHARED[w]] for w in (0, 1)]
+        offsets = [OFFSETS[w] + tuple(OFFSETS[1 - w][k] for k in SHARED[w]) for w in (0, 1)]
         back = [SIDE - jnp.where(core == 0, *(lookup([o[k] for o in offsets[w]], slot, 2) for w in (0, 1)))
                 for k in range(3)]
         return pltpu.make_async_remote_copy(
@@ -330,13 +329,14 @@
             @pl.when(opened != NONE)
             def _(opened=opened):
                 spread(opened)
-        ended = chosen(3, n)
-
-        @pl.when(ended != NONE)
-        def _():
-            finish(ended)
-
-        tile((chosen(4, n), chosen(5, n)), chosen(6, n))
+        for place in (3, 4):
+            ended = chosen(place, n)
+
+            @pl.when(ended != NONE)
+            def _(ended=ended):
+                finish(ended)
+
+        tile((chosen(5, n), chosen(6, n)), chosen(7, n))
         return carry
 
     lax.fori_loop(0, len(STEPS), step, 0)

time: 63.5 us -> 55.6 us (0.88)
  Pallas kernels: 62.1 us -> 54.2 us
    pallas_call x1, Pallas kernels: 62.1 us -> 54.2 us  [body(): pl.pallas_call(functools.partial(kernel, chunks), out_shape=jax.ShapeDtyp...]
where the time goes in v6:
time: 55.6 us; the launch traced here: 55.4 us
  Pallas kernels  54.2 us (97%)
  local copies, waits for them, and re-layouts  1.22 us (2%)
    pallas_call x1, Pallas kernels, body(): pl.pallas_call(functools.partial(kernel, chunks), out_shape=jax.ShapeDtyp...  54.2 us
    unnamed x3, local copies, waits for them, and re-layouts  1.22 us

profile of v6, /device:TPU:1, one launch (start us, length us, event | category | flops | bytes accessed | tf_op | source)
XLA Modules:
  0.0 55.4 jit_solution(6303710184429141966)
XLA Ops:
  0.0 54.2 %shard_map.28 = f32[1,256]{1,0:T(1,128)} custom-call(f32[256,768]{1,0:T(8,128)} %emb_ref.1, s32[1,256]{1,0:T(1,128)} %bitcast.3), custom_call_target="tpu_custom_call" | custom-call | tf_op jit(solution)/shard_map/pallas_call | solution.py:379
  54.2 0.0 copy-start
  54.2 0.7 %copy-done = f32[1,256]{1,0:T(1,128)S(1)} copy-done((f32[1,256]{1,0:T(1,128)S(1)}, f32[1,256]{1,0:T(1,128)}, u32[]{:S(2)}) %copy-start) | copy-done | bytes 1048
  54.9 0.6 %copy.4 = f32[256]{0:T(256)} copy(f32[256]{0:T(256)S(1)} %bitcast.2) | data formatting | bytes 2048
Async XLA Ops:
  54.2 0.7 %copy-start = (f32[1,256]{1,0:T(1,128)S(1)}, f32[1,256]{1,0:T(1,128)}, u32[]{:S(2)}) copy-start(f32[1,256]{1,0:T(1,128)} %shard_map.28) | copy-start | bytes 3076

commit v7 on v6

--- a/solution.py
+++ b/solution.py
@@ -14,102 +14,102 @@
 DIRS = ((1, 0, 0), (3, 0, 0), (0, 1, 0), (0, 3, 0), (0, 0, 1), (0, 0, 3))
 
 OFFSETS = (
-    ((0, 0, 0), (1, 0, 0), (2, 0, 0), (0, 1, 0), (0, 2, 0), (0, 3, 0),
-     (3, 0, 1), (0, 0, 1), (2, 0, 2), (3, 0, 2), (0, 1, 3), (0, 2, 3)),
-    ((0, 0, 0), (1, 0, 3), (2, 0, 3), (0, 0, 3), (0, 1, 3), (0, 2, 3),
-     (0, 3, 3), (3, 0, 0), (2, 0, 1), (3, 0, 1), (0, 1, 2), (0, 2, 2)),
+    ((0, 0, 0), (1, 0, 0), (2, 0, 0), (0, 1, 0), (3, 1, 0), (2, 2, 0),
+     (3, 2, 0), (0, 0, 1), (0, 0, 2), (0, 3, 2), (0, 0, 3), (0, 3, 3)),
+    ((0, 0, 0), (0, 3, 0), (1, 3, 0), (2, 3, 0), (3, 0, 0), (2, 1, 0),
+     (3, 1, 0), (0, 3, 1), (0, 3, 2), (0, 2, 2), (0, 3, 3), (0, 2, 3)),
 )
 
-SHARED = ((0, 1, 6, 7, 10, 11), (1, 2, 4, 5, 6, 10))
+SHARED = ((0, 2, 4, 7, 9, 11), (1, 2, 4, 7, 8, 11))
 
 FIRST_SENDS = (
-    ((0, 1, 0, 0), (0, 3, 0, 2), (0, 5, 1, 3), (0, 7, 0, 4)),
-    ((0, 7, 0, 1), (0, 3, 0, 5)),
+    ((0, 1, 0, 0), (0, 3, 0, 2), (0, 7, 0, 4), (0, 10, 1, 5)),
+    ((0, 4, 0, 1), (0, 1, 0, 3)),
 )
 
 LAST_SENDS = (
-    ((2, 1), (4, 0), (4, 1), (8, 1), (9, 1), (11, 1)),
-    ((2, 1), (5, 1), (8, 1), (9, 1), (10, 1), (11, 1)),
+    ((1, 0), (1, 1), (2, 0), (2, 1), (3, 0), (3, 1), (4, 0), (4, 1), (5, 0), (5, 1), (6, 0), (6, 1), (7, 0), (7, 1), (8, 0), (8, 1), (9, 0), (9, 1), (10, 0), (10, 1), (11, 0), (11, 1)),
+    ((1, 0), (1, 1), (2, 0), (2, 1), (3, 0), (3, 1), (4, 0), (4, 1), (5, 0), (5, 1), (6, 0), (6, 1), (7, 0), (7, 1), (8, 0), (8, 1), (9, 0), (9, 1), (10, 0), (10, 1), (11, 0), (11, 1)),
 )
 
 STEPS = (
-    (((('s', 0, 1, 1, 0, 1, 0), ('s', 0, 3, 1, 2, 3, 0), ('s', 0, 5, 0, 3, 5, 1), ('s', 0, 7, 1, 4, 7, 0), ('a', 1, 0), ('a', 3, 0), ('a', 5, 1), ('a', 7, 0), ('s', 7, 6, 0, 1), ('s', 3, 10, 0, 5), ('a', 1, 1), ('a', 3, 1), ('a', 5, 0), ('a', 7, 1)), 1, None, None, None, 0, 1, 7),
-     ((('s', 0, 7, 1, 1, 7, 0), ('s', 0, 3, 1, 5, 3, 0), ('a', 3, 0), ('a', 7, 0), ('s', 3, 1, 0, 0), ('s', 3, 4, 0, 2), ('s', 3, 6, 0, 3), ('s', 7, 9, 0, 4), ('a', 3, 1), ('a', 7, 1)), 3, 7, None, None, 3, 7, 0)),
-    (((('t', 0),), None, None, None, None, 0, 1, 12),
-     ((('s', 3, 1, 1, 0, 1, 0), ('s', 3, 4, 1, 2, 4, 0), ('s', 7, 9, 1, 4, 9, 0), ('a', 1, 0), ('a', 4, 0), ('a', 6, 0), ('a', 9, 0), ('s', 9, 8, 0, 1, 7, 1), ('s', 3, 6, 1, 3, 6, 0), ('s', 4, 10, 0, 5, 3, 1), ('a', 1, 1), ('a', 4, 1), ('a', 9, 1)), 1, None, None, None, 0, 1, 4)),
-    (((), 3, None, None, None, 1, 3, 0),
-     ((), None, None, None, None, 1, 3, 9)),
-    (((), 5, None, None, None, 3, 5, 1),
-     ((), 4, None, None, None, 1, 4, 7)),
-    (((), None, None, None, None, 3, 5, 12),
-     ((('t', 3),), None, None, None, None, 3, 1, 15)),
-    (((('s', 7, 6, 1, 1, 6, 0), ('s', 5, 4, 1, 3, 5, 0), ('s', 3, 10, 1, 5, 10, 0)), 7, None, None, None, 5, 7, 3),
-     ((('t', 0),), 9, None, None, None, 4, 9, 12)),
-    (((('t', 3),), None, None, None, None, 1, 3, 15),
-     ((('s', 1, 2, 0, 0, 1, 1), ('s', 9, 8, 1, 1, 8, 0), ('s', 6, 5, 0, 3, 6, 1), ('s', 4, 10, 1, 5, 10, 0)), None, None, None, None, 4, 9, 15)),
-    (((('a', 6, 0), ('a', 10, 0)), None, None, None, None, 5, 7, 15),
-     ((), None, None, None, None, 7, 4, 3)),
-    (((('s', 1, 2, 0, 0, 1, 1), ('s', 3, 4, 0, 2, 3, 1), ('s', 6, 9, 0, 4, 7, 1), ('a', 4, 1), ('a', 6, 1), ('a', 10, 1)), None, None, None, None, 1, 3, 6),
-     ((('a', 6, 1), ('a', 8, 0), ('a', 10, 0), ('s', 10, 11, 0, 2, 4, 1), ('t', 4)), None, None, None, None, 3, 4, 16)),
-    (((), None, None, None, None, 1, 5, 10),
-     ((), None, None, None, None, 0, 1, 6)),
-    (((), 6, None, None, None, 6, 7, 10),
-     ((), None, None, None, None, 7, 9, 6)),
-    (((), None, None, None, None, 7, 6, 5),
-     ((), 6, None, None, None, 9, 6, 4)),
-    (((), None, None, None, None, 7, 6, 12),
-     ((('t', 5),), None, None, None, None, 9, 6, 17)),
-    (((('s', 6, 9, 1, 4, 9, 0),), 10, None, None, None, 10, 0, 12),
-     ((('s', 6, 5, 1, 3, 5, 0), ('t', 2)), None, None, None, None, 4, 9, 14)),
-    (((('t', 1),), None, None, 12, None, 3, 6, 13),
-     ((('a', 2, 0), ('a', 5, 0), ('a', 8, 1), ('a', 10, 1)), None, None, None, None, 0, 1, 10)),
-    (((('a', 2, 0), ('a', 4, 0), ('a', 9, 0)), None, None, None, None, 1, 6, 4),
-     ((('s', 10, 11, 1, 2, 11, 0),), 10, None, None, None, 4, 10, 8)),
-    (((), 4, None, None, None, 10, 4, 13),
-     ((('a', 11, 0),), 8, None, None, None, 6, 8, 12)),
-    (((), None, None, None, None, 10, 4, 15),
-     ((), None, None, None, None, 6, 9, 10)),
-    (((('s', 1, 2, 1, 0, 2, 0), ('s', 9, 8, 0, 1, 6, 1), ('s', 4, 11, 0, 5, 10, 1), ('a', 9, 1)), None, None, None, None, 0, 1, 9),
-     ((), None, None, None, None, 6, 10, 16)),
-    (((), None, None, None, None, 4, 5, 9),
-     ((('s', 1, 2, 1, 0, 2, 0),), None, None, 6, None, 8, 0, 14)),
-    (((('t', 2),), 9, None, 5, None, 7, 9, 14),
-     ((), None, None, 14, None, 8, 10, 15)),
-    (((('t', 4),), None, None, None, None, 0, 7, 16),
-     ((('a', 5, 1),), None, None, 15, None, 1, 7, 5)),
-    (((('s', 9, 8, 1, 1, 8, 0), ('s', 4, 11, 1, 5, 11, 0), ('a', 2, 1), ('a', 8, 0), ('a', 11, 0)), None, None, None, None, 0, 3, 2),
-     ((), None, None, None, None, 8, 9, 5)),
-    (((), None, None, None, None, 4, 6, 2),
-     ((('a', 11, 1),), 5, None, 9, None, 10, 5, 12)),
-    (((), 2, None, 6, None, 9, 2, 10),
-     ((('t', 1),), None, None, None, None, 3, 4, 13)),
-    (((), None, None, None, None, 9, 2, 15),
-     ((), None, None, None, None, 5, 8, 13)),
-    (((), None, None, 15, None, 9, 2, 16),
-     ((), None, None, None, None, 0, 1, 11)),
-    (((('t', 5),), None, None, None, None, 7, 9, 17),
-     ((('a', 2, 1),), 11, None, 1, None, 5, 11, 16)),
-    (((('a', 8, 1), ('a', 11, 1)), None, None, 9, None, 1, 2, 11),
-     ((), None, None, None, None, 11, 0, 12)),
-    (((), None, None, 1, None, 2, 3, 8),
-     ((), None, None, 12, None, 11, 0, 13)),
-    (((), 8, None, 3, None, 2, 8, 14),
-     ((), 2, None, 13, None, 2, 0, 16)),
-    (((), None, None, 2, 14, 4, 10, 8),
-     ((), None, None, 16, None, 3, 4, 2)),
-    (((), None, None, 4, 10, 7, 0, 11),
-     ((), None, None, 3, 4, 5, 7, 2)),
-    (((), None, None, 7, 11, 8, 0, 13),
-     ((), None, None, 5, 7, 8, 2, 17)),
-    (((), None, None, 13, None, 8, 0, 16),
-     ((), None, None, 17, None, 10, 0, 2)),
-    (((), None, None, 16, None, 8, 0, 17),
-     ((), None, None, 10, 0, 11, 2, 8)),
+    (((('s', 0, 1, 1, 0), ('s', 0, 3, 1, 2), ('s', 0, 10, 0, 5), ('s', 0, 7, 1, 4), ('a', 1, 0), ('a', 7, 0), ('a', 10, 1), ('a', 3, 0), ('s', 10, 11, 1, 3), ('s', 7, 8, 0, 4), ('s', 3, 4, 0, 1), ('a', 1, 1), ('t', 0)), 1, None, None, None, 0, 1, 12),
+     ((('s', 0, 4, 1, 1), ('s', 0, 1, 1, 3), ('a', 4, 0), ('a', 1, 0), ('s', 1, 2, 0, 0), ('s', 1, 10, 0, 5), ('s', 4, 6, 0, 2), ('a', 1, 1), ('a', 4, 1)), 1, 4, None, None, 1, 4, 0)),
+    (((('a', 3, 1), ('a', 7, 1), ('a', 10, 0)), 3, None, None, None, 1, 3, 0),
+     ((('s', 1, 10, 1, 5), ('s', 1, 2, 1, 0), ('s', 1, 7, 0, 4), ('s', 4, 6, 1, 2), ('a', 2, 0), ('a', 6, 0), ('a', 10, 0), ('s', 6, 5, 0, 1), ('s', 10, 11, 0, 3), ('s', 1, 7, 1, 4), ('a', 10, 1)), None, None, None, None, 0, 4, 10)),
+    (((), None, None, None, None, 0, 3, 7),
+     ((('a', 2, 1), ('a', 7, 0), ('a', 6, 1), ('t', 3)), 10, None, None, None, 1, 10, 15)),
+    (((), 7, None, None, None, 3, 7, 1),
+     ((), None, None, None, None, 4, 10, 1)),
+    (((), None, None, None, None, 3, 7, 12),
+     ((), None, None, None, None, 4, 10, 2)),
+    (((('s', 3, 4, 1, 1), ('s', 10, 11, 0, 3)), None, None, None, None, 1, 3, 10),
+     ((), 2, None, None, None, 1, 2, 6)),
+    (((('t', 2),), None, None, None, None, 1, 3, 14),
+     ((('s', 10, 11, 1, 3), ('s', 6, 5, 1, 1), ('s', 7, 8, 0, 4), ('s', 2, 3, 0, 0)), 6, None, None, None, 2, 6, 15)),
+    (((('a', 8, 0), ('a', 11, 1)), 10, None, None, None, 7, 10, 14),
+     ((('t', 0),), None, None, None, None, 10, 6, 12)),
+    (((('a', 4, 0), ('s', 4, 6, 0, 2), ('s', 10, 8, 1, 5), ('s', 1, 2, 0, 0), ('a', 4, 1)), None, None, None, None, 1, 10, 4),
+     ((('a', 11, 0), ('a', 7, 1), ('a', 5, 0), ('s', 11, 9, 0, 5), ('t', 2)), None, None, None, None, 1, 2, 14)),
+    (((('a', 11, 0),), 4, None, None, None, 10, 4, 7),
+     ((), None, None, None, None, 0, 2, 7)),
+    (((), None, None, None, None, 10, 4, 12),
+     ((), None, None, None, None, 4, 10, 7)),
+    (((), None, None, None, None, 1, 3, 11),
+     ((('t', 5),), 7, None, None, None, 6, 7, 17)),
+    (((), None, None, None, None, 4, 7, 11),
+     ((), None, None, None, None, 10, 7, 6)),
+    (((), 11, None, None, None, 11, 0, 12),
+     ((('s', 7, 8, 1, 4),), None, None, None, None, 10, 7, 14)),
+    (((('s', 4, 6, 1, 2), ('t', 1)), None, None, 12, None, 10, 11, 13),
+     ((('a', 11, 1),), None, None, None, None, 0, 2, 11)),
+    (((('a', 2, 0), ('a', 6, 0), ('a', 8, 1)), None, None, 10, None, 1, 4, 8),
+     ((('s', 11, 9, 1, 5), ('a', 5, 1), ('a', 3, 0)), None, None, None, None, 6, 7, 11)),
+    (((), 8, None, None, None, 11, 8, 14),
+     ((('a', 8, 0),), 11, None, None, None, 7, 11, 12)),
+    (((('t', 3),), None, None, None, None, 0, 3, 15),
+     ((('a', 9, 0), ('t', 4)), 5, None, 7, None, 6, 5, 16)),
+    (((('s', 1, 2, 1, 0), ('s', 6, 5, 0, 1), ('s', 8, 9, 0, 3), ('a', 6, 1)), None, None, None, None, 0, 1, 6),
+     ((), None, None, None, None, 6, 5, 16)),
+    (((), None, None, None, None, 7, 8, 6),
+     ((('s', 2, 3, 1, 0),), None, None, 16, None, 10, 11, 5)),
+    (((('t', 5),), None, None, None, None, 0, 3, 17),
+     ((), None, None, None, None, 11, 5, 15)),
+    (((('s', 6, 5, 1, 1), ('s', 8, 9, 1, 3), ('a', 9, 0), ('a', 5, 0), ('a', 2, 1)), None, None, None, None, 0, 4, 2),
+     ((('a', 8, 1),), None, None, 15, None, 2, 4, 8)),
+    (((), 6, 2, 4, None, 6, 2, 11),
+     ((), None, None, None, None, 5, 6, 8)),
+    (((), None, None, None, None, 6, 2, 14),
+     ((('a', 9, 1),), 8, None, 6, None, 5, 8, 12)),
+    (((), None, None, 14, None, 6, 2, 15),
+     ((), None, None, None, None, 11, 8, 14)),
+    (((), None, None, None, None, 6, 2, 17),
+     ((('t', 1),), None, None, None, None, 1, 5, 13)),
+    (((), None, None, None, None, 7, 8, 2),
+     ((), None, None, None, None, 8, 10, 13)),
+    (((('t', 4),), None, None, None, None, 3, 6, 16),
+     ((('a', 3, 1),), None, None, None, None, 0, 2, 9)),
+    (((('a', 5, 1), ('a', 9, 1)), None, None, 6, None, 2, 7, 5),
+     ((), 9, None, 2, None, 9, 0, 12)),
+    (((), 5, None, 7, None, 5, 0, 15),
+     ((), None, None, 12, None, 9, 0, 13)),
+    (((), None, None, 15, None, 5, 0, 16),
+     ((), None, None, 13, None, 1, 4, 3)),
+    (((), None, None, 16, None, 5, 0, 17),
+     ((), 3, None, 1, 4, 5, 3, 17)),
+    (((), None, None, 17, None, 8, 5, 13),
+     ((), None, None, 17, None, 8, 10, 3)),
+    (((), None, None, 13, None, 8, 11, 5),
+     ((), None, None, 8, 10, 9, 3, 5)),
+    (((), None, None, 8, 11, 1, 2, 9),
+     ((), None, None, 5, None, 9, 3, 14)),
+    (((), None, None, 5, 1, 3, 0, 9),
+     ((), None, None, 9, 14, 11, 0, 3)),
 )
 
 TAIL = (
-    (8, 0, 17),
-    (11, 2, 8),
+    (2, 3, 0, 9),
+    (11, 0, 3),
 )
 
 
@@ -355,7 +355,7 @@
 
     rest = incoming.at[pl.ds(1, HELD - 1)]
     pltpu.make_async_copy(rest, rest, result_recv).wait()
-    out_ref[...] = jnp.max(incoming[...], axis=0)
+    out_ref[...] = jnp.max(incoming[...], axis=0).reshape(rows)
 
     for which in (0, 1):
         @pl.when(core == which)
@@ -376,9 +376,9 @@
     rows, width = embeddings.shape
     chunks = 1 + max(h for sends in LAST_SENDS for _, h in sends)
     dma = pltpu.SemaphoreType.DMA
-    best = pl.pallas_call(
+    return pl.pallas_call(
         functools.partial(kernel, chunks),
-        out_shape=jax.ShapeDtypeStruct((1, rows), jnp.float32),
+        out_shape=jax.ShapeDtypeStruct((rows,), jnp.float32),
         in_specs=[pl.BlockSpec(memory_space=pl.ANY), pl.BlockSpec(memory_space=pl.ANY)],
         out_specs=pl.BlockSpec(memory_space=pltpu.VMEM),
         scratch_shapes=[
@@ -397,7 +397,6 @@
         compiler_params=pltpu.CompilerParams(
             collective_id=0, has_side_effects=True, vmem_limit_bytes=VMEM_BYTES),
     )(embeddings, cluster_ids.reshape(1, rows))
-    return best.reshape(rows)
 
 
 def solution(mesh):

time: 55.6 us -> 55.5 us (level)
  the two profiles are of different devices: /device:TPU:1 before, /device:TPU:2 now
where the time goes in v7:
time: 55.5 us; the launch traced here: 55.4 us
  Pallas kernels  54.1 us (97%)
  local copies, waits for them, and re-layouts  1.24 us (2%)
    pallas_call x1, Pallas kernels, body(): pl.pallas_call(functools.partial(kernel, chunks), out_shape=jax.ShapeDtyp...  54.1 us
    unnamed x1, local copies, waits for them, and re-layouts  1.24 us

profile of v7, /device:TPU:2, one launch (start us, length us, event | category | flops | bytes accessed | tf_op | source)
XLA Modules:
  0.0 55.4 jit_solution(5974360585645809677)
XLA Ops:
  0.0 54.1 %shard_map.28 = f32[256]{0:T(256)} custom-call(f32[256,768]{1,0:T(8,128)} %emb_ref.1, s32[1,256]{1,0:T(1,128)} %bitcast.1), custom_call_target="tpu_custom_call" | custom-call | tf_op jit(solution)/shard_map/pallas_call | solution.py:379
  54.1 1.2 %copy.4 = f32[256]{0:T(256)} copy(f32[256]{0:T(256)} %shard_map.28) | data formatting | bytes 2048

commit v8 on v7

--- a/solution.py
+++ b/solution.py
@@ -14,17 +14,17 @@
 DIRS = ((1, 0, 0), (3, 0, 0), (0, 1, 0), (0, 3, 0), (0, 0, 1), (0, 0, 3))
 
 OFFSETS = (
-    ((0, 0, 0), (1, 0, 0), (2, 0, 0), (0, 1, 0), (3, 1, 0), (2, 2, 0),
-     (3, 2, 0), (0, 0, 1), (0, 0, 2), (0, 3, 2), (0, 0, 3), (0, 3, 3)),
-    ((0, 0, 0), (0, 3, 0), (1, 3, 0), (2, 3, 0), (3, 0, 0), (2, 1, 0),
-     (3, 1, 0), (0, 3, 1), (0, 3, 2), (0, 2, 2), (0, 3, 3), (0, 2, 3)),
-)
-
-SHARED = ((0, 2, 4, 7, 9, 11), (1, 2, 4, 7, 8, 11))
+    ((0, 0, 0), (0, 1, 0), (1, 1, 0), (0, 2, 0), (1, 2, 0), (0, 3, 0),
+     (3, 0, 0), (0, 0, 1), (0, 0, 2), (2, 0, 2), (2, 0, 3), (3, 0, 3)),
+    ((0, 0, 0), (1, 1, 0), (2, 1, 0), (1, 2, 0), (2, 2, 0), (1, 3, 0),
+     (1, 0, 0), (1, 0, 1), (1, 0, 2), (3, 0, 2), (3, 0, 3), (0, 0, 3)),
+)
+
+SHARED = ((2, 5, 7, 9, 10, 11), (0, 2, 4, 7, 8, 11))
 
 FIRST_SENDS = (
-    ((0, 1, 0, 0), (0, 3, 0, 2), (0, 7, 0, 4), (0, 10, 1, 5)),
-    ((0, 4, 0, 1), (0, 1, 0, 3)),
+    ((0, 6, 0, 1), (0, 1, 0, 2), (0, 5, 0, 3), (0, 7, 0, 4)),
+    ((0, 6, 0, 0), (0, 11, 0, 5)),
 )
 
 LAST_SENDS = (
@@ -33,83 +33,47 @@
 )
 
 STEPS = (
-    (((('s', 0, 1, 1, 0), ('s', 0, 3, 1, 2), ('s', 0, 10, 0, 5), ('s', 0, 7, 1, 4), ('a', 1, 0), ('a', 7, 0), ('a', 10, 1), ('a', 3, 0), ('s', 10, 11, 1, 3), ('s', 7, 8, 0, 4), ('s', 3, 4, 0, 1), ('a', 1, 1), ('t', 0)), 1, None, None, None, 0, 1, 12),
-     ((('s', 0, 4, 1, 1), ('s', 0, 1, 1, 3), ('a', 4, 0), ('a', 1, 0), ('s', 1, 2, 0, 0), ('s', 1, 10, 0, 5), ('s', 4, 6, 0, 2), ('a', 1, 1), ('a', 4, 1)), 1, 4, None, None, 1, 4, 0)),
-    (((('a', 3, 1), ('a', 7, 1), ('a', 10, 0)), 3, None, None, None, 1, 3, 0),
-     ((('s', 1, 10, 1, 5), ('s', 1, 2, 1, 0), ('s', 1, 7, 0, 4), ('s', 4, 6, 1, 2), ('a', 2, 0), ('a', 6, 0), ('a', 10, 0), ('s', 6, 5, 0, 1), ('s', 10, 11, 0, 3), ('s', 1, 7, 1, 4), ('a', 10, 1)), None, None, None, None, 0, 4, 10)),
-    (((), None, None, None, None, 0, 3, 7),
-     ((('a', 2, 1), ('a', 7, 0), ('a', 6, 1), ('t', 3)), 10, None, None, None, 1, 10, 15)),
-    (((), 7, None, None, None, 3, 7, 1),
-     ((), None, None, None, None, 4, 10, 1)),
-    (((), None, None, None, None, 3, 7, 12),
-     ((), None, None, None, None, 4, 10, 2)),
-    (((('s', 3, 4, 1, 1), ('s', 10, 11, 0, 3)), None, None, None, None, 1, 3, 10),
-     ((), 2, None, None, None, 1, 2, 6)),
-    (((('t', 2),), None, None, None, None, 1, 3, 14),
-     ((('s', 10, 11, 1, 3), ('s', 6, 5, 1, 1), ('s', 7, 8, 0, 4), ('s', 2, 3, 0, 0)), 6, None, None, None, 2, 6, 15)),
-    (((('a', 8, 0), ('a', 11, 1)), 10, None, None, None, 7, 10, 14),
-     ((('t', 0),), None, None, None, None, 10, 6, 12)),
-    (((('a', 4, 0), ('s', 4, 6, 0, 2), ('s', 10, 8, 1, 5), ('s', 1, 2, 0, 0), ('a', 4, 1)), None, None, None, None, 1, 10, 4),
-     ((('a', 11, 0), ('a', 7, 1), ('a', 5, 0), ('s', 11, 9, 0, 5), ('t', 2)), None, None, None, None, 1, 2, 14)),
-    (((('a', 11, 0),), 4, None, None, None, 10, 4, 7),
-     ((), None, None, None, None, 0, 2, 7)),
-    (((), None, None, None, None, 10, 4, 12),
-     ((), None, None, None, None, 4, 10, 7)),
-    (((), None, None, None, None, 1, 3, 11),
-     ((('t', 5),), 7, None, None, None, 6, 7, 17)),
-    (((), None, None, None, None, 4, 7, 11),
-     ((), None, None, None, None, 10, 7, 6)),
-    (((), 11, None, None, None, 11, 0, 12),
-     ((('s', 7, 8, 1, 4),), None, None, None, None, 10, 7, 14)),
-    (((('s', 4, 6, 1, 2), ('t', 1)), None, None, 12, None, 10, 11, 13),
-     ((('a', 11, 1),), None, None, None, None, 0, 2, 11)),
-    (((('a', 2, 0), ('a', 6, 0), ('a', 8, 1)), None, None, 10, None, 1, 4, 8),
-     ((('s', 11, 9, 1, 5), ('a', 5, 1), ('a', 3, 0)), None, None, None, None, 6, 7, 11)),
-    (((), 8, None, None, None, 11, 8, 14),
-     ((('a', 8, 0),), 11, None, None, None, 7, 11, 12)),
-    (((('t', 3),), None, None, None, None, 0, 3, 15),
-     ((('a', 9, 0), ('t', 4)), 5, None, 7, None, 6, 5, 16)),
-    (((('s', 1, 2, 1, 0), ('s', 6, 5, 0, 1), ('s', 8, 9, 0, 3), ('a', 6, 1)), None, None, None, None, 0, 1, 6),
-     ((), None, None, None, None, 6, 5, 16)),
-    (((), None, None, None, None, 7, 8, 6),
-     ((('s', 2, 3, 1, 0),), None, None, 16, None, 10, 11, 5)),
-    (((('t', 5),), None, None, None, None, 0, 3, 17),
-     ((), None, None, None, None, 11, 5, 15)),
-    (((('s', 6, 5, 1, 1), ('s', 8, 9, 1, 3), ('a', 9, 0), ('a', 5, 0), ('a', 2, 1)), None, None, None, None, 0, 4, 2),
-     ((('a', 8, 1),), None, None, 15, None, 2, 4, 8)),
-    (((), 6, 2, 4, None, 6, 2, 11),
-     ((), None, None, None, None, 5, 6, 8)),
-    (((), None, None, None, None, 6, 2, 14),
-     ((('a', 9, 1),), 8, None, 6, None, 5, 8, 12)),
-    (((), None, None, 14, None, 6, 2, 15),
-     ((), None, None, None, None, 11, 8, 14)),
-    (((), None, None, None, None, 6, 2, 17),
-     ((('t', 1),), None, None, None, None, 1, 5, 13)),
-    (((), None, None, None, None, 7, 8, 2),
-     ((), None, None, None, None, 8, 10, 13)),
-    (((('t', 4),), None, None, None, None, 3, 6, 16),
-     ((('a', 3, 1),), None, None, None, None, 0, 2, 9)),
-    (((('a', 5, 1), ('a', 9, 1)), None, None, 6, None, 2, 7, 5),
-     ((), 9, None, 2, None, 9, 0, 12)),
-    (((), 5, None, 7, None, 5, 0, 15),
-     ((), None, None, 12, None, 9, 0, 13)),
-    (((), None, None, 15, None, 5, 0, 16),
-     ((), None, None, 13, None, 1, 4, 3)),
-    (((), None, None, 16, None, 5, 0, 17),
-     ((), 3, None, 1, 4, 5, 3, 17)),
-    (((), None, None, 17, None, 8, 5, 13),
-     ((), None, None, 17, None, 8, 10, 3)),
-    (((), None, None, 13, None, 8, 11, 5),
-     ((), None, None, 8, 10, 9, 3, 5)),
-    (((), None, None, 8, 11, 1, 2, 9),
-     ((), None, None, 5, None, 9, 3, 14)),
-    (((), None, None, 5, 1, 3, 0, 9),
-     ((), None, None, 9, 14, 11, 0, 3)),
+    (((('s', 0, 6, 1, 1), ('s', 0, 1, 1, 2), ('s', 0, 5, 1, 3), ('s', 0, 7, 1, 4), ('a', 7, 0), ('a', 6, 0), ('a', 5, 0), ('a', 1, 0), ('s', 1, 2, 0, 0), ('s', 6, 11, 0, 5), ('s', 5, 3, 0, 3), ('a', 1, 1), ('a', 6, 1), ('a', 5, 1)), (1, 6, 5, None), (None, None), (1, 6, 0, 6, 5, 1)),
+     ((('s', 0, 6, 1, 0), ('s', 0, 11, 1, 5), ('a', 11, 0), ('a', 6, 0), ('s', 11, 10, 0, 1), ('s', 6, 7, 0, 4), ('s', 6, 1, 0, 2), ('a', 6, 1), ('a', 11, 1), ('t', 0)), (6, 11, None, None), (None, None), (0, 6, 12, 6, 11, 0))),
+    (((('a', 7, 1),), (7, None, None, None), (None, None), (0, 1, 7, 6, 7, 5)),
+     ((('s', 6, 1, 1, 2), ('s', 6, 5, 1, 3), ('s', 11, 10, 1, 1), ('s', 6, 7, 1, 4), ('a', 7, 0), ('a', 1, 0), ('a', 10, 0), ('s', 1, 2, 0, 0), ('s', 1, 3, 0, 2), ('s', 6, 5, 0, 3), ('s', 10, 9, 0, 5), ('a', 7, 1)), (7, None, None, None), (None, None), (6, 7, 11, 11, 7, 12))),
+    (((('s', 1, 2, 1, 0), ('s', 6, 11, 1, 5), ('t', 5)), (None, None, None, None), (None, None), (1, 5, 17, 6, 7, 17)),
+     ((('a', 5, 1), ('a', 10, 1), ('a', 1, 1)), (None, None, None, None), (None, None), (6, 7, 10, 0, 6, 1))),
+    (((('a', 11, 0), ('a', 2, 0), ('a', 3, 0), ('s', 7, 8, 0, 4), ('s', 11, 10, 0, 1), ('a', 11, 1)), (11, None, None, None), (None, None), (1, 5, 11, 6, 11, 7)),
+     ((), (10, 1, None, None), (None, None), (7, 10, 1, 10, 1, 12))),
+    (((('a', 2, 1),), (None, None, None, None), (None, None), (5, 6, 2, 7, 11, 2)),
+     ((('s', 1, 2, 1, 0), ('s', 10, 9, 1, 5), ('s', 7, 8, 0, 4), ('t', 3), ('t', 1)), (None, None, None, None), (None, None), (10, 1, 15, 0, 6, 13))),
+    (((('s', 2, 4, 0, 2), ('s', 11, 10, 1, 1), ('t', 2)), (2, None, None, None), (None, None), (1, 2, 14, 5, 6, 14)),
+     ((('a', 2, 0), ('a', 5, 0), ('t', 5)), (5, None, None, None), (None, None), (0, 7, 5, 1, 5, 17))),
+    (((('s', 5, 3, 1, 3), ('a', 8, 0), ('a', 10, 0), ('s', 7, 8, 1, 4), ('s', 10, 9, 0, 5), ('s', 2, 4, 1, 2), ('a', 4, 0), ('a', 3, 1), ('t', 1)), (3, None, None, None), (None, None), (1, 6, 13, 2, 3, 17)),
+     ((('a', 3, 0), ('a', 9, 0)), (None, None, None, None), (None, None), (10, 5, 13, 10, 11, 5))),
+    (((('a', 10, 1), ('t', 4)), (None, None, None, None), (None, None), (5, 3, 16, 7, 11, 3)),
+     ((('s', 3, 4, 0, 0), ('s', 5, 3, 1, 3), ('a', 8, 0), ('a', 2, 1)), (None, None, None, None), (None, None), (11, 5, 1, 0, 5, 2))),
+    (((), (None, None, None, None), (None, None), (11, 3, 14, 0, 2, 10)),
+     ((('a', 9, 1),), (2, None, None, None), (None, None), (5, 2, 12, 5, 2, 15))),
+    (((('s', 10, 9, 1, 5), ('t', 0)), (None, None, None, None), (None, None), (3, 5, 10, 5, 6, 12)),
+     ((('s', 7, 8, 1, 4), ('s', 2, 4, 1, 2)), (None, None, None, None), (12, None), (5, 2, 15, 7, 10, 2))),
+    (((('a', 4, 1), ('t', 3)), (4, None, None, None), (None, None), (1, 3, 15, 4, 0, 14)),
+     ((('a', 3, 1),), (3, None, None, None), (5, None), (1, 2, 9, 2, 3, 17))),
+    (((('a', 9, 0), ('a', 8, 1)), (None, None, None, None), (14, None), (4, 0, 16, 5, 4, 15)),
+     ((('a', 4, 0),), (9, None, None, None), (None, None), (7, 9, 3, 9, 3, 13))),
+    (((), (10, None, None, None), (16, 5), (10, 4, 7, 0, 1, 8)),
+     ((), (None, None, None, None), (None, None), (9, 3, 15, 10, 11, 3))),
+    (((), (8, None, None, None), (7, None), (2, 3, 8, 6, 8, 4)),
+     ((('t', 4),), (None, None, None, None), (15, 10), (1, 3, 16, 6, 0, 16))),
+    (((('a', 9, 1),), (None, None, None, None), (6, 4), (8, 0, 15, 10, 8, 12)),
+     ((('a', 4, 1), ('a', 8, 1), ('t', 2)), (8, None, None, None), (16, None), (0, 7, 4, 0, 8, 14))),
+    (((), (None, None, None, None), (15, None), (10, 8, 13, 10, 8, 17)),
+     ((), (None, None, None, None), (7, 14), (1, 2, 8, 3, 6, 8))),
+    (((), (None, None, None, None), (13, 10), (1, 2, 9, 3, 0, 9)),
+     ((), (4, None, None, None), (1, 2), (4, 8, 9, 4, 8, 17))),
+    (((), (9, None, None, None), (17, 1), (9, 0, 12, 11, 9, 8)),
+     ((), (None, None, None, None), (3, 6), (8, 0, 13, 11, 0, 8))),
 )
 
 TAIL = (
-    (2, 3, 0, 9),
-    (11, 0, 3),
+    (2, 3, 0, 12, 11, 9, 8),
+    (9, 4, 17, 13, 11, 0, 8),
 )
 
 
@@ -119,17 +83,25 @@
 NONE = 31
 
 
-def lookup(values, n, bits=5):
+def words(values, bits=5):
     each = 30 // bits
-    words = [sum(v << (bits * k) for k, v in enumerate(values[s:s + each])) for s in range(0, len(values), each)]
-    word = jnp.int32(words[0])
-    for k, w in enumerate(words[1:], 1):
-        word = jnp.where(n >= each * k, jnp.int32(w), word)
+    return [sum(v << (bits * k) for k, v in enumerate(values[s:s + each])) for s in range(0, len(values), each)]
+
+
+def lookup(packed, n, bits=5):
+    each = 30 // bits
+    word = packed[0]
+    for k, w in enumerate(packed[1:], 1):
+        word = jnp.where(n >= each * k, w, word)
     return lax.rem(lax.shift_right_logical(word, bits * lax.rem(n, each)), 1 << bits)
 
 
-def column(which, place):
-    return [NONE if pair[which][place] is None else pair[which][place] for pair in STEPS]
+def of_core(core, lists, bits=5):
+    return [jnp.where(core == 0, jnp.int32(a), jnp.int32(b)) for a, b in zip(*(words(v, bits) for v in lists))]
+
+
+def column(which, place, k):
+    return [NONE if pair[which][place][k] is None else pair[which][place][k] for pair in STEPS]
 
 
 def kernel(chunks, emb_ref, lab_ref, out_ref, emb, ids, buf, labels, label_rows, row_best, column_best, outgoing,
@@ -253,8 +225,7 @@
 
     def answer(slot):
         offsets = [OFFSETS[w] + tuple(OFFSETS[1 - w][k] for k in SHARED[w]) for w in (0, 1)]
-        back = [SIDE - jnp.where(core == 0, *(lookup([o[k] for o in offsets[w]], slot, 2) for w in (0, 1)))
-                for k in range(3)]
+        back = [SIDE - lookup(of_core(core, [[o[k] for o in held] for held in offsets], 2), slot, 2) for k in range(3)]
         return pltpu.make_async_remote_copy(
             src_ref=outgoing.at[slot], dst_ref=incoming.at[slot],
             send_sem=result_send.at[slot], recv_sem=result_recv,
@@ -309,9 +280,10 @@
                                 sent(*op[5:])
                             send(*op[1:5])
 
-    def chosen(place, n):
-        return jnp.where(core == 0, lookup(column(0, place), n), lookup(column(1, place), n))
-
+    def table(place):
+        return [of_core(core, [column(w, place, k) for w in (0, 1)]) for k in range(len(STEPS[0][0][place]))]
+
+    to_open, to_finish, to_compare = table(1), table(2), table(3)
     spread(0)
     tile((0,), 0, own=True)
 
@@ -323,28 +295,24 @@
                     @pl.when(n == k)
                     def _(k=k):
                         moves(k)
-        for place in (1, 2):
-            opened = chosen(place, n)
-
-            @pl.when(opened != NONE)
-            def _(opened=opened):
-                spread(opened)
-        for place in (3, 4):
-            ended = chosen(place, n)
-
-            @pl.when(ended != NONE)
-            def _(ended=ended):
-                finish(ended)
-
-        tile((chosen(5, n), chosen(6, n)), chosen(7, n))
+        for listed, act in ((to_open, spread), (to_finish, finish)):
+            for packed in listed:
+                slot = lookup(packed, n)
+
+                @pl.when(slot != NONE)
+                def _(slot=slot, act=act):
+                    act(slot)
+        units = [lookup(packed, n) for packed in to_compare]
+        for k in range(0, len(units), 3):
+            tile(units[k:k + 2], units[k + 2])
         return carry
 
     lax.fori_loop(0, len(STEPS), step, 0)
     left = max(len(t) for t in TAIL)
+    ends = of_core(core, [(list(t) + [NONE] * left)[:left] for t in TAIL])
 
     def last(n, carry):
-        ends = [(list(t) + [NONE] * left)[:left] for t in TAIL]
-        ended = jnp.where(core == 0, lookup(ends[0], n), lookup(ends[1], n))
+        ended = lookup(ends, n)
 
         @pl.when(ended != NONE)
         def _():

time: 55.5 us -> 50.4 us (0.908)
  the two profiles are of different devices: /device:TPU:2 before, /device:TPU:0 now
where the time goes in v8:
time: 50.4 us; the launch traced here: 50.3 us
  Pallas kernels  49 us (97%)
  local copies, waits for them, and re-layouts  1.24 us (2%)
    pallas_call x1, Pallas kernels, body(): pl.pallas_call(functools.partial(kernel, chunks), out_shape=jax.ShapeDtyp...  49 us
    unnamed x1, local copies, waits for them, and re-layouts  1.24 us

profile of v8, /device:TPU:0, one launch (start us, length us, event | category | flops | bytes accessed | tf_op | source)
XLA Modules:
  0.0 50.3 jit_solution(7566050293457723879)
XLA Ops:
  0.0 49.0 %shard_map.28 = f32[256]{0:T(256)} custom-call(f32[256,768]{1,0:T(8,128)} %emb_ref.1, s32[1,256]{1,0:T(1,128)} %bitcast.1), custom_call_target="tpu_custom_call" | custom-call | tf_op jit(solution)/shard_map/pallas_call | solution.py:347
  49.1 1.2 %copy.4 = f32[256]{0:T(256)} copy(f32[256]{0:T(256)} %shard_map.28) | data formatting | bytes 2048

commit v9 on v8

--- a/solution.py
+++ b/solution.py
@@ -14,17 +14,17 @@
 DIRS = ((1, 0, 0), (3, 0, 0), (0, 1, 0), (0, 3, 0), (0, 0, 1), (0, 0, 3))
 
 OFFSETS = (
-    ((0, 0, 0), (0, 1, 0), (1, 1, 0), (0, 2, 0), (1, 2, 0), (0, 3, 0),
-     (3, 0, 0), (0, 0, 1), (0, 0, 2), (2, 0, 2), (2, 0, 3), (3, 0, 3)),
-    ((0, 0, 0), (1, 1, 0), (2, 1, 0), (1, 2, 0), (2, 2, 0), (1, 3, 0),
-     (1, 0, 0), (1, 0, 1), (1, 0, 2), (3, 0, 2), (3, 0, 3), (0, 0, 3)),
-)
-
-SHARED = ((2, 5, 7, 9, 10, 11), (0, 2, 4, 7, 8, 11))
+    ((0, 0, 0), (3, 0, 0), (0, 1, 0), (0, 2, 0), (2, 2, 0), (2, 3, 0),
+     (3, 3, 0), (0, 0, 1), (1, 0, 1), (0, 0, 2), (1, 0, 2), (0, 0, 3)),
+    ((0, 0, 0), (1, 0, 0), (1, 1, 0), (1, 2, 0), (3, 2, 0), (3, 3, 0),
+     (0, 3, 0), (1, 0, 1), (2, 0, 1), (1, 0, 2), (2, 0, 2), (1, 0, 3)),
+)
+
+SHARED = ((2, 4, 5, 6, 8, 11), (0, 2, 3, 6, 8, 10))
 
 FIRST_SENDS = (
-    ((0, 6, 0, 1), (0, 1, 0, 2), (0, 5, 0, 3), (0, 7, 0, 4)),
-    ((0, 6, 0, 0), (0, 11, 0, 5)),
+    ((0, 1, 0, 1), (0, 2, 0, 2), (0, 7, 1, 4), (0, 11, 0, 5)),
+    ((0, 1, 0, 0), (0, 6, 0, 3)),
 )
 
 LAST_SENDS = (
@@ -33,49 +33,48 @@
 )
 
 STEPS = (
-    (((('s', 0, 6, 1, 1), ('s', 0, 1, 1, 2), ('s', 0, 5, 1, 3), ('s', 0, 7, 1, 4), ('a', 7, 0), ('a', 6, 0), ('a', 5, 0), ('a', 1, 0), ('s', 1, 2, 0, 0), ('s', 6, 11, 0, 5), ('s', 5, 3, 0, 3), ('a', 1, 1), ('a', 6, 1), ('a', 5, 1)), (1, 6, 5, None), (None, None), (1, 6, 0, 6, 5, 1)),
-     ((('s', 0, 6, 1, 0), ('s', 0, 11, 1, 5), ('a', 11, 0), ('a', 6, 0), ('s', 11, 10, 0, 1), ('s', 6, 7, 0, 4), ('s', 6, 1, 0, 2), ('a', 6, 1), ('a', 11, 1), ('t', 0)), (6, 11, None, None), (None, None), (0, 6, 12, 6, 11, 0))),
-    (((('a', 7, 1),), (7, None, None, None), (None, None), (0, 1, 7, 6, 7, 5)),
-     ((('s', 6, 1, 1, 2), ('s', 6, 5, 1, 3), ('s', 11, 10, 1, 1), ('s', 6, 7, 1, 4), ('a', 7, 0), ('a', 1, 0), ('a', 10, 0), ('s', 1, 2, 0, 0), ('s', 1, 3, 0, 2), ('s', 6, 5, 0, 3), ('s', 10, 9, 0, 5), ('a', 7, 1)), (7, None, None, None), (None, None), (6, 7, 11, 11, 7, 12))),
-    (((('s', 1, 2, 1, 0), ('s', 6, 11, 1, 5), ('t', 5)), (None, None, None, None), (None, None), (1, 5, 17, 6, 7, 17)),
-     ((('a', 5, 1), ('a', 10, 1), ('a', 1, 1)), (None, None, None, None), (None, None), (6, 7, 10, 0, 6, 1))),
-    (((('a', 11, 0), ('a', 2, 0), ('a', 3, 0), ('s', 7, 8, 0, 4), ('s', 11, 10, 0, 1), ('a', 11, 1)), (11, None, None, None), (None, None), (1, 5, 11, 6, 11, 7)),
-     ((), (10, 1, None, None), (None, None), (7, 10, 1, 10, 1, 12))),
-    (((('a', 2, 1),), (None, None, None, None), (None, None), (5, 6, 2, 7, 11, 2)),
-     ((('s', 1, 2, 1, 0), ('s', 10, 9, 1, 5), ('s', 7, 8, 0, 4), ('t', 3), ('t', 1)), (None, None, None, None), (None, None), (10, 1, 15, 0, 6, 13))),
-    (((('s', 2, 4, 0, 2), ('s', 11, 10, 1, 1), ('t', 2)), (2, None, None, None), (None, None), (1, 2, 14, 5, 6, 14)),
-     ((('a', 2, 0), ('a', 5, 0), ('t', 5)), (5, None, None, None), (None, None), (0, 7, 5, 1, 5, 17))),
-    (((('s', 5, 3, 1, 3), ('a', 8, 0), ('a', 10, 0), ('s', 7, 8, 1, 4), ('s', 10, 9, 0, 5), ('s', 2, 4, 1, 2), ('a', 4, 0), ('a', 3, 1), ('t', 1)), (3, None, None, None), (None, None), (1, 6, 13, 2, 3, 17)),
-     ((('a', 3, 0), ('a', 9, 0)), (None, None, None, None), (None, None), (10, 5, 13, 10, 11, 5))),
-    (((('a', 10, 1), ('t', 4)), (None, None, None, None), (None, None), (5, 3, 16, 7, 11, 3)),
-     ((('s', 3, 4, 0, 0), ('s', 5, 3, 1, 3), ('a', 8, 0), ('a', 2, 1)), (None, None, None, None), (None, None), (11, 5, 1, 0, 5, 2))),
-    (((), (None, None, None, None), (None, None), (11, 3, 14, 0, 2, 10)),
-     ((('a', 9, 1),), (2, None, None, None), (None, None), (5, 2, 12, 5, 2, 15))),
-    (((('s', 10, 9, 1, 5), ('t', 0)), (None, None, None, None), (None, None), (3, 5, 10, 5, 6, 12)),
-     ((('s', 7, 8, 1, 4), ('s', 2, 4, 1, 2)), (None, None, None, None), (12, None), (5, 2, 15, 7, 10, 2))),
-    (((('a', 4, 1), ('t', 3)), (4, None, None, None), (None, None), (1, 3, 15, 4, 0, 14)),
-     ((('a', 3, 1),), (3, None, None, None), (5, None), (1, 2, 9, 2, 3, 17))),
-    (((('a', 9, 0), ('a', 8, 1)), (None, None, None, None), (14, None), (4, 0, 16, 5, 4, 15)),
-     ((('a', 4, 0),), (9, None, None, None), (None, None), (7, 9, 3, 9, 3, 13))),
-    (((), (10, None, None, None), (16, 5), (10, 4, 7, 0, 1, 8)),
-     ((), (None, None, None, None), (None, None), (9, 3, 15, 10, 11, 3))),
-    (((), (8, None, None, None), (7, None), (2, 3, 8, 6, 8, 4)),
-     ((('t', 4),), (None, None, None, None), (15, 10), (1, 3, 16, 6, 0, 16))),
-    (((('a', 9, 1),), (None, None, None, None), (6, 4), (8, 0, 15, 10, 8, 12)),
-     ((('a', 4, 1), ('a', 8, 1), ('t', 2)), (8, None, None, None), (16, None), (0, 7, 4, 0, 8, 14))),
-    (((), (None, None, None, None), (15, None), (10, 8, 13, 10, 8, 17)),
-     ((), (None, None, None, None), (7, 14), (1, 2, 8, 3, 6, 8))),
-    (((), (None, None, None, None), (13, 10), (1, 2, 9, 3, 0, 9)),
-     ((), (4, None, None, None), (1, 2), (4, 8, 9, 4, 8, 17))),
-    (((), (9, None, None, None), (17, 1), (9, 0, 12, 11, 9, 8)),
-     ((), (None, None, None, None), (3, 6), (8, 0, 13, 11, 0, 8))),
+    (((('s', 0, 7, 0, 4), ('s', 0, 2, 1, 2), ('s', 0, 1, 1, 1), ('s', 0, 11, 1, 5), ('a', 11, 0), ('a', 2, 0), ('a', 7, 1), ('s', 11, 9, 0, 5), ('a', 1, 0), ('s', 1, 6, 0, 3), ('s', 7, 8, 1, 0), ('a', 2, 1), ('a', 7, 0), ('a', 1, 1)), (2, 7, None, None), (None, None), (2, 7, 0, 0, 7, 1)),
+     ((('s', 0, 1, 1, 0), ('s', 0, 6, 1, 3), ('a', 6, 0), ('a', 1, 0), ('s', 6, 5, 0, 1), ('s', 1, 2, 0, 2), ('s', 1, 7, 0, 4), ('t', 0), ('a', 1, 1), ('a', 6, 1)), (1, 6, None, None), (None, None), (0, 1, 12, 1, 6, 0))),
+    (((('a', 11, 1), ('s', 1, 6, 1, 3), ('s', 7, 8, 0, 0), ('a', 8, 1)), (1, None, None, None), (None, None), (7, 1, 2, 1, 2, 11)),
+     ((('s', 1, 7, 1, 4), ('s', 1, 2, 1, 2), ('s', 1, 11, 0, 5), ('s', 6, 5, 1, 1), ('a', 7, 0), ('a', 5, 0), ('a', 2, 0), ('s', 1, 11, 1, 5), ('s', 5, 4, 0, 3), ('a', 5, 1), ('s', 7, 8, 0, 0)), (5, None, None, None), (None, None), (6, 5, 1, 6, 5, 12))),
+    (((('a', 6, 0), ('a', 9, 0), ('s', 2, 3, 0, 2), ('s', 7, 9, 1, 4), ('s', 6, 5, 0, 1), ('a', 8, 0), ('t', 3)), (None, None, None, None), (None, None), (1, 7, 15, 1, 2, 8)),
+     ((('t', 1), ('a', 7, 1), ('a', 2, 1)), (None, None, None, None), (None, None), (6, 5, 13, 0, 1, 7))),
+    (((), (8, 11, None, None), (None, None), (7, 8, 11, 11, 8, 15)),
+     ((), (None, None, None, None), (None, None), (5, 6, 7, 5, 6, 2))),
+    (((('a', 6, 1), ('s', 6, 5, 1, 1)), (None, None, None, None), (None, None), (2, 7, 6, 8, 11, 6)),
+     ((('s', 5, 4, 1, 3), ('a', 11, 0), ('s', 7, 8, 1, 0), ('s', 2, 3, 0, 2), ('s', 11, 9, 0, 5), ('t', 4)), (7, 2, None, None), (None, None), (7, 2, 12, 0, 1, 16))),
+    (((('s', 8, 10, 1, 4), ('t', 2), ('t', 0)), (6, None, None, None), (None, None), (8, 11, 14, 1, 6, 12)),
+     ((('a', 11, 1),), (None, None, None, None), (None, None), (0, 5, 11, 6, 7, 11))),
+    (((('a', 3, 0), ('a', 5, 0), ('a', 9, 1)), (None, None, None, None), (None, None), (7, 8, 12, 2, 6, 9)),
+     ((('a', 8, 0), ('a', 4, 0)), (11, None, None, None), (None, None), (7, 11, 2, 7, 11, 13))),
+    (((('t', 5),), (9, None, None, None), (None, None), (11, 9, 12, 1, 7, 17)),
+     ((('s', 8, 10, 0, 4), ('s', 11, 9, 1, 5), ('a', 4, 1), ('t', 3)), (4, None, None, None), (None, None), (7, 11, 15, 11, 4, 16))),
+    (((('s', 9, 10, 0, 0), ('s', 2, 3, 1, 2), ('s', 5, 4, 0, 3), ('a', 5, 1)), (None, None, None, None), (None, None), (0, 2, 5, 8, 9, 5)),
+     ((('a', 8, 1), ('a', 9, 0), ('a', 3, 0)), (8, None, None, None), (None, None), (4, 8, 13, 5, 11, 8))),
+    (((), (5, None, None, None), (None, None), (9, 5, 15, 11, 0, 5)),
+     ((('s', 2, 3, 1, 2), ('s', 8, 10, 1, 4)), (None, None, None, None), (None, None), (7, 8, 4, 11, 8, 12))),
+    (((('s', 5, 4, 1, 3), ('t', 1), ('t', 4)), (None, None, None, None), (None, None), (7, 9, 13, 1, 5, 16)),
+     ((('a', 9, 1), ('a', 10, 0)), (None, None, None, None), (11, 12), (2, 4, 9, 5, 6, 9))),
+    (((('a', 3, 1),), (3, None, None, None), (None, None), (0, 6, 3, 3, 0, 15)),
+     ((), (None, None, None, None), (None, None), (0, 2, 8, 4, 8, 13))),
+    (((('a', 10, 1), ('a', 4, 0), ('a', 10, 0)), (None, None, None, None), (6, 15), (5, 3, 17, 7, 8, 3)),
+     ((), (9, None, None, None), (2, None), (8, 9, 15, 9, 0, 13))),
+    (((), (10, None, None, None), (5, 17), (11, 3, 13, 9, 10, 3)),
+     ((('t', 2),), (None, None, None, None), (13, None), (1, 7, 14, 9, 0, 14))),
+    (((('a', 4, 1),), (None, None, None, None), (None, None), (9, 10, 14, 10, 0, 12)),
+     ((('a', 10, 1),), (None, None, None, None), (14, None), (0, 4, 10, 5, 0, 10))),
+    (((), (None, None, None, None), (14, 12), (1, 2, 10, 11, 3, 16)),
+     ((('a', 3, 1), ('t', 5)), (3, None, None, None), (5, None), (0, 3, 17, 1, 4, 3))),
+    (((), (None, None, None, None), (1, 2), (10, 0, 13, 3, 7, 4)),
+     ((), (10, None, None, None), (0, 17), (6, 7, 3, 10, 3, 15))),
+    (((), (4, None, None, None), (11, 10), (4, 0, 16, 8, 9, 4)),
+     ((), (None, None, None, None), (1, 4), (9, 3, 16, 8, 9, 3))),
 )
 
 TAIL = (
-    (2, 3, 0, 12, 11, 9, 8),
-    (9, 4, 17, 13, 11, 0, 8),
-)
-
+    (13, 3, 7, 0, 16, 8, 9, 4),
+    (6, 7, 10, 15, 16, 8, 9, 3),
+)
 
 SLOTS = len(OFFSETS[0])
 EXTRA = len(SHARED[0])
@@ -321,10 +320,6 @@
 
     lax.fori_loop(0, left, last, 0)
 
-    rest = incoming.at[pl.ds(1, HELD - 1)]
-    pltpu.make_async_copy(rest, rest, result_recv).wait()
-    out_ref[...] = jnp.max(incoming[...], axis=0).reshape(rows)
-
     for which in (0, 1):
         @pl.when(core == which)
         def _(which=which):
@@ -338,6 +333,9 @@
         relay_label(0, slot, 0).wait_send()
     for slot in range(1, HELD):
         answer(slot).wait_send()
+    rest = incoming.at[pl.ds(1, HELD - 1)]
+    pltpu.make_async_copy(rest, rest, result_recv).wait()
+    out_ref[...] = jnp.max(incoming[...], axis=0).reshape(rows)
 
 
 def body(embeddings, cluster_ids):

time: 50.4 us -> 50.4 us (level)
  the two profiles are of different devices: /device:TPU:0 before, /device:TPU:1 now
where the time goes in v9:
time: 50.4 us; the launch traced here: 50.3 us
  Pallas kernels  49 us (97%)
  local copies, waits for them, and re-layouts  1.24 us (2%)
    pallas_call x1, Pallas kernels, body(): pl.pallas_call(functools.partial(kernel, chunks), out_shape=jax.ShapeDtyp...  49 us
    unnamed x1, local copies, waits for them, and re-layouts  1.24 us

profile of v9, /device:TPU:1, one launch (start us, length us, event | category | flops | bytes accessed | tf_op | source)
XLA Modules:
  0.0 50.3 jit_solution(5114399346975262569)
XLA Ops:
  0.0 49.0 %shard_map.28 = f32[256]{0:T(256)} custom-call(f32[256,768]{1,0:T(8,128)} %emb_ref.1, s32[1,256]{1,0:T(1,128)} %bitcast.1), custom_call_target="tpu_custom_call" | custom-call | tf_op jit(solution)/shard_map/pallas_call | solution.py:345
  49.0 1.2 %copy.4 = f32[256]{0:T(256)} copy(f32[256]{0:T(256)} %shard_map.28) | data formatting | bytes 2048

commit v10 on v9

--- a/solution.py
+++ b/solution.py
@@ -33,47 +33,47 @@
 )
 
 STEPS = (
-    (((('s', 0, 7, 0, 4), ('s', 0, 2, 1, 2), ('s', 0, 1, 1, 1), ('s', 0, 11, 1, 5), ('a', 11, 0), ('a', 2, 0), ('a', 7, 1), ('s', 11, 9, 0, 5), ('a', 1, 0), ('s', 1, 6, 0, 3), ('s', 7, 8, 1, 0), ('a', 2, 1), ('a', 7, 0), ('a', 1, 1)), (2, 7, None, None), (None, None), (2, 7, 0, 0, 7, 1)),
-     ((('s', 0, 1, 1, 0), ('s', 0, 6, 1, 3), ('a', 6, 0), ('a', 1, 0), ('s', 6, 5, 0, 1), ('s', 1, 2, 0, 2), ('s', 1, 7, 0, 4), ('t', 0), ('a', 1, 1), ('a', 6, 1)), (1, 6, None, None), (None, None), (0, 1, 12, 1, 6, 0))),
-    (((('a', 11, 1), ('s', 1, 6, 1, 3), ('s', 7, 8, 0, 0), ('a', 8, 1)), (1, None, None, None), (None, None), (7, 1, 2, 1, 2, 11)),
-     ((('s', 1, 7, 1, 4), ('s', 1, 2, 1, 2), ('s', 1, 11, 0, 5), ('s', 6, 5, 1, 1), ('a', 7, 0), ('a', 5, 0), ('a', 2, 0), ('s', 1, 11, 1, 5), ('s', 5, 4, 0, 3), ('a', 5, 1), ('s', 7, 8, 0, 0)), (5, None, None, None), (None, None), (6, 5, 1, 6, 5, 12))),
-    (((('a', 6, 0), ('a', 9, 0), ('s', 2, 3, 0, 2), ('s', 7, 9, 1, 4), ('s', 6, 5, 0, 1), ('a', 8, 0), ('t', 3)), (None, None, None, None), (None, None), (1, 7, 15, 1, 2, 8)),
-     ((('t', 1), ('a', 7, 1), ('a', 2, 1)), (None, None, None, None), (None, None), (6, 5, 13, 0, 1, 7))),
-    (((), (8, 11, None, None), (None, None), (7, 8, 11, 11, 8, 15)),
-     ((), (None, None, None, None), (None, None), (5, 6, 7, 5, 6, 2))),
-    (((('a', 6, 1), ('s', 6, 5, 1, 1)), (None, None, None, None), (None, None), (2, 7, 6, 8, 11, 6)),
-     ((('s', 5, 4, 1, 3), ('a', 11, 0), ('s', 7, 8, 1, 0), ('s', 2, 3, 0, 2), ('s', 11, 9, 0, 5), ('t', 4)), (7, 2, None, None), (None, None), (7, 2, 12, 0, 1, 16))),
-    (((('s', 8, 10, 1, 4), ('t', 2), ('t', 0)), (6, None, None, None), (None, None), (8, 11, 14, 1, 6, 12)),
-     ((('a', 11, 1),), (None, None, None, None), (None, None), (0, 5, 11, 6, 7, 11))),
-    (((('a', 3, 0), ('a', 5, 0), ('a', 9, 1)), (None, None, None, None), (None, None), (7, 8, 12, 2, 6, 9)),
-     ((('a', 8, 0), ('a', 4, 0)), (11, None, None, None), (None, None), (7, 11, 2, 7, 11, 13))),
-    (((('t', 5),), (9, None, None, None), (None, None), (11, 9, 12, 1, 7, 17)),
-     ((('s', 8, 10, 0, 4), ('s', 11, 9, 1, 5), ('a', 4, 1), ('t', 3)), (4, None, None, None), (None, None), (7, 11, 15, 11, 4, 16))),
-    (((('s', 9, 10, 0, 0), ('s', 2, 3, 1, 2), ('s', 5, 4, 0, 3), ('a', 5, 1)), (None, None, None, None), (None, None), (0, 2, 5, 8, 9, 5)),
-     ((('a', 8, 1), ('a', 9, 0), ('a', 3, 0)), (8, None, None, None), (None, None), (4, 8, 13, 5, 11, 8))),
-    (((), (5, None, None, None), (None, None), (9, 5, 15, 11, 0, 5)),
-     ((('s', 2, 3, 1, 2), ('s', 8, 10, 1, 4)), (None, None, None, None), (None, None), (7, 8, 4, 11, 8, 12))),
-    (((('s', 5, 4, 1, 3), ('t', 1), ('t', 4)), (None, None, None, None), (None, None), (7, 9, 13, 1, 5, 16)),
-     ((('a', 9, 1), ('a', 10, 0)), (None, None, None, None), (11, 12), (2, 4, 9, 5, 6, 9))),
-    (((('a', 3, 1),), (3, None, None, None), (None, None), (0, 6, 3, 3, 0, 15)),
-     ((), (None, None, None, None), (None, None), (0, 2, 8, 4, 8, 13))),
-    (((('a', 10, 1), ('a', 4, 0), ('a', 10, 0)), (None, None, None, None), (6, 15), (5, 3, 17, 7, 8, 3)),
-     ((), (9, None, None, None), (2, None), (8, 9, 15, 9, 0, 13))),
-    (((), (10, None, None, None), (5, 17), (11, 3, 13, 9, 10, 3)),
-     ((('t', 2),), (None, None, None, None), (13, None), (1, 7, 14, 9, 0, 14))),
-    (((('a', 4, 1),), (None, None, None, None), (None, None), (9, 10, 14, 10, 0, 12)),
-     ((('a', 10, 1),), (None, None, None, None), (14, None), (0, 4, 10, 5, 0, 10))),
-    (((), (None, None, None, None), (14, 12), (1, 2, 10, 11, 3, 16)),
-     ((('a', 3, 1), ('t', 5)), (3, None, None, None), (5, None), (0, 3, 17, 1, 4, 3))),
-    (((), (None, None, None, None), (1, 2), (10, 0, 13, 3, 7, 4)),
-     ((), (10, None, None, None), (0, 17), (6, 7, 3, 10, 3, 15))),
-    (((), (4, None, None, None), (11, 10), (4, 0, 16, 8, 9, 4)),
-     ((), (None, None, None, None), (1, 4), (9, 3, 16, 8, 9, 3))),
+    (((('s', 0, 7, 0, 4), ('s', 0, 2, 1, 2), ('s', 0, 1, 1, 1), ('s', 0, 11, 1, 5), ('a', 2, 0), ('a', 7, 1), ('a', 11, 0), ('s', 11, 9, 0, 5), ('a', 1, 0), ('s', 1, 6, 0, 3), ('s', 7, 8, 1, 0), ('a', 2, 1), ('a', 7, 0), ('a', 1, 1)), (2, 7, None, None), (None, None, None), (2, 7, 0, 0, 7, 1)),
+     ((('s', 0, 6, 1, 3), ('s', 0, 1, 1, 0), ('a', 6, 0), ('a', 1, 0), ('s', 6, 5, 0, 1), ('s', 1, 2, 0, 2), ('s', 1, 7, 0, 4), ('t', 0), ('a', 1, 1), ('a', 6, 1)), (1, 6, None, None), (None, None, None), (0, 1, 12, 1, 6, 0))),
+    (((('a', 11, 1), ('s', 7, 8, 0, 0), ('s', 1, 6, 1, 3), ('t', 3), ('a', 8, 1)), (1, None, None, None), (None, None, None), (7, 1, 2, 1, 2, 11)),
+     ((('s', 1, 7, 1, 4), ('s', 1, 2, 1, 2), ('s', 1, 11, 0, 5), ('s', 6, 5, 1, 1), ('a', 7, 0), ('a', 5, 0), ('a', 2, 0), ('s', 5, 4, 0, 3), ('s', 1, 11, 1, 5), ('a', 5, 1), ('s', 7, 8, 0, 0)), (5, None, None, None), (None, None, None), (6, 5, 1, 6, 5, 12))),
+    (((('a', 6, 0), ('s', 2, 3, 0, 2), ('s', 6, 5, 0, 1), ('s', 7, 9, 1, 4), ('a', 8, 0)), (None, None, None, None), (None, None, None), (1, 7, 15, 1, 2, 8)),
+     ((('t', 1), ('a', 7, 1), ('a', 2, 1)), (None, None, None, None), (None, None, None), (6, 5, 13, 0, 1, 7))),
+    (((), (8, 11, None, None), (None, None, None), (7, 8, 11, 11, 8, 15)),
+     ((), (None, None, None, None), (None, None, None), (5, 6, 7, 5, 6, 2))),
+    (((('a', 6, 1), ('s', 6, 5, 1, 1), ('s', 8, 10, 1, 4), ('t', 2)), (None, None, None, None), (None, None, None), (2, 7, 6, 8, 11, 6)),
+     ((('s', 5, 4, 1, 3), ('a', 11, 0), ('s', 7, 8, 1, 0), ('s', 2, 3, 0, 2), ('s', 11, 9, 0, 5), ('t', 4)), (7, 2, None, None), (None, None, None), (7, 2, 12, 0, 1, 16))),
+    (((('t', 0),), (6, None, None, None), (None, None, None), (8, 11, 14, 1, 6, 12)),
+     ((('a', 11, 1),), (None, None, None, None), (None, None, None), (0, 5, 11, 6, 7, 11))),
+    (((('a', 3, 0), ('a', 9, 0), ('a', 5, 0), ('a', 9, 1)), (None, None, None, None), (None, None, None), (7, 8, 12, 2, 6, 9)),
+     ((('a', 8, 0), ('a', 4, 0)), (11, None, None, None), (None, None, None), (7, 11, 2, 7, 11, 13))),
+    (((('t', 5),), (9, None, None, None), (None, None, None), (11, 9, 12, 1, 7, 17)),
+     ((('s', 8, 10, 0, 4), ('s', 11, 9, 1, 5), ('a', 4, 1), ('t', 3)), (4, None, None, None), (None, None, None), (7, 11, 15, 11, 4, 16))),
+    (((('s', 9, 10, 0, 0), ('s', 2, 3, 1, 2), ('s', 5, 4, 0, 3), ('a', 5, 1)), (None, None, None, None), (None, None, None), (0, 2, 5, 8, 9, 5)),
+     ((('a', 8, 1), ('a', 9, 0), ('a', 3, 0)), (8, None, None, None), (None, None, None), (4, 8, 13, 5, 11, 8))),
+    (((), (5, None, None, None), (None, None, None), (9, 5, 15, 11, 0, 5)),
+     ((('s', 2, 3, 1, 2), ('s', 8, 10, 1, 4)), (None, None, None, None), (None, None, None), (7, 8, 4, 11, 8, 12))),
+    (((('s', 5, 4, 1, 3), ('t', 1), ('t', 4)), (None, None, None, None), (None, None, None), (7, 9, 13, 1, 5, 16)),
+     ((('a', 9, 1),), (None, None, None, None), (11, 12, None), (2, 4, 9, 5, 6, 9))),
+    (((('a', 3, 1),), (3, None, None, None), (None, None, None), (0, 6, 3, 3, 0, 15)),
+     ((('a', 10, 0),), (None, None, None, None), (None, None, None), (0, 2, 8, 4, 8, 13))),
+    (((('a', 10, 1), ('a', 4, 0), ('a', 10, 0)), (10, None, None, None), (6, 15, None), (9, 10, 14, 10, 0, 12)),
+     ((), (9, None, None, None), (2, None, None), (8, 9, 15, 9, 0, 13))),
+    (((), (None, None, None, None), (14, 12, None), (5, 3, 17, 7, 8, 3)),
+     ((('t', 2),), (None, None, None, None), (13, None, None), (1, 7, 14, 9, 0, 14))),
+    (((), (None, None, None, None), (5, 17, None), (11, 3, 13, 9, 10, 3)),
+     ((('a', 10, 1),), (None, None, None, None), (14, None, None), (0, 4, 10, 5, 0, 10))),
+    (((('a', 4, 1),), (None, None, None, None), (None, None, None), (1, 2, 10, 11, 3, 16)),
+     ((('a', 3, 1), ('t', 5)), (3, None, None, None), (5, None, None), (0, 3, 17, 1, 4, 3))),
+    (((), (None, None, None, None), (1, 2, 11), (10, 0, 13, 3, 7, 4)),
+     ((), (10, None, None, None), (0, 17, 1), (6, 7, 3, 10, 3, 15))),
+    (((), (4, None, None, None), (10, 13, 3), (4, 0, 16, 8, 9, 4)),
+     ((), (None, None, None, None), (4, 6, 7), (9, 3, 16, 8, 9, 3))),
 )
 
 TAIL = (
-    (13, 3, 7, 0, 16, 8, 9, 4),
-    (6, 7, 10, 15, 16, 8, 9, 3),
+    (7, 0, 16, 8, 9, 4),
+    (10, 15, 16, 8, 9, 3),
 )
 
 SLOTS = len(OFFSETS[0])
@@ -84,7 +84,7 @@
 
 def words(values, bits=5):
     each = 30 // bits
-    return [sum(v << (bits * k) for k, v in enumerate(values[s:s + each])) for s in range(0, len(values), each)]
+    return [sum(v * (1 << bits * k) for k, v in enumerate(values[s:s + each])) for s in range(0, len(values), each)]
 
 
 def lookup(packed, n, bits=5):
@@ -96,7 +96,8 @@
 
 
 def of_core(core, lists, bits=5):
-    return [jnp.where(core == 0, jnp.int32(a), jnp.int32(b)) for a, b in zip(*(words(v, bits) for v in lists))]
+    return [jnp.where(core == 0, jnp.asarray(a, jnp.int32), jnp.asarray(b, jnp.int32))
+            for a, b in zip(*(words(v, bits) for v in lists))]
 
 
 def column(which, place, k):
@@ -166,6 +167,12 @@
             if h == 0:
                 share_label(slot, k).start()
             share(slot, k, h).start()
+
+    homes = []
+    for which in (0, 1):
+        offsets = OFFSETS[which] + tuple(OFFSETS[1 - which][k] for k in SHARED[which])
+        homes.append([at([SIDE - k for k in o], which if n < SLOTS else 1 - which) for n, o in enumerate(offsets)])
+    home_x, home_mem = (of_core(core, [[h[k] for h in held] for held in homes]) for k in (0, 1))
 
     load_ids.wait()
     labels[0] = ids[...].astype(jnp.float32)
@@ -223,12 +230,10 @@
             row_best[a] = tops[n]
 
     def answer(slot):
-        offsets = [OFFSETS[w] + tuple(OFFSETS[1 - w][k] for k in SHARED[w]) for w in (0, 1)]
-        back = [SIDE - lookup(of_core(core, [[o[k] for o in held] for held in offsets], 2), slot, 2) for k in range(3)]
         return pltpu.make_async_remote_copy(
             src_ref=outgoing.at[slot], dst_ref=incoming.at[slot],
             send_sem=result_send.at[slot], recv_sem=result_recv,
-            device_id=at(back, jnp.where(slot < SLOTS, core, other)), device_id_type=MESH)
+            device_id=(lookup(home_x, slot), lookup(home_mem, slot)), device_id_type=MESH)
 
     def finish(slot):
         by_column = jnp.max(column_best[slot], axis=0, keepdims=True)
@@ -244,10 +249,6 @@
         @pl.when(slot > 0)
         def _():
             answer(slot).start()
-
-        @pl.when(slot == 0)
-        def _():
-            incoming[0] = outgoing[0]
 
     def arrived(which, slot, h):
         pltpu.make_async_copy(chunk_of(slot, h), chunk_of(slot, h), recv_sem.at[slot, h]).wait()
@@ -309,16 +310,17 @@
     lax.fori_loop(0, len(STEPS), step, 0)
     left = max(len(t) for t in TAIL)
     ends = of_core(core, [(list(t) + [NONE] * left)[:left] for t in TAIL])
-
-    def last(n, carry):
-        ended = lookup(ends, n)
-
-        @pl.when(ended != NONE)
-        def _():
-            finish(ended)
-        return carry
-
-    lax.fori_loop(0, left, last, 0)
+    ended = [lookup(ends, n) for n in range(left)]
+    for slot in ended:
+        held = jnp.where(slot == NONE, 0, slot)
+        by_row = jnp.max(row_best[jnp.minimum(held, SLOTS - 1)].T, axis=0, keepdims=True)
+        by_column = jnp.max(column_best[held], axis=0, keepdims=True)
+        outgoing[held] = jnp.where(held < SLOTS, jnp.maximum(by_row, by_column), by_column)
+    for slot in ended:
+        @pl.when((slot != NONE) & (slot > 0))
+        def _(slot=slot):
+            answer(slot).start()
+    incoming[0] = outgoing[0]
 
     for which in (0, 1):
         @pl.when(core == which)

time: 50.4 us -> 50.2 us (level)
  no operation moved by 1% of the time
where the time goes in v10:
time: 50.2 us; the launch traced here: 50.1 us
  Pallas kernels  48.8 us (97%)
  local copies, waits for them, and re-layouts  1.24 us (2%)
    pallas_call x1, Pallas kernels, body(): pl.pallas_call(functools.partial(kernel, chunks), out_shape=jax.ShapeDtyp...  48.8 us
    unnamed x1, local copies, waits for them, and re-layouts  1.24 us

profile of v10, /device:TPU:1, one launch (start us, length us, event | category | flops | bytes accessed | tf_op | source)
XLA Modules:
  0.0 50.1 jit_solution(12787444008928083116)
XLA Ops:
  0.0 48.8 %shard_map.28 = f32[256]{0:T(256)} custom-call(f32[256,768]{1,0:T(8,128)} %emb_ref.1, s32[1,256]{1,0:T(1,128)} %bitcast.1), custom_call_target="tpu_custom_call" | custom-call | tf_op jit(solution)/shard_map/pallas_call | solution.py:347
  48.9 1.2 %copy.4 = f32[256]{0:T(256)} copy(f32[256]{0:T(256)} %shard_map.28) | data formatting | bytes 2048

commit v11 on v10

--- a/solution.py
+++ b/solution.py
@@ -14,66 +14,66 @@
 DIRS = ((1, 0, 0), (3, 0, 0), (0, 1, 0), (0, 3, 0), (0, 0, 1), (0, 0, 3))
 
 OFFSETS = (
-    ((0, 0, 0), (3, 0, 0), (0, 1, 0), (0, 2, 0), (2, 2, 0), (2, 3, 0),
-     (3, 3, 0), (0, 0, 1), (1, 0, 1), (0, 0, 2), (1, 0, 2), (0, 0, 3)),
-    ((0, 0, 0), (1, 0, 0), (1, 1, 0), (1, 2, 0), (3, 2, 0), (3, 3, 0),
-     (0, 3, 0), (1, 0, 1), (2, 0, 1), (1, 0, 2), (2, 0, 2), (1, 0, 3)),
-)
-
-SHARED = ((2, 4, 5, 6, 8, 11), (0, 2, 3, 6, 8, 10))
+    ((0, 0, 0), (0, 1, 0), (2, 1, 0), (3, 1, 0), (1, 3, 0), (2, 3, 0),
+     (1, 0, 0), (0, 1, 1), (0, 1, 2), (0, 2, 2), (0, 1, 3), (0, 2, 3)),
+    ((0, 0, 0), (2, 0, 0), (3, 0, 0), (1, 2, 0), (2, 2, 0), (0, 3, 0),
+     (1, 3, 0), (0, 0, 1), (0, 0, 2), (0, 1, 2), (0, 0, 3), (0, 1, 3)),
+)
+
+SHARED = ((0, 2, 6, 7, 9, 11), (3, 5, 6, 7, 8, 11))
 
 FIRST_SENDS = (
-    ((0, 1, 0, 1), (0, 2, 0, 2), (0, 7, 1, 4), (0, 11, 0, 5)),
-    ((0, 1, 0, 0), (0, 6, 0, 3)),
+    ((0, 1, 0, 2), (0, 6, 0, 0)),
+    ((0, 5, 0, 3), (0, 10, 0, 5), (0, 7, 1, 4), (0, 2, 0, 1)),
 )
 
 LAST_SENDS = (
-    ((1, 0), (1, 1), (2, 0), (2, 1), (3, 0), (3, 1), (4, 0), (4, 1), (5, 0), (5, 1), (6, 0), (6, 1), (7, 0), (7, 1), (8, 0), (8, 1), (9, 0), (9, 1), (10, 0), (10, 1), (11, 0), (11, 1)),
-    ((1, 0), (1, 1), (2, 0), (2, 1), (3, 0), (3, 1), (4, 0), (4, 1), (5, 0), (5, 1), (6, 0), (6, 1), (7, 0), (7, 1), (8, 0), (8, 1), (9, 0), (9, 1), (10, 0), (10, 1), (11, 0), (11, 1)),
+    ((2, 3), (4, 3), (5, 3), (8, 3), (9, 2), (9, 3)),
+    ((1, 3), (3, 3), (4, 3), (8, 2), (9, 2), (9, 3)),
 )
 
 STEPS = (
-    (((('s', 0, 7, 0, 4), ('s', 0, 2, 1, 2), ('s', 0, 1, 1, 1), ('s', 0, 11, 1, 5), ('a', 2, 0), ('a', 7, 1), ('a', 11, 0), ('s', 11, 9, 0, 5), ('a', 1, 0), ('s', 1, 6, 0, 3), ('s', 7, 8, 1, 0), ('a', 2, 1), ('a', 7, 0), ('a', 1, 1)), (2, 7, None, None), (None, None, None), (2, 7, 0, 0, 7, 1)),
-     ((('s', 0, 6, 1, 3), ('s', 0, 1, 1, 0), ('a', 6, 0), ('a', 1, 0), ('s', 6, 5, 0, 1), ('s', 1, 2, 0, 2), ('s', 1, 7, 0, 4), ('t', 0), ('a', 1, 1), ('a', 6, 1)), (1, 6, None, None), (None, None, None), (0, 1, 12, 1, 6, 0))),
-    (((('a', 11, 1), ('s', 7, 8, 0, 0), ('s', 1, 6, 1, 3), ('t', 3), ('a', 8, 1)), (1, None, None, None), (None, None, None), (7, 1, 2, 1, 2, 11)),
-     ((('s', 1, 7, 1, 4), ('s', 1, 2, 1, 2), ('s', 1, 11, 0, 5), ('s', 6, 5, 1, 1), ('a', 7, 0), ('a', 5, 0), ('a', 2, 0), ('s', 5, 4, 0, 3), ('s', 1, 11, 1, 5), ('a', 5, 1), ('s', 7, 8, 0, 0)), (5, None, None, None), (None, None, None), (6, 5, 1, 6, 5, 12))),
-    (((('a', 6, 0), ('s', 2, 3, 0, 2), ('s', 6, 5, 0, 1), ('s', 7, 9, 1, 4), ('a', 8, 0)), (None, None, None, None), (None, None, None), (1, 7, 15, 1, 2, 8)),
-     ((('t', 1), ('a', 7, 1), ('a', 2, 1)), (None, None, None, None), (None, None, None), (6, 5, 13, 0, 1, 7))),
-    (((), (8, 11, None, None), (None, None, None), (7, 8, 11, 11, 8, 15)),
-     ((), (None, None, None, None), (None, None, None), (5, 6, 7, 5, 6, 2))),
-    (((('a', 6, 1), ('s', 6, 5, 1, 1), ('s', 8, 10, 1, 4), ('t', 2)), (None, None, None, None), (None, None, None), (2, 7, 6, 8, 11, 6)),
-     ((('s', 5, 4, 1, 3), ('a', 11, 0), ('s', 7, 8, 1, 0), ('s', 2, 3, 0, 2), ('s', 11, 9, 0, 5), ('t', 4)), (7, 2, None, None), (None, None, None), (7, 2, 12, 0, 1, 16))),
-    (((('t', 0),), (6, None, None, None), (None, None, None), (8, 11, 14, 1, 6, 12)),
-     ((('a', 11, 1),), (None, None, None, None), (None, None, None), (0, 5, 11, 6, 7, 11))),
-    (((('a', 3, 0), ('a', 9, 0), ('a', 5, 0), ('a', 9, 1)), (None, None, None, None), (None, None, None), (7, 8, 12, 2, 6, 9)),
-     ((('a', 8, 0), ('a', 4, 0)), (11, None, None, None), (None, None, None), (7, 11, 2, 7, 11, 13))),
-    (((('t', 5),), (9, None, None, None), (None, None, None), (11, 9, 12, 1, 7, 17)),
-     ((('s', 8, 10, 0, 4), ('s', 11, 9, 1, 5), ('a', 4, 1), ('t', 3)), (4, None, None, None), (None, None, None), (7, 11, 15, 11, 4, 16))),
-    (((('s', 9, 10, 0, 0), ('s', 2, 3, 1, 2), ('s', 5, 4, 0, 3), ('a', 5, 1)), (None, None, None, None), (None, None, None), (0, 2, 5, 8, 9, 5)),
-     ((('a', 8, 1), ('a', 9, 0), ('a', 3, 0)), (8, None, None, None), (None, None, None), (4, 8, 13, 5, 11, 8))),
-    (((), (5, None, None, None), (None, None, None), (9, 5, 15, 11, 0, 5)),
-     ((('s', 2, 3, 1, 2), ('s', 8, 10, 1, 4)), (None, None, None, None), (None, None, None), (7, 8, 4, 11, 8, 12))),
-    (((('s', 5, 4, 1, 3), ('t', 1), ('t', 4)), (None, None, None, None), (None, None, None), (7, 9, 13, 1, 5, 16)),
-     ((('a', 9, 1),), (None, None, None, None), (11, 12, None), (2, 4, 9, 5, 6, 9))),
-    (((('a', 3, 1),), (3, None, None, None), (None, None, None), (0, 6, 3, 3, 0, 15)),
-     ((('a', 10, 0),), (None, None, None, None), (None, None, None), (0, 2, 8, 4, 8, 13))),
-    (((('a', 10, 1), ('a', 4, 0), ('a', 10, 0)), (10, None, None, None), (6, 15, None), (9, 10, 14, 10, 0, 12)),
-     ((), (9, None, None, None), (2, None, None), (8, 9, 15, 9, 0, 13))),
-    (((), (None, None, None, None), (14, 12, None), (5, 3, 17, 7, 8, 3)),
-     ((('t', 2),), (None, None, None, None), (13, None, None), (1, 7, 14, 9, 0, 14))),
-    (((), (None, None, None, None), (5, 17, None), (11, 3, 13, 9, 10, 3)),
-     ((('a', 10, 1),), (None, None, None, None), (14, None, None), (0, 4, 10, 5, 0, 10))),
-    (((('a', 4, 1),), (None, None, None, None), (None, None, None), (1, 2, 10, 11, 3, 16)),
-     ((('a', 3, 1), ('t', 5)), (3, None, None, None), (5, None, None), (0, 3, 17, 1, 4, 3))),
-    (((), (None, None, None, None), (1, 2, 11), (10, 0, 13, 3, 7, 4)),
-     ((), (10, None, None, None), (0, 17, 1), (6, 7, 3, 10, 3, 15))),
-    (((), (4, None, None, None), (10, 13, 3), (4, 0, 16, 8, 9, 4)),
-     ((), (None, None, None, None), (4, 6, 7), (9, 3, 16, 8, 9, 3))),
+    (((('s', 0, 1, 1, 2, 1, 0), ('s', 0, 6, 1, 0, 6, 0), ('a', 1, 0), ('a', 6, 0), ('s', 1, 10, 0, 5), ('s', 1, 3, 0, 1), ('s', 6, 4, 0, 3), ('s', 1, 7, 0, 4), ('s', 0, 1, 2, 2, 1, 1), ('s', 0, 6, 2, 0, 6, 1), ('a', 1, 1), ('a', 6, 1), ('s', 1, 10, 1, 5, 10, 0), ('s', 1, 3, 1, 1, 3, 0), ('s', 6, 4, 1, 3, 4, 0), ('s', 1, 7, 1, 4, 7, 0), ('s', 0, 1, 3, 2, 1, 2), ('s', 0, 6, 3, 0, 6, 2), ('a', 3, 0), ('a', 4, 0), ('a', 7, 0), ('a', 10, 0), ('a', 1, 2), ('a', 6, 2), ('s', 1, 10, 2, 5, 10, 1), ('s', 1, 3, 2, 1, 3, 1), ('s', 6, 4, 2, 3, 4, 1), ('s', 1, 7, 2, 4, 7, 1), ('s', 4, 5, 0, 0, 6, 3), ('s', 10, 11, 0, 2, 1, 3), ('a', 3, 1), ('a', 4, 1), ('a', 7, 1), ('a', 10, 1), ('a', 1, 3), ('a', 6, 3), ('t', 0)), (1, 6, None, None), (None, None, None), (0, 1, 12, 1, 6, 0)),
+     ((('s', 0, 5, 1, 3, 5, 0), ('s', 0, 10, 2, 5, 10, 0), ('s', 0, 7, 3, 4, 7, 1), ('s', 0, 2, 1, 1, 2, 0), ('a', 2, 0), ('a', 5, 0), ('a', 7, 1), ('a', 10, 0), ('s', 5, 6, 0, 0), ('s', 10, 11, 0, 2), ('s', 0, 5, 2, 3, 5, 1), ('s', 0, 7, 0, 4, 7, 3), ('s', 0, 10, 1, 5, 10, 2), ('s', 0, 2, 2, 1, 2, 1), ('a', 2, 1), ('a', 5, 1), ('a', 7, 3), ('a', 10, 2), ('s', 5, 6, 1, 0, 6, 0), ('s', 10, 11, 2, 2, 11, 0), ('s', 0, 5, 3, 3, 5, 2), ('s', 7, 8, 1, 4, 7, 0), ('s', 0, 2, 3, 1, 2, 2), ('s', 0, 10, 3, 5, 10, 1), ('a', 6, 0), ('a', 11, 0), ('a', 2, 2), ('a', 5, 2), ('a', 7, 0), ('a', 10, 1), ('s', 5, 6, 2, 0, 6, 1), ('s', 10, 11, 1, 2, 11, 2), ('s', 6, 3, 0, 3, 5, 3), ('s', 0, 7, 2, 4, 8, 1), ('s', 2, 1, 0, 1, 2, 3), ('s', 11, 9, 0, 5, 10, 3), ('a', 6, 1), ('a', 11, 2), ('a', 2, 3), ('a', 5, 3), ('a', 8, 1), ('a', 10, 3)), (5, 2, None, None), (None, None, None), (0, 5, 10, 2, 5, 0))),
+    (((('s', 1, 10, 3, 5, 10, 2), ('s', 1, 3, 3, 1, 3, 2), ('s', 6, 4, 3, 3, 4, 2), ('s', 1, 7, 3, 4, 7, 2), ('s', 10, 11, 1, 2, 11, 0), ('s', 4, 5, 1, 0, 5, 0), ('a', 3, 2), ('a', 4, 2), ('a', 7, 2), ('a', 10, 2), ('a', 5, 0), ('a', 11, 0), ('s', 10, 8, 0, 5, 10, 3), ('s', 3, 2, 0, 1, 3, 3), ('s', 7, 8, 1, 4, 7, 3), ('s', 4, 5, 2, 0, 5, 1), ('s', 10, 11, 2, 2, 11, 1), ('a', 3, 3), ('a', 4, 3), ('a', 7, 3), ('a', 10, 3), ('t', 3)), (None, None, None, None), (None, None, None), (0, 1, 15, 0, 1, 7)),
+     ((('s', 5, 6, 3, 0, 6, 2), ('s', 8, 9, 1, 2, 11, 1), ('t', 2)), (10, None, None, None), (None, None, None), (2, 5, 14, 5, 10, 2))),
+    (((('a', 5, 1), ('a', 11, 1)), (3, 4, None, None), (None, None, None), (0, 3, 10, 3, 4, 7)),
+     ((('s', 6, 3, 1, 3, 3, 0), ('s', 7, 8, 3, 4, 7, 2), ('s', 2, 1, 1, 1, 1, 0), ('s', 11, 9, 2, 5, 9, 0), ('a', 6, 2), ('a', 11, 1), ('a', 1, 0), ('a', 3, 0), ('a', 7, 2), ('a', 9, 0)), (7, None, None, None), (None, None, None), (2, 5, 7, 10, 7, 14))),
+    (((('s', 10, 8, 2, 5, 8, 0), ('s', 3, 2, 1, 1, 2, 0), ('s', 7, 8, 3, 4, 8, 1)), (None, None, None, None), (None, None, None), (3, 4, 15, 4, 6, 3)),
+     ((('s', 3, 4, 0, 0, 6, 3), ('s', 10, 11, 3, 2, 9, 1), ('s', 6, 3, 2, 3, 3, 1), ('s', 7, 8, 0, 4, 8, 3), ('s', 2, 1, 2, 1, 1, 1), ('a', 6, 3), ('a', 9, 1)), (6, None, None, None), (None, None, None), (2, 10, 6, 10, 6, 7))),
+    (((('s', 10, 11, 3, 2, 11, 2), ('s', 4, 5, 3, 0, 5, 2)), (7, None, None, None), (None, None, None), (4, 7, 10, 4, 7, 12)),
+     ((('t', 3), ('t', 0)), (None, None, None, None), (None, None, None), (2, 5, 15, 5, 6, 12))),
+    (((('a', 8, 0), ('t', 1)), (10, None, None, None), (None, None, None), (4, 10, 13, 6, 3, 12)),
+     ((('a', 3, 1), ('a', 1, 1), ('a', 8, 3), ('a', 9, 2), ('s', 3, 4, 1, 0, 4, 0), ('s', 8, 9, 3, 2, 11, 3), ('s', 6, 3, 3, 3, 3, 2), ('s', 7, 8, 2, 4, 8, 0), ('s', 2, 1, 3, 1, 1, 2), ('a', 4, 0), ('a', 11, 3)), (None, None, None, None), (None, None, None), (2, 5, 11, 6, 7, 11))),
+    (((('a', 2, 0), ('a', 8, 1), ('a', 5, 2), ('a', 11, 2), ('s', 11, 9, 1, 5, 8, 2)), (None, None, None, None), (None, None, None), (6, 4, 1, 7, 10, 6)),
+     ((('a', 3, 2),), (11, None, None, None), (None, None, None), (6, 11, 15, 10, 11, 12))),
+    (((('s', 3, 2, 2, 1, 2, 1), ('s', 8, 9, 0, 2, 11, 3), ('a', 8, 2), ('a', 2, 1), ('a', 8, 3), ('t', 5)), (None, None, None, None), (None, None, None), (0, 1, 17, 0, 3, 8)),
+     ((('a', 1, 2), ('a', 8, 0), ('s', 3, 4, 2, 0, 4, 1), ('a', 3, 3)), (None, None, None, None), (None, None, None), (0, 2, 3, 7, 11, 3))),
+    (((('a', 5, 3), ('a', 11, 3), ('s', 11, 9, 3, 5, 9, 1), ('s', 8, 9, 2, 2, 9, 0), ('t', 2)), (8, None, None, None), (None, None, None), (4, 6, 8, 10, 8, 14)),
+     ((('a', 4, 1), ('s', 3, 4, 3, 0, 4, 2), ('a', 9, 3), ('a', 8, 2)), (3, None, None, None), (7, None, None), (11, 3, 14, 2, 5, 9))),
+    (((('s', 3, 2, 3, 1, 2, 2), ('a', 9, 1)), (5, None, None, None), (None, None, None), (0, 3, 11, 4, 5, 11)),
+     ((('a', 1, 3), ('t', 4)), (None, None, None, None), (None, None, None), (2, 5, 9, 3, 5, 16))),
+    (((('a', 9, 0),), (None, None, None, None), (None, None, None), (4, 5, 17, 7, 8, 5)),
+     ((('a', 4, 2), ('t', 5), ('t', 1)), (9, None, None, None), (None, None, None), (3, 5, 17, 9, 10, 13))),
+    (((('a', 2, 2),), (None, None, None, None), (None, None, None), (8, 5, 13, 10, 5, 15)),
+     ((), (8, None, None, None), (5, None, None), (9, 8, 6, 9, 8, 12))),
+    (((('a', 9, 3), ('a', 9, 2), ('t', 4)), (11, None, None, None), (10, None, None), (11, 0, 13, 0, 4, 16)),
+     ((('a', 4, 3),), (None, None, None, None), (12, None, None), (9, 8, 14, 0, 6, 1))),
+    (((('a', 2, 3),), (None, None, None, None), (13, 4, None), (0, 3, 9, 1, 6, 2)),
+     ((), (1, None, None, None), (6, None, None), (1, 0, 14, 1, 0, 16))),
+    (((), (2, None, None, None), (3, 1, 6), (2, 0, 15, 2, 0, 16)),
+     ((), (None, None, None, None), (14, 16, None), (2, 1, 8, 3, 1, 15))),
+    (((), (None, None, None, None), (15, 16, None), (2, 0, 17, 7, 8, 2)),
+     ((), (None, None, None, None), (2, 3, 15), (8, 1, 13, 9, 10, 1))),
+    (((), (9, None, None, None), (17, 7, 8), (9, 2, 5, 11, 0, 2)),
+     ((), (4, None, None, None), (13, 9, None), (1, 4, 17, 8, 10, 4))),
+    (((), (None, None, None, None), (9, 5, 0), (11, 2, 12, 11, 2, 14)),
+     ((), (None, None, None, None), (17, 8, 10), (11, 0, 4, 11, 4, 1))),
 )
 
 TAIL = (
-    (7, 0, 16, 8, 9, 4),
-    (10, 15, 16, 8, 9, 3),
+    (12, 11, 2, 14),
+    (0, 11, 4, 1),
 )
 
 SLOTS = len(OFFSETS[0])

time: 50.2 us -> 51.1 us (1.018)
  Pallas kernels: 48.8 us -> 49.6 us
    pallas_call x1, Pallas kernels: 48.8 us -> 49.6 us  [body(): pl.pallas_call(functools.partial(kernel, chunks), out_shape=jax.ShapeDtyp...]
where the time goes in v11:
time: 51.1 us; the launch traced here: 50.8 us
  Pallas kernels  49.6 us (97%)
  local copies, waits for them, and re-layouts  1.24 us (2%)
    pallas_call x1, Pallas kernels, body(): pl.pallas_call(functools.partial(kernel, chunks), out_shape=jax.ShapeDtyp...  49.6 us
    unnamed x1, local copies, waits for them, and re-layouts  1.24 us

profile of v11, /device:TPU:1, one launch (start us, length us, event | category | flops | bytes accessed | tf_op | source)
XLA Modules:
  0.0 50.8 jit_solution(13676993166692676038)
XLA Ops:
  0.0 49.6 %shard_map.28 = f32[256]{0:T(256)} custom-call(f32[256,768]{1,0:T(8,128)} %emb_ref.1, s32[1,256]{1,0:T(1,128)} %bitcast.1), custom_call_target="tpu_custom_call" | custom-call | tf_op jit(solution)/shard_map/pallas_call | solution.py:347
  49.6 1.2 %copy.4 = f32[256]{0:T(256)} copy(f32[256]{0:T(256)} %shard_map.28) | data formatting | bytes 2048

commit v12 on v11

--- a/solution.py
+++ b/solution.py
@@ -14,66 +14,66 @@
 DIRS = ((1, 0, 0), (3, 0, 0), (0, 1, 0), (0, 3, 0), (0, 0, 1), (0, 0, 3))
 
 OFFSETS = (
-    ((0, 0, 0), (0, 1, 0), (2, 1, 0), (3, 1, 0), (1, 3, 0), (2, 3, 0),
-     (1, 0, 0), (0, 1, 1), (0, 1, 2), (0, 2, 2), (0, 1, 3), (0, 2, 3)),
-    ((0, 0, 0), (2, 0, 0), (3, 0, 0), (1, 2, 0), (2, 2, 0), (0, 3, 0),
-     (1, 3, 0), (0, 0, 1), (0, 0, 2), (0, 1, 2), (0, 0, 3), (0, 1, 3)),
-)
-
-SHARED = ((0, 2, 6, 7, 9, 11), (3, 5, 6, 7, 8, 11))
+    ((0, 0, 0), (0, 0, 1), (1, 0, 1), (1, 0, 2), (2, 0, 2), (0, 1, 3),
+     (0, 2, 3), (2, 0, 0), (3, 0, 0), (0, 1, 0), (0, 2, 0), (0, 3, 0)),
+    ((0, 0, 0), (1, 0, 0), (1, 0, 1), (2, 0, 1), (0, 1, 2), (0, 2, 2),
+     (0, 0, 3), (2, 0, 3), (3, 0, 3), (0, 1, 3), (0, 2, 3), (0, 3, 3)),
+)
+
+SHARED = ((1, 2, 3, 4, 8, 11), (0, 2, 5, 6, 7, 8))
 
 FIRST_SENDS = (
-    ((0, 1, 0, 2), (0, 6, 0, 0)),
-    ((0, 5, 0, 3), (0, 10, 0, 5), (0, 7, 1, 4), (0, 2, 0, 1)),
+    ((0, 1, 0, 4), (0, 9, 0, 2), (0, 8, 0, 1), (0, 11, 0, 3)),
+    ((0, 6, 0, 5), (0, 1, 0, 0)),
 )
 
 LAST_SENDS = (
-    ((2, 3), (4, 3), (5, 3), (8, 3), (9, 2), (9, 3)),
-    ((1, 3), (3, 3), (4, 3), (8, 2), (9, 2), (9, 3)),
+    ((1, 1), (2, 1), (3, 1), (4, 0), (4, 1), (6, 0), (6, 1), (7, 1), (10, 0), (10, 1)),
+    ((1, 1), (2, 0), (2, 1), (3, 0), (3, 1), (5, 0), (5, 1), (6, 1), (7, 0), (7, 1), (8, 1), (10, 1)),
 )
 
 STEPS = (
-    (((('s', 0, 1, 1, 2, 1, 0), ('s', 0, 6, 1, 0, 6, 0), ('a', 1, 0), ('a', 6, 0), ('s', 1, 10, 0, 5), ('s', 1, 3, 0, 1), ('s', 6, 4, 0, 3), ('s', 1, 7, 0, 4), ('s', 0, 1, 2, 2, 1, 1), ('s', 0, 6, 2, 0, 6, 1), ('a', 1, 1), ('a', 6, 1), ('s', 1, 10, 1, 5, 10, 0), ('s', 1, 3, 1, 1, 3, 0), ('s', 6, 4, 1, 3, 4, 0), ('s', 1, 7, 1, 4, 7, 0), ('s', 0, 1, 3, 2, 1, 2), ('s', 0, 6, 3, 0, 6, 2), ('a', 3, 0), ('a', 4, 0), ('a', 7, 0), ('a', 10, 0), ('a', 1, 2), ('a', 6, 2), ('s', 1, 10, 2, 5, 10, 1), ('s', 1, 3, 2, 1, 3, 1), ('s', 6, 4, 2, 3, 4, 1), ('s', 1, 7, 2, 4, 7, 1), ('s', 4, 5, 0, 0, 6, 3), ('s', 10, 11, 0, 2, 1, 3), ('a', 3, 1), ('a', 4, 1), ('a', 7, 1), ('a', 10, 1), ('a', 1, 3), ('a', 6, 3), ('t', 0)), (1, 6, None, None), (None, None, None), (0, 1, 12, 1, 6, 0)),
-     ((('s', 0, 5, 1, 3, 5, 0), ('s', 0, 10, 2, 5, 10, 0), ('s', 0, 7, 3, 4, 7, 1), ('s', 0, 2, 1, 1, 2, 0), ('a', 2, 0), ('a', 5, 0), ('a', 7, 1), ('a', 10, 0), ('s', 5, 6, 0, 0), ('s', 10, 11, 0, 2), ('s', 0, 5, 2, 3, 5, 1), ('s', 0, 7, 0, 4, 7, 3), ('s', 0, 10, 1, 5, 10, 2), ('s', 0, 2, 2, 1, 2, 1), ('a', 2, 1), ('a', 5, 1), ('a', 7, 3), ('a', 10, 2), ('s', 5, 6, 1, 0, 6, 0), ('s', 10, 11, 2, 2, 11, 0), ('s', 0, 5, 3, 3, 5, 2), ('s', 7, 8, 1, 4, 7, 0), ('s', 0, 2, 3, 1, 2, 2), ('s', 0, 10, 3, 5, 10, 1), ('a', 6, 0), ('a', 11, 0), ('a', 2, 2), ('a', 5, 2), ('a', 7, 0), ('a', 10, 1), ('s', 5, 6, 2, 0, 6, 1), ('s', 10, 11, 1, 2, 11, 2), ('s', 6, 3, 0, 3, 5, 3), ('s', 0, 7, 2, 4, 8, 1), ('s', 2, 1, 0, 1, 2, 3), ('s', 11, 9, 0, 5, 10, 3), ('a', 6, 1), ('a', 11, 2), ('a', 2, 3), ('a', 5, 3), ('a', 8, 1), ('a', 10, 3)), (5, 2, None, None), (None, None, None), (0, 5, 10, 2, 5, 0))),
-    (((('s', 1, 10, 3, 5, 10, 2), ('s', 1, 3, 3, 1, 3, 2), ('s', 6, 4, 3, 3, 4, 2), ('s', 1, 7, 3, 4, 7, 2), ('s', 10, 11, 1, 2, 11, 0), ('s', 4, 5, 1, 0, 5, 0), ('a', 3, 2), ('a', 4, 2), ('a', 7, 2), ('a', 10, 2), ('a', 5, 0), ('a', 11, 0), ('s', 10, 8, 0, 5, 10, 3), ('s', 3, 2, 0, 1, 3, 3), ('s', 7, 8, 1, 4, 7, 3), ('s', 4, 5, 2, 0, 5, 1), ('s', 10, 11, 2, 2, 11, 1), ('a', 3, 3), ('a', 4, 3), ('a', 7, 3), ('a', 10, 3), ('t', 3)), (None, None, None, None), (None, None, None), (0, 1, 15, 0, 1, 7)),
-     ((('s', 5, 6, 3, 0, 6, 2), ('s', 8, 9, 1, 2, 11, 1), ('t', 2)), (10, None, None, None), (None, None, None), (2, 5, 14, 5, 10, 2))),
-    (((('a', 5, 1), ('a', 11, 1)), (3, 4, None, None), (None, None, None), (0, 3, 10, 3, 4, 7)),
-     ((('s', 6, 3, 1, 3, 3, 0), ('s', 7, 8, 3, 4, 7, 2), ('s', 2, 1, 1, 1, 1, 0), ('s', 11, 9, 2, 5, 9, 0), ('a', 6, 2), ('a', 11, 1), ('a', 1, 0), ('a', 3, 0), ('a', 7, 2), ('a', 9, 0)), (7, None, None, None), (None, None, None), (2, 5, 7, 10, 7, 14))),
-    (((('s', 10, 8, 2, 5, 8, 0), ('s', 3, 2, 1, 1, 2, 0), ('s', 7, 8, 3, 4, 8, 1)), (None, None, None, None), (None, None, None), (3, 4, 15, 4, 6, 3)),
-     ((('s', 3, 4, 0, 0, 6, 3), ('s', 10, 11, 3, 2, 9, 1), ('s', 6, 3, 2, 3, 3, 1), ('s', 7, 8, 0, 4, 8, 3), ('s', 2, 1, 2, 1, 1, 1), ('a', 6, 3), ('a', 9, 1)), (6, None, None, None), (None, None, None), (2, 10, 6, 10, 6, 7))),
-    (((('s', 10, 11, 3, 2, 11, 2), ('s', 4, 5, 3, 0, 5, 2)), (7, None, None, None), (None, None, None), (4, 7, 10, 4, 7, 12)),
-     ((('t', 3), ('t', 0)), (None, None, None, None), (None, None, None), (2, 5, 15, 5, 6, 12))),
-    (((('a', 8, 0), ('t', 1)), (10, None, None, None), (None, None, None), (4, 10, 13, 6, 3, 12)),
-     ((('a', 3, 1), ('a', 1, 1), ('a', 8, 3), ('a', 9, 2), ('s', 3, 4, 1, 0, 4, 0), ('s', 8, 9, 3, 2, 11, 3), ('s', 6, 3, 3, 3, 3, 2), ('s', 7, 8, 2, 4, 8, 0), ('s', 2, 1, 3, 1, 1, 2), ('a', 4, 0), ('a', 11, 3)), (None, None, None, None), (None, None, None), (2, 5, 11, 6, 7, 11))),
-    (((('a', 2, 0), ('a', 8, 1), ('a', 5, 2), ('a', 11, 2), ('s', 11, 9, 1, 5, 8, 2)), (None, None, None, None), (None, None, None), (6, 4, 1, 7, 10, 6)),
-     ((('a', 3, 2),), (11, None, None, None), (None, None, None), (6, 11, 15, 10, 11, 12))),
-    (((('s', 3, 2, 2, 1, 2, 1), ('s', 8, 9, 0, 2, 11, 3), ('a', 8, 2), ('a', 2, 1), ('a', 8, 3), ('t', 5)), (None, None, None, None), (None, None, None), (0, 1, 17, 0, 3, 8)),
-     ((('a', 1, 2), ('a', 8, 0), ('s', 3, 4, 2, 0, 4, 1), ('a', 3, 3)), (None, None, None, None), (None, None, None), (0, 2, 3, 7, 11, 3))),
-    (((('a', 5, 3), ('a', 11, 3), ('s', 11, 9, 3, 5, 9, 1), ('s', 8, 9, 2, 2, 9, 0), ('t', 2)), (8, None, None, None), (None, None, None), (4, 6, 8, 10, 8, 14)),
-     ((('a', 4, 1), ('s', 3, 4, 3, 0, 4, 2), ('a', 9, 3), ('a', 8, 2)), (3, None, None, None), (7, None, None), (11, 3, 14, 2, 5, 9))),
-    (((('s', 3, 2, 3, 1, 2, 2), ('a', 9, 1)), (5, None, None, None), (None, None, None), (0, 3, 11, 4, 5, 11)),
-     ((('a', 1, 3), ('t', 4)), (None, None, None, None), (None, None, None), (2, 5, 9, 3, 5, 16))),
-    (((('a', 9, 0),), (None, None, None, None), (None, None, None), (4, 5, 17, 7, 8, 5)),
-     ((('a', 4, 2), ('t', 5), ('t', 1)), (9, None, None, None), (None, None, None), (3, 5, 17, 9, 10, 13))),
-    (((('a', 2, 2),), (None, None, None, None), (None, None, None), (8, 5, 13, 10, 5, 15)),
-     ((), (8, None, None, None), (5, None, None), (9, 8, 6, 9, 8, 12))),
-    (((('a', 9, 3), ('a', 9, 2), ('t', 4)), (11, None, None, None), (10, None, None), (11, 0, 13, 0, 4, 16)),
-     ((('a', 4, 3),), (None, None, None, None), (12, None, None), (9, 8, 14, 0, 6, 1))),
-    (((('a', 2, 3),), (None, None, None, None), (13, 4, None), (0, 3, 9, 1, 6, 2)),
-     ((), (1, None, None, None), (6, None, None), (1, 0, 14, 1, 0, 16))),
-    (((), (2, None, None, None), (3, 1, 6), (2, 0, 15, 2, 0, 16)),
-     ((), (None, None, None, None), (14, 16, None), (2, 1, 8, 3, 1, 15))),
-    (((), (None, None, None, None), (15, 16, None), (2, 0, 17, 7, 8, 2)),
-     ((), (None, None, None, None), (2, 3, 15), (8, 1, 13, 9, 10, 1))),
-    (((), (9, None, None, None), (17, 7, 8), (9, 2, 5, 11, 0, 2)),
-     ((), (4, None, None, None), (13, 9, None), (1, 4, 17, 8, 10, 4))),
-    (((), (None, None, None, None), (9, 5, 0), (11, 2, 12, 11, 2, 14)),
-     ((), (None, None, None, None), (17, 8, 10), (11, 0, 4, 11, 4, 1))),
+    (((('s', 0, 8, 1, 1, 8, 0), ('s', 0, 9, 1, 2), ('s', 0, 11, 1, 3, 11, 0), ('s', 0, 1, 1, 4, 9, 0), ('a', 1, 0), ('a', 8, 0), ('a', 11, 0), ('a', 9, 0), ('s', 9, 5, 0, 5, 1, 0), ('s', 1, 2, 0, 0), ('s', 8, 7, 0, 1, 8, 1), ('s', 11, 10, 0, 3, 9, 1), ('a', 1, 1), ('t', 0), ('a', 11, 1), ('a', 9, 1), ('a', 8, 1), ('s', 1, 2, 1, 0), ('s', 9, 5, 1, 5, 5, 0), ('s', 9, 10, 1, 2, 2, 0), ('a', 2, 0), ('s', 8, 7, 1, 1, 7, 0), ('s', 2, 3, 0, 4, 11, 1)), (8, 9, 11, None), (None, None, None), (8, 9, 1, 9, 11, 12)),
+     ((('t', 0), ('s', 0, 6, 1, 5, 6, 0), ('s', 0, 1, 1, 0), ('a', 6, 0), ('a', 1, 0), ('s', 6, 11, 0, 3), ('s', 6, 9, 0, 2), ('s', 6, 8, 0, 1), ('s', 1, 2, 0, 4), ('a', 1, 1), ('a', 6, 1)), (1, 6, None, None), (None, None, None), (0, 1, 12, 1, 6, 0))),
+    (((('a', 7, 0), ('a', 5, 0), ('s', 5, 6, 0, 2), ('a', 10, 0)), (1, None, None, None), (None, None, None), (1, 8, 11, 1, 8, 12)),
+     ((('s', 1, 2, 1, 4), ('s', 6, 8, 1, 1, 1, 0), ('s', 6, 9, 1, 2, 9, 0), ('s', 6, 11, 1, 3, 11, 0), ('a', 8, 0), ('a', 2, 0), ('a', 9, 0), ('s', 2, 3, 0, 0), ('a', 11, 0), ('s', 9, 4, 0, 5), ('s', 11, 10, 0, 3, 11, 1), ('a', 2, 1), ('a', 9, 1)), (2, None, None, None), (None, None, None), (1, 2, 6, 6, 2, 12))),
+    (((('t', 1),), (None, None, None, None), (None, None, None), (0, 8, 9, 1, 8, 0)),
+     ((('s', 2, 3, 1, 0, 8, 0), ('s', 8, 7, 0, 1), ('s', 9, 4, 1, 5), ('a', 11, 1)), (None, None, None, None), (None, None, None), (0, 1, 9, 2, 6, 9))),
+    (((('a', 10, 1),), (None, None, None, None), (None, None, None), (9, 11, 13, 1, 8, 10)),
+     ((('a', 8, 1), ('t', 5)), (9, 11, None, None), (None, None, None), (2, 9, 11, 9, 11, 12))),
+    (((('a', 2, 1), ('s', 2, 3, 1, 4, 3, 0), ('a', 5, 1)), (2, 10, None, None), (None, None, None), (1, 2, 5, 10, 11, 2)),
+     ((), (None, None, None, None), (None, None, None), (9, 11, 8, 0, 1, 11))),
+    (((('a', 3, 0), ('t', 5), ('s', 5, 6, 1, 2), ('s', 3, 4, 0, 0, 5, 1)), (None, None, None, None), (None, None, None), (11, 2, 9, 1, 2, 17)),
+     ((('a', 4, 0), ('a', 3, 0)), (None, None, None, None), (None, None, None), (1, 2, 8, 2, 9, 17))),
+    (((('a', 7, 1),), (5, None, None, None), (None, None, None), (5, 9, 17, 2, 5, 8)),
+     ((('t', 2), ('s', 11, 10, 1, 3, 4, 0), ('t', 1)), (None, None, None, None), (None, None, None), (0, 6, 14, 6, 9, 13))),
+    (((('a', 6, 0), ('t', 4)), (None, None, None, None), (None, None, None), (10, 5, 13, 0, 2, 7)),
+     ((('a', 10, 0), ('s', 10, 5, 0, 5, 9, 1), ('s', 8, 7, 1, 1, 10, 0), ('a', 3, 1), ('a', 4, 1)), (8, 3, 4, None), (None, None, None), (8, 3, 14, 8, 4, 12))),
+    (((), (None, None, None, None), (None, None, None), (0, 2, 7, 5, 9, 7)),
+     ((('s', 4, 5, 1, 2, 4, 1),), (None, None, None, None), (12, None, None), (8, 11, 4, 11, 4, 17))),
+    (((('a', 3, 1), ('s', 3, 4, 1, 0)), (None, None, None, None), (None, None, None), (10, 11, 16, 2, 9, 16)),
+     ((('t', 4),), (None, None, None, None), (None, None, None), (11, 4, 17, 4, 6, 16))),
+    (((('a', 6, 1),), (3, 7, None, None), (2, None, None), (3, 0, 12, 7, 3, 10)),
+     ((), (None, None, None, None), (11, None, None), (4, 9, 3, 0, 2, 4))),
+    (((), (6, None, None, None), (None, None, None), (7, 6, 13, 8, 0, 6)),
+     ((('a', 10, 1), ('a', 7, 0)), (10, None, None, None), (None, None, None), (4, 10, 13, 10, 0, 17))),
+    (((('t', 3), ('t', 2), ('a', 4, 0)), (None, None, None, None), (13, None, None), (7, 3, 17, 8, 11, 3)),
+     ((), (None, None, None, None), (17, None, None), (3, 8, 10, 10, 0, 16))),
+    (((), (None, None, None, None), (17, 8, None), (9, 10, 14, 0, 5, 3)),
+     ((), (None, None, None, None), (8, None, None), (9, 3, 16, 1, 2, 10))),
+    (((('a', 4, 1),), (None, None, None, None), (None, None, None), (1, 3, 15, 1, 7, 6)),
+     ((('a', 5, 0), ('t', 3), ('a', 7, 1), ('a', 5, 1)), (None, None, None, None), (16, None, None), (4, 6, 7, 9, 10, 7))),
+    (((), (None, None, None, None), (3, 1, None), (10, 7, 12, 5, 7, 4)),
+     ((), (7, 5, None, None), (4, 6, 9), (7, 5, 13, 0, 2, 5))),
+    (((), (4, None, None, None), (12, 5, 7), (9, 10, 4, 11, 4, 15)),
+     ((), (None, None, None, None), (13, 2, None), (3, 0, 5, 10, 7, 14))),
+    (((), (None, None, None, None), (9, 10, 4), (11, 6, 14, 6, 0, 16)),
+     ((), (None, None, None, None), (5, 10, 14), (0, 7, 15, 1, 3, 7))),
 )
 
 TAIL = (
-    (12, 11, 2, 14),
-    (0, 11, 4, 1),
+    (15, 11, 14, 6, 0, 16),
+    (0, 15, 1, 3, 7),
 )
 
 SLOTS = len(OFFSETS[0])
@@ -124,10 +124,11 @@
         x, y, z = (lax.rem(g + k, SIDE) for g, k in zip((gx, gy, gz), offset))
         return (x, (z * SIDE + y) * 2 + on)
 
+    near = [at(direction, core) for direction in DIRS]
     barrier = pltpu.get_barrier_semaphore()
-    for direction in DIRS:
-        pl.semaphore_signal(barrier, inc=1, device_id=at(direction, core), device_id_type=MESH)
-    pl.semaphore_signal(barrier, inc=1, device_id=at((0, 0, 0), other), device_id_type=MESH)
+    for device in near:
+        pl.semaphore_signal(barrier, inc=1, device_id=device, device_id_type=MESH)
+    pl.semaphore_signal(barrier, inc=1, device_id=(gx, mem + 1 - 2 * core), device_id_type=MESH)
 
     def chunk_of(slot, h):
         return buf.at[slot, pl.ds(h * part, part)]
@@ -136,13 +137,13 @@
         return pltpu.make_async_remote_copy(
             src_ref=chunk_of(source, h), dst_ref=chunk_of(target, h),
             send_sem=send_sem.at[target, h], recv_sem=recv_sem.at[target, h],
-            device_id=at(DIRS[direction], core), device_id_type=MESH)
+            device_id=near[direction], device_id_type=MESH)
 
     def relay_label(source, target, direction):
         return pltpu.make_async_remote_copy(
             src_ref=labels.at[source], dst_ref=labels.at[target],
             send_sem=label_send.at[target], recv_sem=label_recv.at[target],
-            device_id=at(DIRS[direction], core), device_id_type=MESH)
+            device_id=near[direction], device_id_type=MESH)
 
     def send(source, target, h, direction):
         if h == 0:
@@ -153,13 +154,13 @@
         return pltpu.make_async_remote_copy(
             src_ref=chunk_of(slot, h), dst_ref=chunk_of(SLOTS + k, h),
             send_sem=give_sem.at[k, h], recv_sem=take_sem.at[k, h],
-            device_id=at((0, 0, 0), other), device_id_type=MESH)
+            device_id=(gx, mem + 1 - 2 * core), device_id_type=MESH)
 
     def share_label(slot, k):
         return pltpu.make_async_remote_copy(
             src_ref=labels.at[slot], dst_ref=labels.at[SLOTS + k],
             send_sem=label_give.at[k], recv_sem=label_take.at[k],
-            device_id=at((0, 0, 0), other), device_id_type=MESH)
+            device_id=(gx, mem + 1 - 2 * core), device_id_type=MESH)
 
     def give(which, slot, h):
         if slot in SHARED[1 - which]:

time: 51.1 us -> 47.5 us (0.930)
  Pallas kernels: 49.6 us -> 46.1 us
    pallas_call x1, Pallas kernels: 49.6 us -> 46.1 us  [body(): pl.pallas_call(functools.partial(kernel, chunks), out_shape=jax.ShapeDtyp...]
where the time goes in v12:
time: 47.5 us; the launch traced here: 47.4 us
  Pallas kernels  46.1 us (97%)
  local copies, waits for them, and re-layouts  1.24 us (3%)
    pallas_call x1, Pallas kernels, body(): pl.pallas_call(functools.partial(kernel, chunks), out_shape=jax.ShapeDtyp...  46.1 us
    unnamed x1, local copies, waits for them, and re-layouts  1.24 us

profile of v12, /device:TPU:1, one launch (start us, length us, event | category | flops | bytes accessed | tf_op | source)
XLA Modules:
  0.0 47.4 jit_solution(9752127920922394636)
XLA Ops:
  0.0 46.1 %shard_map.28 = f32[256]{0:T(256)} custom-call(f32[256,768]{1,0:T(8,128)} %emb_ref.1, s32[1,256]{1,0:T(1,128)} %bitcast.1), custom_call_target="tpu_custom_call" | custom-call | tf_op jit(solution)/shard_map/pallas_call | solution.py:348
  46.2 1.2 %copy.4 = f32[256]{0:T(256)} copy(f32[256]{0:T(256)} %shard_map.28) | data formatting | bytes 2048

commit v13 on v12

--- a/solution.py
+++ b/solution.py
@@ -80,6 +80,7 @@
 EXTRA = len(SHARED[0])
 HELD = SLOTS + EXTRA
 NONE = 31
+GROUP = 64
 
 
 def words(values, bits=5):
@@ -214,21 +215,23 @@
         sims = lax.dot_general(jnp.concatenate([buf[a] for a in left], axis=0), buf[right], (((1,), (1,)), ((), ())),
                                preferred_element_type=jnp.float32)
         names = labels[right]
-        tops = [row_best[a] for a in left]
-        for k in range(rows // 128):
-            lanes = slice(k * 128, (k + 1) * 128)
-            high = column_best[right, :, lanes]
-            for n, a in enumerate(left):
-                keep = label_rows[a] == names[:, lanes]
-                if own:
-                    keep = keep & (lax.broadcasted_iota(jnp.int32, (rows, 128), 0)
-                                   != lax.broadcasted_iota(jnp.int32, (rows, 128), 1) + k * 128)
-                scores = jnp.where(keep, sims[n * rows:(n + 1) * rows, lanes], FILL)
-                tops[n] = jnp.maximum(tops[n], scores)
-                high = jnp.maximum(high, jnp.max(scores.reshape(rows // 8, 8, 128), axis=0))
-            column_best[right, :, lanes] = high
+        lanes = [slice(k, k + 128) for k in range(0, rows, 128)]
+        high = [column_best[right, :, k] for k in lanes]
         for n, a in enumerate(left):
-            row_best[a] = tops[n]
+            for r in range(0, rows, GROUP):
+                mine = label_rows[a, pl.ds(r, GROUP)]
+                top = row_best[a, pl.ds(r, GROUP)]
+                for m, k in enumerate(lanes):
+                    keep = mine == names[:, k]
+                    if own:
+                        keep = keep & (lax.broadcasted_iota(jnp.int32, (GROUP, 128), 0) + r
+                                       != lax.broadcasted_iota(jnp.int32, (GROUP, 128), 1) + m * 128)
+                    scores = jnp.where(keep, sims[n * rows + r:n * rows + r + GROUP, k], FILL)
+                    top = jnp.maximum(top, scores)
+                    high[m] = jnp.maximum(high[m], jnp.max(scores.reshape(GROUP // 8, 8, 128), axis=0))
+                row_best[a, pl.ds(r, GROUP)] = top
+        for m, k in enumerate(lanes):
+            column_best[right, :, k] = high[m]
 
     def answer(slot):
         return pltpu.make_async_remote_copy(

time: 47.5 us -> 47.4 us (level)
  no operation moved by 1% of the time
where the time goes in v13:
time: 47.4 us; the launch traced here: 47.3 us
  Pallas kernels  46.1 us (97%)
  local copies, waits for them, and re-layouts  1.24 us (3%)
    pallas_call x1, Pallas kernels, body(): pl.pallas_call(functools.partial(kernel, chunks), out_shape=jax.ShapeDtyp...  46.1 us
    unnamed x1, local copies, waits for them, and re-layouts  1.24 us

profile of v13, /device:TPU:1, one launch (start us, length us, event | category | flops | bytes accessed | tf_op | source)
XLA Modules:
  0.0 47.3 jit_solution(916919256941541112)
XLA Ops:
  0.0 46.1 %shard_map.28 = f32[256]{0:T(256)} custom-call(f32[256,768]{1,0:T(8,128)} %emb_ref.1, s32[1,256]{1,0:T(1,128)} %bitcast.1), custom_call_target="tpu_custom_call" | custom-call | tf_op jit(solution)/shard_map/pallas_call | solution.py:351
  46.1 1.2 %copy.4 = f32[256]{0:T(256)} copy(f32[256]{0:T(256)} %shard_map.28) | data formatting | bytes 2048

commit v14 on v13

--- a/solution.py
+++ b/solution.py
@@ -14,66 +14,66 @@
 DIRS = ((1, 0, 0), (3, 0, 0), (0, 1, 0), (0, 3, 0), (0, 0, 1), (0, 0, 3))
 
 OFFSETS = (
-    ((0, 0, 0), (0, 0, 1), (1, 0, 1), (1, 0, 2), (2, 0, 2), (0, 1, 3),
-     (0, 2, 3), (2, 0, 0), (3, 0, 0), (0, 1, 0), (0, 2, 0), (0, 3, 0)),
-    ((0, 0, 0), (1, 0, 0), (1, 0, 1), (2, 0, 1), (0, 1, 2), (0, 2, 2),
-     (0, 0, 3), (2, 0, 3), (3, 0, 3), (0, 1, 3), (0, 2, 3), (0, 3, 3)),
-)
-
-SHARED = ((1, 2, 3, 4, 8, 11), (0, 2, 5, 6, 7, 8))
+    ((0, 0, 0), (0, 3, 3), (0, 2, 3), (0, 3, 0), (1, 0, 0), (2, 0, 0),
+     (0, 1, 0), (0, 2, 0), (0, 0, 1), (3, 0, 1), (2, 0, 2), (3, 0, 2)),
+    ((0, 0, 0), (0, 3, 2), (0, 2, 2), (0, 3, 3), (0, 0, 3), (1, 0, 3),
+     (2, 0, 3), (0, 1, 3), (0, 2, 3), (3, 0, 0), (2, 0, 1), (3, 0, 1)),
+)
+
+SHARED = ((1, 5, 7, 9, 10, 11), (0, 1, 2, 4, 5, 9))
 
 FIRST_SENDS = (
-    ((0, 1, 0, 4), (0, 9, 0, 2), (0, 8, 0, 1), (0, 11, 0, 3)),
-    ((0, 6, 0, 5), (0, 1, 0, 0)),
+    ((0, 8, 0, 4), (0, 3, 0, 3), (0, 4, 0, 0), (0, 6, 0, 2)),
+    ((0, 4, 0, 5), (0, 9, 0, 1)),
 )
 
 LAST_SENDS = (
-    ((1, 1), (2, 1), (3, 1), (4, 0), (4, 1), (6, 0), (6, 1), (7, 1), (10, 0), (10, 1)),
-    ((1, 1), (2, 0), (2, 1), (3, 0), (3, 1), (5, 0), (5, 1), (6, 1), (7, 0), (7, 1), (8, 1), (10, 1)),
+    ((1, 1), (2, 1), (5, 1), (6, 1), (7, 0), (9, 1), (10, 0), (10, 1), (11, 0), (11, 1)),
+    ((2, 0), (2, 1), (3, 0), (3, 1), (6, 1), (8, 1), (9, 0), (9, 1), (10, 1), (11, 1)),
 )
 
 STEPS = (
-    (((('s', 0, 8, 1, 1, 8, 0), ('s', 0, 9, 1, 2), ('s', 0, 11, 1, 3, 11, 0), ('s', 0, 1, 1, 4, 9, 0), ('a', 1, 0), ('a', 8, 0), ('a', 11, 0), ('a', 9, 0), ('s', 9, 5, 0, 5, 1, 0), ('s', 1, 2, 0, 0), ('s', 8, 7, 0, 1, 8, 1), ('s', 11, 10, 0, 3, 9, 1), ('a', 1, 1), ('t', 0), ('a', 11, 1), ('a', 9, 1), ('a', 8, 1), ('s', 1, 2, 1, 0), ('s', 9, 5, 1, 5, 5, 0), ('s', 9, 10, 1, 2, 2, 0), ('a', 2, 0), ('s', 8, 7, 1, 1, 7, 0), ('s', 2, 3, 0, 4, 11, 1)), (8, 9, 11, None), (None, None, None), (8, 9, 1, 9, 11, 12)),
-     ((('t', 0), ('s', 0, 6, 1, 5, 6, 0), ('s', 0, 1, 1, 0), ('a', 6, 0), ('a', 1, 0), ('s', 6, 11, 0, 3), ('s', 6, 9, 0, 2), ('s', 6, 8, 0, 1), ('s', 1, 2, 0, 4), ('a', 1, 1), ('a', 6, 1)), (1, 6, None, None), (None, None, None), (0, 1, 12, 1, 6, 0))),
-    (((('a', 7, 0), ('a', 5, 0), ('s', 5, 6, 0, 2), ('a', 10, 0)), (1, None, None, None), (None, None, None), (1, 8, 11, 1, 8, 12)),
-     ((('s', 1, 2, 1, 4), ('s', 6, 8, 1, 1, 1, 0), ('s', 6, 9, 1, 2, 9, 0), ('s', 6, 11, 1, 3, 11, 0), ('a', 8, 0), ('a', 2, 0), ('a', 9, 0), ('s', 2, 3, 0, 0), ('a', 11, 0), ('s', 9, 4, 0, 5), ('s', 11, 10, 0, 3, 11, 1), ('a', 2, 1), ('a', 9, 1)), (2, None, None, None), (None, None, None), (1, 2, 6, 6, 2, 12))),
-    (((('t', 1),), (None, None, None, None), (None, None, None), (0, 8, 9, 1, 8, 0)),
-     ((('s', 2, 3, 1, 0, 8, 0), ('s', 8, 7, 0, 1), ('s', 9, 4, 1, 5), ('a', 11, 1)), (None, None, None, None), (None, None, None), (0, 1, 9, 2, 6, 9))),
-    (((('a', 10, 1),), (None, None, None, None), (None, None, None), (9, 11, 13, 1, 8, 10)),
-     ((('a', 8, 1), ('t', 5)), (9, 11, None, None), (None, None, None), (2, 9, 11, 9, 11, 12))),
-    (((('a', 2, 1), ('s', 2, 3, 1, 4, 3, 0), ('a', 5, 1)), (2, 10, None, None), (None, None, None), (1, 2, 5, 10, 11, 2)),
-     ((), (None, None, None, None), (None, None, None), (9, 11, 8, 0, 1, 11))),
-    (((('a', 3, 0), ('t', 5), ('s', 5, 6, 1, 2), ('s', 3, 4, 0, 0, 5, 1)), (None, None, None, None), (None, None, None), (11, 2, 9, 1, 2, 17)),
-     ((('a', 4, 0), ('a', 3, 0)), (None, None, None, None), (None, None, None), (1, 2, 8, 2, 9, 17))),
-    (((('a', 7, 1),), (5, None, None, None), (None, None, None), (5, 9, 17, 2, 5, 8)),
-     ((('t', 2), ('s', 11, 10, 1, 3, 4, 0), ('t', 1)), (None, None, None, None), (None, None, None), (0, 6, 14, 6, 9, 13))),
-    (((('a', 6, 0), ('t', 4)), (None, None, None, None), (None, None, None), (10, 5, 13, 0, 2, 7)),
-     ((('a', 10, 0), ('s', 10, 5, 0, 5, 9, 1), ('s', 8, 7, 1, 1, 10, 0), ('a', 3, 1), ('a', 4, 1)), (8, 3, 4, None), (None, None, None), (8, 3, 14, 8, 4, 12))),
-    (((), (None, None, None, None), (None, None, None), (0, 2, 7, 5, 9, 7)),
-     ((('s', 4, 5, 1, 2, 4, 1),), (None, None, None, None), (12, None, None), (8, 11, 4, 11, 4, 17))),
-    (((('a', 3, 1), ('s', 3, 4, 1, 0)), (None, None, None, None), (None, None, None), (10, 11, 16, 2, 9, 16)),
-     ((('t', 4),), (None, None, None, None), (None, None, None), (11, 4, 17, 4, 6, 16))),
-    (((('a', 6, 1),), (3, 7, None, None), (2, None, None), (3, 0, 12, 7, 3, 10)),
-     ((), (None, None, None, None), (11, None, None), (4, 9, 3, 0, 2, 4))),
-    (((), (6, None, None, None), (None, None, None), (7, 6, 13, 8, 0, 6)),
-     ((('a', 10, 1), ('a', 7, 0)), (10, None, None, None), (None, None, None), (4, 10, 13, 10, 0, 17))),
-    (((('t', 3), ('t', 2), ('a', 4, 0)), (None, None, None, None), (13, None, None), (7, 3, 17, 8, 11, 3)),
-     ((), (None, None, None, None), (17, None, None), (3, 8, 10, 10, 0, 16))),
-    (((), (None, None, None, None), (17, 8, None), (9, 10, 14, 0, 5, 3)),
-     ((), (None, None, None, None), (8, None, None), (9, 3, 16, 1, 2, 10))),
-    (((('a', 4, 1),), (None, None, None, None), (None, None, None), (1, 3, 15, 1, 7, 6)),
-     ((('a', 5, 0), ('t', 3), ('a', 7, 1), ('a', 5, 1)), (None, None, None, None), (16, None, None), (4, 6, 7, 9, 10, 7))),
-    (((), (None, None, None, None), (3, 1, None), (10, 7, 12, 5, 7, 4)),
-     ((), (7, 5, None, None), (4, 6, 9), (7, 5, 13, 0, 2, 5))),
-    (((), (4, None, None, None), (12, 5, 7), (9, 10, 4, 11, 4, 15)),
-     ((), (None, None, None, None), (13, 2, None), (3, 0, 5, 10, 7, 14))),
-    (((), (None, None, None, None), (9, 10, 4), (11, 6, 14, 6, 0, 16)),
-     ((), (None, None, None, None), (5, 10, 14), (0, 7, 15, 1, 3, 7))),
+    (((('s', 0, 8, 1, 4, 8, 0), ('s', 0, 3, 1, 3, 3, 0), ('s', 0, 4, 1, 0, 4, 0), ('s', 0, 6, 1, 2, 6, 0), ('a', 6, 0), ('a', 4, 0), ('a', 8, 0), ('a', 3, 0), ('s', 8, 9, 0, 1), ('s', 3, 1, 0, 5), ('s', 4, 5, 0, 0, 4, 1), ('s', 6, 7, 0, 2), ('a', 4, 1), ('a', 3, 1), ('a', 6, 1), ('a', 8, 1)), (3, 4, None, None), (None, None, None), (0, 3, 8, 3, 4, 0)),
+     ((('s', 0, 4, 1, 5, 4, 0), ('s', 0, 9, 1, 1), ('t', 0), ('a', 4, 0), ('s', 4, 7, 0, 2), ('s', 4, 3, 0, 3), ('a', 9, 0), ('s', 4, 5, 0, 0), ('s', 9, 11, 0, 4), ('a', 4, 1), ('a', 9, 1)), (4, 9, None, None), (None, None, None), (0, 4, 12, 4, 9, 0))),
+    (((('s', 8, 9, 1, 1, 9, 0), ('s', 3, 7, 1, 3, 3, 1), ('s', 3, 1, 1, 5, 1, 0), ('a', 9, 0), ('t', 3)), (6, None, None, None), (None, None, None), (3, 4, 15, 4, 6, 3)),
+     ((('s', 9, 11, 1, 4, 11, 0), ('s', 4, 5, 1, 0, 5, 0), ('s', 4, 7, 1, 2, 7, 0), ('s', 4, 3, 1, 3), ('a', 3, 0), ('a', 11, 0), ('s', 3, 1, 0, 5, 4, 1), ('s', 11, 10, 0, 1), ('a', 5, 0), ('a', 7, 0), ('s', 7, 8, 0, 2, 7, 1), ('s', 5, 6, 0, 0, 5, 1), ('a', 11, 1)), (11, None, None, None), (None, None, None), (9, 11, 4, 9, 11, 12))),
+    (((('s', 9, 11, 0, 4, 8, 1), ('a', 1, 0)), (8, None, None, None), (None, None, None), (6, 8, 4, 6, 8, 15)),
+     ((('a', 3, 1), ('s', 3, 1, 1, 5, 1, 0), ('s', 11, 10, 1, 1, 10, 0)), (None, None, None, None), (None, None, None), (0, 4, 3, 9, 11, 3))),
+    (((('s', 4, 5, 1, 0, 5, 0), ('s', 1, 2, 0, 3, 7, 1), ('a', 5, 0), ('a', 7, 0), ('a', 7, 1), ('t', 5)), (7, None, None, None), (None, None, None), (3, 6, 17, 6, 7, 8)),
+     ((('a', 5, 1), ('a', 7, 1), ('t', 3)), (3, None, None, None), (None, None, None), (11, 3, 15, 0, 3, 7))),
+    (((('a', 1, 1), ('a', 9, 1), ('s', 9, 11, 1, 4), ('a', 11, 0), ('s', 11, 10, 0, 1)), (None, None, None, None), (None, None, None), (3, 4, 9, 6, 7, 9)),
+     ((('a', 1, 0), ('a', 10, 0)), (7, None, None, None), (None, None, None), (3, 7, 12, 9, 11, 7))),
+    (((), (1, None, None, None), (None, None, None), (7, 1, 4, 7, 1, 17)),
+     ((), (None, None, None, None), (None, None, None), (3, 7, 5, 9, 11, 5))),
+    (((('s', 1, 2, 1, 3, 2, 0), ('t', 1), ('t', 2)), (9, None, None, None), (None, None, None), (8, 9, 14, 3, 6, 13)),
+     ((('s', 7, 8, 1, 2, 8, 0), ('t', 1), ('t', 5)), (5, None, None, None), (None, None, None), (0, 4, 13, 3, 5, 17))),
+    (((('a', 5, 1),), (None, None, None, None), (None, None, None), (8, 9, 1, 1, 3, 14)),
+     ((('a', 8, 0), ('s', 8, 2, 0, 5, 1, 1), ('a', 1, 1)), (1, None, None, None), (None, None, None), (0, 5, 1, 5, 1, 12))),
+    (((), (None, None, None, None), (None, None, None), (7, 8, 13, 0, 1, 5)),
+     ((('s', 5, 6, 1, 0, 6, 0), ('s', 1, 2, 1, 3), ('a', 6, 0)), (None, None, None, None), (12, None, None), (7, 1, 15, 7, 11, 1))),
+    (((('a', 11, 1), ('a', 2, 0)), (None, None, None, None), (None, None, None), (0, 1, 5, 3, 7, 5)),
+     ((('t', 4), ('a', 10, 1)), (None, None, None, None), (None, None, None), (7, 11, 1, 1, 3, 16))),
+    (((('s', 11, 10, 1, 1),), (5, 11, None, None), (None, None, None), (4, 6, 11, 5, 11, 14)),
+     ((), (10, None, None, None), (7, None, None), (1, 3, 10, 4, 10, 16))),
+    (((), (None, None, None, None), (14, None, None), (7, 5, 15, 0, 1, 11)),
+     ((('a', 8, 1),), (8, None, None, None), (None, None, None), (5, 10, 13, 1, 8, 17))),
+    (((('a', 10, 0), ('a', 2, 1), ('t', 0)), (None, None, None, None), (None, None, None), (11, 0, 15, 6, 8, 12)),
+     ((('a', 2, 0),), (None, None, None, None), (None, None, None), (5, 9, 8, 8, 0, 15))),
+    (((('t', 4),), (2, None, None, None), (15, None, None), (3, 6, 16, 2, 0, 13)),
+     ((('a', 6, 1),), (None, None, None, None), (5, 15, None), (8, 0, 16, 10, 11, 8))),
+    (((), (None, None, None, None), (6, 13, None), (9, 2, 5, 4, 8, 2)),
+     ((('a', 2, 1), ('t', 2)), (6, None, None, None), (16, None, None), (0, 6, 14, 1, 3, 6))),
+    (((('a', 10, 1),), (None, None, None, None), (9, 4, 8), (7, 2, 16, 5, 2, 17)),
+     ((), (None, None, None, None), (14, 1, 3), (4, 8, 6, 8, 6, 13))),
+    (((), (10, None, None, None), (16, 2, 17), (11, 10, 7, 11, 10, 12)),
+     ((), (None, None, None, None), (4, 8, 13), (9, 10, 6, 0, 10, 2))),
+    (((), (None, None, None, None), (7, 11, 12), (1, 3, 10, 5, 0, 10)),
+     ((), (2, None, None, None), (9, 10, None), (6, 2, 17, 11, 0, 2))),
 )
 
 TAIL = (
-    (15, 11, 14, 6, 0, 16),
-    (0, 15, 1, 3, 7),
+    (1, 3, 5, 0, 10),
+    (6, 17, 11, 0, 2),
 )
 
 SLOTS = len(OFFSETS[0])

time: 47.4 us -> 46.3 us (0.977)
  Pallas kernels: 46.1 us -> 44.9 us
    pallas_call x1, Pallas kernels: 46.1 us -> 44.9 us  [body(): pl.pallas_call(functools.partial(kernel, chunks), out_shape=jax.ShapeDtyp...]
where the time goes in v14:
time: 46.3 us; the launch traced here: 46.2 us
  Pallas kernels  44.9 us (97%)
  local copies, waits for them, and re-layouts  1.24 us (3%)
    pallas_call x1, Pallas kernels, body(): pl.pallas_call(functools.partial(kernel, chunks), out_shape=jax.ShapeDtyp...  44.9 us
    unnamed x1, local copies, waits for them, and re-layouts  1.24 us

profile of v14, /device:TPU:1, one launch (start us, length us, event | category | flops | bytes accessed | tf_op | source)
XLA Modules:
  0.0 46.2 jit_solution(12479704239673838657)
XLA Ops:
  0.0 44.9 %shard_map.28 = f32[256]{0:T(256)} custom-call(f32[256,768]{1,0:T(8,128)} %emb_ref.1, s32[1,256]{1,0:T(1,128)} %bitcast.1), custom_call_target="tpu_custom_call" | custom-call | tf_op jit(solution)/shard_map/pallas_call | solution.py:351
  44.9 1.2 %copy.4 = f32[256]{0:T(256)} copy(f32[256]{0:T(256)} %shard_map.28) | data formatting | bytes 2048

commit v15 on v14

--- a/solution.py
+++ b/solution.py
@@ -14,66 +14,66 @@
 DIRS = ((1, 0, 0), (3, 0, 0), (0, 1, 0), (0, 3, 0), (0, 0, 1), (0, 0, 3))
 
 OFFSETS = (
-    ((0, 0, 0), (0, 3, 3), (0, 2, 3), (0, 3, 0), (1, 0, 0), (2, 0, 0),
-     (0, 1, 0), (0, 2, 0), (0, 0, 1), (3, 0, 1), (2, 0, 2), (3, 0, 2)),
-    ((0, 0, 0), (0, 3, 2), (0, 2, 2), (0, 3, 3), (0, 0, 3), (1, 0, 3),
-     (2, 0, 3), (0, 1, 3), (0, 2, 3), (3, 0, 0), (2, 0, 1), (3, 0, 1)),
-)
-
-SHARED = ((1, 5, 7, 9, 10, 11), (0, 1, 2, 4, 5, 9))
+    ((0, 0, 0), (3, 0, 0), (3, 1, 0), (2, 1, 0), (0, 2, 0), (2, 2, 0),
+     (0, 3, 0), (0, 0, 1), (0, 0, 2), (1, 0, 2), (0, 0, 3), (1, 0, 3)),
+    ((0, 0, 0), (1, 0, 0), (0, 1, 0), (3, 1, 0), (1, 2, 0), (3, 2, 0),
+     (1, 3, 0), (1, 0, 1), (1, 0, 2), (2, 0, 2), (1, 0, 3), (2, 0, 3)),
+)
+
+SHARED = ((2, 3, 5, 6, 7, 11), (0, 2, 4, 6, 9, 11))
 
 FIRST_SENDS = (
-    ((0, 8, 0, 4), (0, 3, 0, 3), (0, 4, 0, 0), (0, 6, 0, 2)),
-    ((0, 4, 0, 5), (0, 9, 0, 1)),
+    ((0, 1, 0, 1), (0, 10, 0, 5), (0, 6, 0, 3), (0, 7, 0, 4)),
+    ((0, 1, 0, 0), (0, 2, 0, 2)),
 )
 
 LAST_SENDS = (
-    ((1, 1), (2, 1), (5, 1), (6, 1), (7, 0), (9, 1), (10, 0), (10, 1), (11, 0), (11, 1)),
-    ((2, 0), (2, 1), (3, 0), (3, 1), (6, 1), (8, 1), (9, 0), (9, 1), (10, 1), (11, 1)),
+    ((1, 1), (2, 1), (3, 0), (3, 1), (4, 0), (5, 0), (5, 1), (6, 0), (6, 1), (7, 1), (8, 0), (8, 1), (9, 0), (9, 1), (10, 1)),
+    ((3, 0), (3, 1), (4, 0), (4, 1), (5, 0), (5, 1), (6, 1), (7, 0), (7, 1), (8, 0), (8, 1), (9, 0), (9, 1), (10, 1), (11, 0), (11, 1)),
 )
 
 STEPS = (
-    (((('s', 0, 8, 1, 4, 8, 0), ('s', 0, 3, 1, 3, 3, 0), ('s', 0, 4, 1, 0, 4, 0), ('s', 0, 6, 1, 2, 6, 0), ('a', 6, 0), ('a', 4, 0), ('a', 8, 0), ('a', 3, 0), ('s', 8, 9, 0, 1), ('s', 3, 1, 0, 5), ('s', 4, 5, 0, 0, 4, 1), ('s', 6, 7, 0, 2), ('a', 4, 1), ('a', 3, 1), ('a', 6, 1), ('a', 8, 1)), (3, 4, None, None), (None, None, None), (0, 3, 8, 3, 4, 0)),
-     ((('s', 0, 4, 1, 5, 4, 0), ('s', 0, 9, 1, 1), ('t', 0), ('a', 4, 0), ('s', 4, 7, 0, 2), ('s', 4, 3, 0, 3), ('a', 9, 0), ('s', 4, 5, 0, 0), ('s', 9, 11, 0, 4), ('a', 4, 1), ('a', 9, 1)), (4, 9, None, None), (None, None, None), (0, 4, 12, 4, 9, 0))),
-    (((('s', 8, 9, 1, 1, 9, 0), ('s', 3, 7, 1, 3, 3, 1), ('s', 3, 1, 1, 5, 1, 0), ('a', 9, 0), ('t', 3)), (6, None, None, None), (None, None, None), (3, 4, 15, 4, 6, 3)),
-     ((('s', 9, 11, 1, 4, 11, 0), ('s', 4, 5, 1, 0, 5, 0), ('s', 4, 7, 1, 2, 7, 0), ('s', 4, 3, 1, 3), ('a', 3, 0), ('a', 11, 0), ('s', 3, 1, 0, 5, 4, 1), ('s', 11, 10, 0, 1), ('a', 5, 0), ('a', 7, 0), ('s', 7, 8, 0, 2, 7, 1), ('s', 5, 6, 0, 0, 5, 1), ('a', 11, 1)), (11, None, None, None), (None, None, None), (9, 11, 4, 9, 11, 12))),
-    (((('s', 9, 11, 0, 4, 8, 1), ('a', 1, 0)), (8, None, None, None), (None, None, None), (6, 8, 4, 6, 8, 15)),
-     ((('a', 3, 1), ('s', 3, 1, 1, 5, 1, 0), ('s', 11, 10, 1, 1, 10, 0)), (None, None, None, None), (None, None, None), (0, 4, 3, 9, 11, 3))),
-    (((('s', 4, 5, 1, 0, 5, 0), ('s', 1, 2, 0, 3, 7, 1), ('a', 5, 0), ('a', 7, 0), ('a', 7, 1), ('t', 5)), (7, None, None, None), (None, None, None), (3, 6, 17, 6, 7, 8)),
-     ((('a', 5, 1), ('a', 7, 1), ('t', 3)), (3, None, None, None), (None, None, None), (11, 3, 15, 0, 3, 7))),
-    (((('a', 1, 1), ('a', 9, 1), ('s', 9, 11, 1, 4), ('a', 11, 0), ('s', 11, 10, 0, 1)), (None, None, None, None), (None, None, None), (3, 4, 9, 6, 7, 9)),
-     ((('a', 1, 0), ('a', 10, 0)), (7, None, None, None), (None, None, None), (3, 7, 12, 9, 11, 7))),
-    (((), (1, None, None, None), (None, None, None), (7, 1, 4, 7, 1, 17)),
-     ((), (None, None, None, None), (None, None, None), (3, 7, 5, 9, 11, 5))),
-    (((('s', 1, 2, 1, 3, 2, 0), ('t', 1), ('t', 2)), (9, None, None, None), (None, None, None), (8, 9, 14, 3, 6, 13)),
-     ((('s', 7, 8, 1, 2, 8, 0), ('t', 1), ('t', 5)), (5, None, None, None), (None, None, None), (0, 4, 13, 3, 5, 17))),
-    (((('a', 5, 1),), (None, None, None, None), (None, None, None), (8, 9, 1, 1, 3, 14)),
-     ((('a', 8, 0), ('s', 8, 2, 0, 5, 1, 1), ('a', 1, 1)), (1, None, None, None), (None, None, None), (0, 5, 1, 5, 1, 12))),
-    (((), (None, None, None, None), (None, None, None), (7, 8, 13, 0, 1, 5)),
-     ((('s', 5, 6, 1, 0, 6, 0), ('s', 1, 2, 1, 3), ('a', 6, 0)), (None, None, None, None), (12, None, None), (7, 1, 15, 7, 11, 1))),
-    (((('a', 11, 1), ('a', 2, 0)), (None, None, None, None), (None, None, None), (0, 1, 5, 3, 7, 5)),
-     ((('t', 4), ('a', 10, 1)), (None, None, None, None), (None, None, None), (7, 11, 1, 1, 3, 16))),
-    (((('s', 11, 10, 1, 1),), (5, 11, None, None), (None, None, None), (4, 6, 11, 5, 11, 14)),
-     ((), (10, None, None, None), (7, None, None), (1, 3, 10, 4, 10, 16))),
-    (((), (None, None, None, None), (14, None, None), (7, 5, 15, 0, 1, 11)),
-     ((('a', 8, 1),), (8, None, None, None), (None, None, None), (5, 10, 13, 1, 8, 17))),
-    (((('a', 10, 0), ('a', 2, 1), ('t', 0)), (None, None, None, None), (None, None, None), (11, 0, 15, 6, 8, 12)),
-     ((('a', 2, 0),), (None, None, None, None), (None, None, None), (5, 9, 8, 8, 0, 15))),
-    (((('t', 4),), (2, None, None, None), (15, None, None), (3, 6, 16, 2, 0, 13)),
-     ((('a', 6, 1),), (None, None, None, None), (5, 15, None), (8, 0, 16, 10, 11, 8))),
-    (((), (None, None, None, None), (6, 13, None), (9, 2, 5, 4, 8, 2)),
-     ((('a', 2, 1), ('t', 2)), (6, None, None, None), (16, None, None), (0, 6, 14, 1, 3, 6))),
-    (((('a', 10, 1),), (None, None, None, None), (9, 4, 8), (7, 2, 16, 5, 2, 17)),
-     ((), (None, None, None, None), (14, 1, 3), (4, 8, 6, 8, 6, 13))),
-    (((), (10, None, None, None), (16, 2, 17), (11, 10, 7, 11, 10, 12)),
-     ((), (None, None, None, None), (4, 8, 13), (9, 10, 6, 0, 10, 2))),
-    (((), (None, None, None, None), (7, 11, 12), (1, 3, 10, 5, 0, 10)),
-     ((), (2, None, None, None), (9, 10, None), (6, 2, 17, 11, 0, 2))),
+    (((('s', 0, 7, 1, 4, 1, 0), ('s', 0, 1, 1, 1), ('s', 0, 10, 1, 5), ('a', 10, 0), ('a', 6, 0), ('a', 1, 0), ('s', 10, 11, 0, 0, 10, 0), ('s', 0, 6, 1, 3), ('s', 1, 2, 0, 2), ('a', 1, 1), ('a', 7, 1), ('s', 1, 2, 1, 2, 11, 0), ('a', 10, 1), ('s', 10, 11, 1, 0, 7, 0), ('s', 6, 4, 0, 3), ('a', 6, 1), ('s', 10, 8, 0, 5, 2, 0), ('a', 2, 0), ('a', 7, 0), ('s', 7, 8, 1, 4), ('s', 2, 3, 0, 1), ('a', 2, 1), ('t', 0), ('a', 11, 0), ('s', 6, 4, 1, 3, 11, 1), ('s', 11, 9, 0, 5), ('s', 2, 3, 1, 1), ('t', 1)), (10, 2, 6, 7), (None, None, None), (10, 2, 7, 6, 7, 1)),
+     ((('t', 0), ('s', 0, 2, 1, 2, 2, 0), ('s', 0, 1, 1, 0), ('a', 2, 0), ('a', 1, 0), ('s', 1, 7, 0, 4, 1, 0), ('s', 1, 6, 0, 3), ('s', 2, 3, 0, 1), ('s', 1, 10, 0, 5), ('a', 1, 1), ('a', 2, 1), ('s', 2, 3, 1, 1, 2, 1), ('s', 1, 10, 1, 5), ('s', 1, 7, 1, 4), ('a', 10, 0), ('a', 3, 0), ('s', 1, 6, 1, 3), ('s', 10, 11, 0, 0, 6, 0), ('s', 3, 5, 0, 2, 1, 1), ('a', 6, 0), ('t', 3), ('a', 7, 0), ('a', 3, 1), ('a', 7, 1), ('a', 10, 1)), (3, 10, 1, 2), (None, None, None), (3, 10, 15, 1, 2, 0))),
+    (((('a', 11, 1), ('a', 4, 0)), (1, None, None, None), (None, None, None), (1, 6, 12, 1, 6, 11)),
+     ((('s', 7, 8, 0, 4), ('s', 10, 11, 1, 0, 10, 0), ('s', 3, 5, 1, 2), ('a', 11, 0), ('a', 6, 1), ('t', 1)), (7, None, None, None), (None, None, None), (7, 10, 6, 2, 3, 6))),
+    (((('a', 8, 0), ('a', 8, 1)), (8, None, None, None), (None, None, None), (7, 10, 13, 6, 8, 2)),
+     ((('a', 5, 0),), (None, None, None, None), (None, None, None), (0, 1, 12, 0, 2, 7))),
+    (((), (None, None, None, None), (None, None, None), (0, 6, 7, 7, 10, 12)),
+     ((('s', 7, 8, 1, 4), ('s', 6, 4, 0, 3)), (6, None, None, None), (None, None, None), (1, 6, 13, 0, 1, 10))),
+    (((('t', 3), ('a', 3, 0), ('s', 3, 5, 0, 2, 4, 1), ('s', 8, 9, 1, 0), ('a', 9, 0), ('a', 3, 1), ('a', 4, 1)), (11, None, None, None), (None, None, None), (8, 11, 13, 0, 2, 4)),
+     ((('t', 5), ('a', 11, 1)), (11, None, None, None), (None, None, None), (10, 11, 13, 2, 3, 12))),
+    (((), (None, None, None, None), (None, None, None), (1, 6, 10, 7, 8, 15)),
+     ((('a', 5, 1), ('s', 6, 4, 1, 3)), (None, None, None, None), (None, None, None), (6, 11, 12, 2, 3, 1))),
+    (((), (None, None, None, None), (None, None, None), (10, 11, 15, 1, 6, 0)),
+     ((('a', 8, 0),), (None, None, None, None), (None, None, None), (0, 3, 11, 3, 10, 7))),
+    (((), (3, 4, None, None), (None, None, None), (3, 0, 12, 4, 3, 11)),
+     ((('s', 8, 9, 0, 0), ('t', 2)), (None, None, None, None), (None, None, None), (6, 7, 11, 1, 10, 14))),
+    (((('t', 4), ('t', 5), ('s', 3, 5, 1, 2)), (None, None, None, None), (None, None, None), (1, 3, 17, 1, 6, 8)),
+     ((('a', 8, 1), ('s', 11, 9, 1, 5)), (None, None, None, None), (None, None, None), (2, 3, 8, 10, 11, 5))),
+    (((('t', 2),), (None, None, None, None), (None, None, None), (0, 6, 3, 8, 4, 12)),
+     ((), (5, None, None, None), (None, None, None), (5, 6, 8, 10, 7, 12))),
+    (((('a', 9, 1),), (9, None, None, None), (12, None, None), (7, 8, 14, 10, 9, 14)),
+     ((), (None, None, None, None), (6, 12, None), (7, 11, 15, 0, 1, 17))),
+    (((('a', 5, 0),), (None, None, None, None), (14, None, None), (6, 0, 9, 4, 3, 16)),
+     ((('a', 4, 0),), (8, None, None, None), (7, None, None), (5, 8, 17, 8, 0, 14))),
+    (((), (None, None, None, None), (6, None, None), (7, 8, 3, 7, 8, 4)),
+     ((('a', 4, 1),), (4, None, None, None), (None, None, None), (10, 11, 4, 8, 4, 13))),
+    (((), (None, None, None, None), (3, None, None), (4, 9, 13, 1, 2, 16)),
+     ((('t', 4),), (None, None, None, None), (None, None, None), (1, 2, 4, 0, 4, 16))),
+    (((('a', 5, 1),), (None, None, None, None), (13, None, None), (9, 0, 15, 4, 7, 5)),
+     ((('a', 9, 1), ('a', 9, 0)), (None, None, None, None), (1, 16, None), (0, 3, 9, 2, 3, 10))),
+    (((), (5, None, None, None), (15, None, None), (7, 5, 17, 1, 4, 9)),
+     ((), (None, None, None, None), (2, 3, 10), (11, 5, 14, 4, 0, 17))),
+    (((), (None, None, None, None), (7, 17, 1), (0, 2, 4, 8, 11, 5)),
+     ((), (9, None, None, None), (11, 14, 17), (9, 0, 13, 8, 0, 15))),
+    (((), (None, None, None, None), (9, 0, 4), (10, 11, 16, 10, 11, 2)),
+     ((), (None, None, None, None), (13, 15, None), (5, 8, 4, 5, 0, 9))),
 )
 
 TAIL = (
-    (1, 3, 5, 0, 10),
-    (6, 17, 11, 0, 2),
+    (8, 5, 16, 10, 11, 2),
+    (8, 4, 5, 0, 9),
 )
 
 SLOTS = len(OFFSETS[0])

time: 46.3 us -> 49 us (1.058)
  Pallas kernels: 44.9 us -> 47.6 us
    pallas_call x1, Pallas kernels: 44.9 us -> 47.6 us  [body(): pl.pallas_call(functools.partial(kernel, chunks), out_shape=jax.ShapeDtyp...]
where the time goes in v15:
time: 49 us; the launch traced here: 48.9 us
  Pallas kernels  47.6 us (97%)
  local copies, waits for them, and re-layouts  1.24 us (3%)
    pallas_call x1, Pallas kernels, body(): pl.pallas_call(functools.partial(kernel, chunks), out_shape=jax.ShapeDtyp...  47.6 us
    unnamed x1, local copies, waits for them, and re-layouts  1.24 us

profile of v15, /device:TPU:1, one launch (start us, length us, event | category | flops | bytes accessed | tf_op | source)
XLA Modules:
  0.0 48.9 jit_solution(17783611584359516718)
XLA Ops:
  0.0 47.6 %shard_map.28 = f32[256]{0:T(256)} custom-call(f32[256,768]{1,0:T(8,128)} %emb_ref.1, s32[1,256]{1,0:T(1,128)} %bitcast.1), custom_call_target="tpu_custom_call" | custom-call | tf_op jit(solution)/shard_map/pallas_call | solution.py:351
  47.6 1.2 %copy.4 = f32[256]{0:T(256)} copy(f32[256]{0:T(256)} %shard_map.28) | data formatting | bytes 2048

commit v16 on v15

--- a/solution.py
+++ b/solution.py
@@ -14,66 +14,66 @@
 DIRS = ((1, 0, 0), (3, 0, 0), (0, 1, 0), (0, 3, 0), (0, 0, 1), (0, 0, 3))
 
 OFFSETS = (
-    ((0, 0, 0), (3, 0, 0), (3, 1, 0), (2, 1, 0), (0, 2, 0), (2, 2, 0),
-     (0, 3, 0), (0, 0, 1), (0, 0, 2), (1, 0, 2), (0, 0, 3), (1, 0, 3)),
-    ((0, 0, 0), (1, 0, 0), (0, 1, 0), (3, 1, 0), (1, 2, 0), (3, 2, 0),
-     (1, 3, 0), (1, 0, 1), (1, 0, 2), (2, 0, 2), (1, 0, 3), (2, 0, 3)),
-)
-
-SHARED = ((2, 3, 5, 6, 7, 11), (0, 2, 4, 6, 9, 11))
+    ((0, 0, 0), (1, 0, 0), (2, 0, 0), (0, 1, 0), (0, 2, 0), (0, 3, 0),
+     (0, 0, 1), (3, 0, 1), (2, 0, 2), (3, 0, 2), (0, 2, 3), (0, 3, 3)),
+    ((0, 0, 0), (0, 0, 3), (1, 0, 3), (2, 0, 3), (0, 1, 3), (0, 2, 3),
+     (0, 3, 3), (3, 0, 0), (2, 0, 1), (3, 0, 1), (0, 2, 2), (0, 3, 2)),
+)
+
+SHARED = ((2, 4, 7, 8, 9, 11), (0, 1, 2, 7, 10, 11))
 
 FIRST_SENDS = (
-    ((0, 1, 0, 1), (0, 10, 0, 5), (0, 6, 0, 3), (0, 7, 0, 4)),
-    ((0, 1, 0, 0), (0, 2, 0, 2)),
+    ((0, 6, 0, 4), (0, 5, 0, 3), (0, 1, 0, 0), (0, 3, 0, 2)),
+    ((0, 1, 0, 5), (0, 7, 0, 1)),
 )
 
 LAST_SENDS = (
-    ((1, 1), (2, 1), (3, 0), (3, 1), (4, 0), (5, 0), (5, 1), (6, 0), (6, 1), (7, 1), (8, 0), (8, 1), (9, 0), (9, 1), (10, 1)),
-    ((3, 0), (3, 1), (4, 0), (4, 1), (5, 0), (5, 1), (6, 1), (7, 0), (7, 1), (8, 0), (8, 1), (9, 0), (9, 1), (10, 1), (11, 0), (11, 1)),
+    ((1, 0), (2, 0), (3, 0), (4, 0), (5, 0), (5, 1), (6, 1), (7, 0), (7, 1), (8, 0), (8, 1), (9, 1), (10, 0), (10, 1), (11, 0), (11, 1)),
+    ((2, 0), (3, 1), (4, 0), (5, 0), (5, 1), (6, 1), (8, 0), (9, 1), (10, 0), (10, 1), (11, 0)),
 )
 
 STEPS = (
-    (((('s', 0, 7, 1, 4, 1, 0), ('s', 0, 1, 1, 1), ('s', 0, 10, 1, 5), ('a', 10, 0), ('a', 6, 0), ('a', 1, 0), ('s', 10, 11, 0, 0, 10, 0), ('s', 0, 6, 1, 3), ('s', 1, 2, 0, 2), ('a', 1, 1), ('a', 7, 1), ('s', 1, 2, 1, 2, 11, 0), ('a', 10, 1), ('s', 10, 11, 1, 0, 7, 0), ('s', 6, 4, 0, 3), ('a', 6, 1), ('s', 10, 8, 0, 5, 2, 0), ('a', 2, 0), ('a', 7, 0), ('s', 7, 8, 1, 4), ('s', 2, 3, 0, 1), ('a', 2, 1), ('t', 0), ('a', 11, 0), ('s', 6, 4, 1, 3, 11, 1), ('s', 11, 9, 0, 5), ('s', 2, 3, 1, 1), ('t', 1)), (10, 2, 6, 7), (None, None, None), (10, 2, 7, 6, 7, 1)),
-     ((('t', 0), ('s', 0, 2, 1, 2, 2, 0), ('s', 0, 1, 1, 0), ('a', 2, 0), ('a', 1, 0), ('s', 1, 7, 0, 4, 1, 0), ('s', 1, 6, 0, 3), ('s', 2, 3, 0, 1), ('s', 1, 10, 0, 5), ('a', 1, 1), ('a', 2, 1), ('s', 2, 3, 1, 1, 2, 1), ('s', 1, 10, 1, 5), ('s', 1, 7, 1, 4), ('a', 10, 0), ('a', 3, 0), ('s', 1, 6, 1, 3), ('s', 10, 11, 0, 0, 6, 0), ('s', 3, 5, 0, 2, 1, 1), ('a', 6, 0), ('t', 3), ('a', 7, 0), ('a', 3, 1), ('a', 7, 1), ('a', 10, 1)), (3, 10, 1, 2), (None, None, None), (3, 10, 15, 1, 2, 0))),
-    (((('a', 11, 1), ('a', 4, 0)), (1, None, None, None), (None, None, None), (1, 6, 12, 1, 6, 11)),
-     ((('s', 7, 8, 0, 4), ('s', 10, 11, 1, 0, 10, 0), ('s', 3, 5, 1, 2), ('a', 11, 0), ('a', 6, 1), ('t', 1)), (7, None, None, None), (None, None, None), (7, 10, 6, 2, 3, 6))),
-    (((('a', 8, 0), ('a', 8, 1)), (8, None, None, None), (None, None, None), (7, 10, 13, 6, 8, 2)),
-     ((('a', 5, 0),), (None, None, None, None), (None, None, None), (0, 1, 12, 0, 2, 7))),
-    (((), (None, None, None, None), (None, None, None), (0, 6, 7, 7, 10, 12)),
-     ((('s', 7, 8, 1, 4), ('s', 6, 4, 0, 3)), (6, None, None, None), (None, None, None), (1, 6, 13, 0, 1, 10))),
-    (((('t', 3), ('a', 3, 0), ('s', 3, 5, 0, 2, 4, 1), ('s', 8, 9, 1, 0), ('a', 9, 0), ('a', 3, 1), ('a', 4, 1)), (11, None, None, None), (None, None, None), (8, 11, 13, 0, 2, 4)),
-     ((('t', 5), ('a', 11, 1)), (11, None, None, None), (None, None, None), (10, 11, 13, 2, 3, 12))),
-    (((), (None, None, None, None), (None, None, None), (1, 6, 10, 7, 8, 15)),
-     ((('a', 5, 1), ('s', 6, 4, 1, 3)), (None, None, None, None), (None, None, None), (6, 11, 12, 2, 3, 1))),
-    (((), (None, None, None, None), (None, None, None), (10, 11, 15, 1, 6, 0)),
-     ((('a', 8, 0),), (None, None, None, None), (None, None, None), (0, 3, 11, 3, 10, 7))),
-    (((), (3, 4, None, None), (None, None, None), (3, 0, 12, 4, 3, 11)),
-     ((('s', 8, 9, 0, 0), ('t', 2)), (None, None, None, None), (None, None, None), (6, 7, 11, 1, 10, 14))),
-    (((('t', 4), ('t', 5), ('s', 3, 5, 1, 2)), (None, None, None, None), (None, None, None), (1, 3, 17, 1, 6, 8)),
-     ((('a', 8, 1), ('s', 11, 9, 1, 5)), (None, None, None, None), (None, None, None), (2, 3, 8, 10, 11, 5))),
-    (((('t', 2),), (None, None, None, None), (None, None, None), (0, 6, 3, 8, 4, 12)),
-     ((), (5, None, None, None), (None, None, None), (5, 6, 8, 10, 7, 12))),
-    (((('a', 9, 1),), (9, None, None, None), (12, None, None), (7, 8, 14, 10, 9, 14)),
-     ((), (None, None, None, None), (6, 12, None), (7, 11, 15, 0, 1, 17))),
-    (((('a', 5, 0),), (None, None, None, None), (14, None, None), (6, 0, 9, 4, 3, 16)),
-     ((('a', 4, 0),), (8, None, None, None), (7, None, None), (5, 8, 17, 8, 0, 14))),
-    (((), (None, None, None, None), (6, None, None), (7, 8, 3, 7, 8, 4)),
-     ((('a', 4, 1),), (4, None, None, None), (None, None, None), (10, 11, 4, 8, 4, 13))),
-    (((), (None, None, None, None), (3, None, None), (4, 9, 13, 1, 2, 16)),
-     ((('t', 4),), (None, None, None, None), (None, None, None), (1, 2, 4, 0, 4, 16))),
-    (((('a', 5, 1),), (None, None, None, None), (13, None, None), (9, 0, 15, 4, 7, 5)),
-     ((('a', 9, 1), ('a', 9, 0)), (None, None, None, None), (1, 16, None), (0, 3, 9, 2, 3, 10))),
-    (((), (5, None, None, None), (15, None, None), (7, 5, 17, 1, 4, 9)),
-     ((), (None, None, None, None), (2, 3, 10), (11, 5, 14, 4, 0, 17))),
-    (((), (None, None, None, None), (7, 17, 1), (0, 2, 4, 8, 11, 5)),
-     ((), (9, None, None, None), (11, 14, 17), (9, 0, 13, 8, 0, 15))),
-    (((), (None, None, None, None), (9, 0, 4), (10, 11, 16, 10, 11, 2)),
-     ((), (None, None, None, None), (13, 15, None), (5, 8, 4, 5, 0, 9))),
+    (((('s', 0, 6, 1, 4, 6, 0), ('s', 0, 5, 1, 3), ('s', 0, 3, 1, 2), ('s', 0, 1, 1, 0), ('a', 1, 0), ('a', 6, 0), ('a', 5, 0), ('a', 3, 0), ('s', 6, 7, 0, 1), ('s', 5, 11, 0, 5), ('s', 1, 2, 0, 0, 1, 1), ('s', 3, 4, 0, 2), ('a', 5, 1), ('a', 3, 1), ('s', 5, 4, 1, 3), ('a', 1, 1), ('s', 5, 11, 1, 5), ('a', 6, 1)), (1, 3, None, None), (None, None, None), (0, 1, 6, 1, 3, 0)),
+     ((('s', 0, 1, 1, 5, 1, 0), ('s', 0, 7, 1, 1, 7, 0), ('a', 1, 0), ('a', 7, 0), ('s', 1, 6, 0, 3), ('s', 1, 2, 0, 0), ('t', 0), ('s', 7, 9, 0, 4), ('s', 1, 4, 0, 2), ('a', 1, 1), ('a', 7, 1), ('s', 1, 6, 1, 3, 7, 1)), (1, 7, None, None), (None, None, None), (0, 1, 12, 1, 7, 0))),
+    (((('t', 2), ('s', 6, 7, 1, 1, 3, 1)), (5, None, None, None), (None, None, None), (1, 3, 14, 3, 5, 1)),
+     ((('s', 1, 4, 1, 2), ('s', 7, 9, 1, 4, 9, 0), ('a', 6, 0), ('s', 1, 2, 1, 0), ('a', 2, 0), ('a', 9, 0), ('s', 9, 8, 0, 1, 6, 0), ('s', 6, 11, 0, 5, 1, 1), ('a', 4, 0), ('s', 4, 5, 0, 2, 4, 1), ('a', 9, 1)), (9, None, None, None), (None, None, None), (7, 9, 1, 7, 9, 12))),
+    (((('a', 7, 0), ('s', 7, 9, 0, 4), ('a', 11, 0)), (6, None, None, None), (None, None, None), (5, 6, 3, 5, 6, 14)),
+     ((('s', 2, 3, 0, 0), ('a', 4, 1), ('s', 9, 8, 1, 1), ('t', 1), ('a', 6, 1), ('s', 6, 11, 1, 5)), (6, None, None, None), (None, None, None), (0, 1, 6, 0, 6, 4))),
+    (((('s', 1, 2, 1, 0), ('s', 11, 10, 0, 3, 4, 1), ('a', 2, 0), ('a', 4, 1), ('a', 4, 0), ('t', 4)), (4, None, None, None), (None, None, None), (3, 5, 16, 5, 4, 6)),
+     ((), (None, None, None, None), (None, None, None), (9, 6, 13, 7, 9, 6))),
+    (((('t', 1), ('a', 7, 1), ('a', 11, 1), ('s', 7, 9, 1, 4), ('a', 9, 0)), (None, None, None, None), (None, None, None), (1, 6, 11, 3, 4, 7)),
+     ((('a', 8, 0), ('a', 2, 1), ('a', 11, 0)), (4, None, None, None), (None, None, None), (6, 4, 12, 7, 9, 4))),
+    (((('s', 11, 10, 1, 3), ('s', 9, 8, 0, 1, 9, 0)), (7, 11, None, None), (None, None, None), (4, 7, 1, 4, 11, 16)),
+     ((('s', 4, 5, 1, 2, 2, 1), ('t', 5), ('t', 3)), (2, None, None, None), (None, None, None), (0, 1, 17, 2, 6, 15))),
+    (((('t', 0), ('a', 2, 1)), (None, None, None, None), (None, None, None), (5, 6, 12, 0, 3, 2)),
+     ((('a', 5, 0), ('s', 2, 3, 1, 0, 3, 0), ('s', 5, 10, 0, 5, 8, 1)), (None, None, None, None), (None, None, None), (4, 6, 2, 7, 9, 2))),
+    (((), (2, None, None, None), (None, None, None), (0, 3, 2, 4, 2, 14)),
+     ((('a', 3, 0), ('a', 11, 1), ('a', 8, 1)), (11, None, None, None), (None, None, None), (4, 9, 11, 4, 11, 13))),
+    (((('a', 9, 1),), (None, None, None, None), (None, None, None), (7, 11, 13, 3, 4, 12)),
+     ((('t', 2),), (None, None, None, None), (None, None, None), (4, 11, 13, 1, 6, 14))),
+    (((('s', 9, 8, 1, 1, 2, 1),), (None, None, None, None), (None, None, None), (4, 7, 2, 0, 1, 9)),
+     ((), (8, None, None, None), (4, None, None), (0, 2, 11, 11, 8, 14))),
+    (((('a', 10, 0), ('a', 8, 0)), (None, None, None, None), (None, None, None), (5, 11, 7, 3, 4, 9)),
+     ((('a', 5, 1), ('s', 5, 10, 1, 5, 11, 1)), (5, None, None, None), (None, None, None), (5, 0, 13, 2, 7, 5))),
+    (((('a', 10, 1), ('t', 5), ('t', 3)), (10, None, None, None), (7, None, None), (10, 0, 12, 3, 4, 15)),
+     ((), (None, None, None, None), (13, None, None), (2, 11, 12, 11, 5, 15))),
+    (((), (9, None, None, None), (12, None, None), (2, 9, 11, 2, 9, 13)),
+     ((('a', 10, 0), ('a', 3, 1)), (None, None, None, None), (12, None, None), (1, 5, 3, 5, 0, 14))),
+    (((), (None, None, None, None), (None, None, None), (5, 10, 15, 5, 6, 13)),
+     ((('t', 4),), (3, None, None, None), (1, 14, None), (0, 3, 16, 2, 8, 17))),
+    (((), (None, None, None, None), (15, 5, 13), (1, 2, 10, 2, 10, 16)),
+     ((), (None, None, None, None), (16, 2, None), (8, 9, 5, 6, 11, 8))),
+    (((('a', 8, 1),), (None, None, None, None), (1, 16, None), (3, 6, 17, 2, 3, 8)),
+     ((), (None, None, None, None), (None, None, None), (5, 3, 17, 6, 7, 3))),
+    (((), (8, None, None, None), (2, 3, None), (4, 11, 8, 9, 8, 17)),
+     ((('a', 10, 1),), (10, None, None, None), (5, 17, 6), (3, 10, 15, 0, 8, 10))),
+    (((), (None, None, None, None), (4, 11, 8), (6, 0, 10, 9, 0, 14)),
+     ((), (None, None, None, None), (7, 15, None), (8, 11, 3, 9, 0, 10))),
 )
 
 TAIL = (
-    (8, 5, 16, 10, 11, 2),
-    (8, 4, 5, 0, 9),
+    (17, 6, 10, 9, 0, 14),
+    (8, 11, 3, 9, 0, 10),
 )
 
 SLOTS = len(OFFSETS[0])

time: 49 us -> 46.5 us (0.949)
  Pallas kernels: 47.6 us -> 45.1 us
    pallas_call x1, Pallas kernels: 47.6 us -> 45.1 us  [body(): pl.pallas_call(functools.partial(kernel, chunks), out_shape=jax.ShapeDtyp...]
where the time goes in v16:
time: 46.5 us; the launch traced here: 46.4 us
  Pallas kernels  45.1 us (97%)
  local copies, waits for them, and re-layouts  1.24 us (3%)
    pallas_call x1, Pallas kernels, body(): pl.pallas_call(functools.partial(kernel, chunks), out_shape=jax.ShapeDtyp...  45.1 us
    unnamed x1, local copies, waits for them, and re-layouts  1.24 us

profile of v16, /device:TPU:1, one launch (start us, length us, event | category | flops | bytes accessed | tf_op | source)
XLA Modules:
  0.0 46.4 jit_solution(2644904551597911993)
XLA Ops:
  0.0 45.1 %shard_map.28 = f32[256]{0:T(256)} custom-call(f32[256,768]{1,0:T(8,128)} %emb_ref.1, s32[1,256]{1,0:T(1,128)} %bitcast.1), custom_call_target="tpu_custom_call" | custom-call | tf_op jit(solution)/shard_map/pallas_call | solution.py:351
  45.1 1.2 %copy.4 = f32[256]{0:T(256)} copy(f32[256]{0:T(256)} %shard_map.28) | data formatting | bytes 2048
